TPU v7x, 256 devices: a whole 4x4x8 slice. The times are simulated.
256 devices in a mesh: group: 8 (over y, core), sub: 32 (over z, x).
Axes of the slice: x: 4, y: 4, z: 8, core: 2. Of those that a mesh axis runs over, the one named last changes fastest.
Arguments:
- residual_in: float32 [128, 9, 32768], P(None, None, ('group', 'sub')), may hold values from -64 to 64
- local_inverse: bfloat16 [256, 2304, 2304], P(('group', 'sub')), may hold values from -0.5 to 1.75
- coarse_inverse: bfloat16 [11520, 11520], P(('group', 'sub')), may hold values from -1 to 1
- cluster_of: int32 [32768], P(('group', 'sub')), may hold values from 0 to 159
- margin_peer: int32 [32768, 1], P(('group', 'sub')), may hold values from 0 to 31; in each aligned block of 128 rows (0 to 127, 128 to 255, ...) at most 8 rows name the same one
- margin_row: int32 [32768], P(('group', 'sub')), may hold values from 0 to 127
Outputs:
- first: float32 [128, 9, 32768], P(None, None, ('group', 'sub'))
- second: float32 [128, 9, 32768], P(None, None, ('group', 'sub'))
Inputs may be any that keep to these rules, and one draw needn't show every extreme that they name: `margin_peer`: among the 128 margin slots of one subdomain no sub index appears more than 8 times, and some subdomain names one exactly 8 times.
All inputs are finite; a program needn't handle non-finite values.
Results may differ from a plain program's by a relative error of at most 0.015.
Values may be sent and summed in bfloat16 or wider, within the bound.
No kernel may reach another device: no remote copies, remote signals or barrier semaphores. Data moves between devices by JAX's collectives and lax.ppermute only.
A program may use at most 128 MiB of HBM per device.

v0:
```python
import jax
import jax.numpy as jnp
from jax import lax
from jax.sharding import PartitionSpec as P

EPSILON = 1e-06


def split_product(values, table):
    high = values.astype(jnp.bfloat16)
    rest = values - high.astype(jnp.float32)
    middle = rest.astype(jnp.bfloat16)
    lowest = (rest - middle.astype(jnp.float32)).astype(jnp.bfloat16)
    total = jnp.dot(high, table, preferred_element_type=jnp.float32)
    total = total + jnp.dot(middle, table, preferred_element_type=jnp.float32)
    return total + jnp.dot(lowest, table, preferred_element_type=jnp.float32)


def body(residual_in, local_inverse, coarse_inverse, cluster_of, margin_peer, margin_row):
    rhs_count = residual_in.shape[0]
    comps = residual_in.shape[1]
    own_cams = residual_in.shape[2]
    over_cams = margin_row.shape[0]
    sub_count = lax.axis_size("sub")
    capacity = max(2, 2 * over_cams // sub_count)
    slot_count = sub_count * capacity
    cl_dev = coarse_inverse.shape[0] // comps
    cl_grp = cl_dev * sub_count
    sub_width = local_inverse.shape[1]
    sub_cams = sub_width // comps
    inverse_block = local_inverse[0]
    line_count = rhs_count * comps
    peer_ids = margin_peer[:, 0]
    peer_hot = (peer_ids[:, None] == jnp.arange(sub_count, dtype=jnp.int32)[None, :]).astype(
        jnp.int32
    )
    slot_ids = jnp.sum((jnp.cumsum(peer_hot, axis=0) - 1) * peer_hot, axis=1)
    dest_ids = peer_ids * capacity + slot_ids
    wanted = jnp.full((slot_count,), -1, jnp.int32).at[dest_ids].set(margin_row)
    incoming = lax.all_to_all(wanted, "sub", split_axis=0, concat_axis=0, tiled=True)
    valid = (incoming >= 0).astype(jnp.float32)[None, :]
    source_rows = jnp.clip(incoming, 0, own_cams - 1)
    cluster_hot = (cluster_of[:, None] == jnp.arange(cl_grp, dtype=jnp.int32)[None, :]).astype(
        jnp.bfloat16
    )
    cluster_back = (jnp.arange(cl_grp, dtype=jnp.int32)[:, None] == cluster_of[None, :]).astype(
        jnp.bfloat16
    )

    def fetch(source):
        outgoing = jnp.take(source, source_rows, axis=1) * valid
        arrived = lax.all_to_all(
            outgoing.astype(jnp.bfloat16), "sub", split_axis=1, concat_axis=1, tiled=True
        ).astype(outgoing.dtype)
        return jnp.take(arrived, dest_ids, axis=1)

    def local_solve(own_part, over_part):
        joined = (
            jnp.concatenate([own_part, over_part], axis=1)
            .astype(jnp.bfloat16)
            .reshape(rhs_count, sub_width)
        )
        result = jnp.dot(joined, inverse_block, preferred_element_type=jnp.float32)
        result = result.reshape(line_count, sub_cams)
        returned = (
            jnp.zeros((line_count, slot_count), jnp.float32)
            .at[:, dest_ids]
            .set(result[:, own_cams:])
        )
        came_back = lax.all_to_all(returned, "sub", split_axis=1, concat_axis=1, tiled=True)
        gathered_back = (
            jnp.zeros((line_count, own_cams), jnp.float32).at[:, source_rows].add(came_back * valid)
        )
        return result[:, :own_cams] + gathered_back

    def coarse_reduce(source):
        local_sums = split_product(source, cluster_hot).reshape(rhs_count, comps, cl_grp)
        return lax.psum_scatter(local_sums, "sub", scatter_dimension=2, tiled=True)

    def add_coarse(block_in):
        return lax.dot_general(
            block_in, coarse_inverse, (((1,), (1,)), ((), ())), preferred_element_type=jnp.float32
        )

    def add_clusters(block_in):
        return split_product(block_in.reshape(line_count, block_in.shape[2]), cluster_back)

    def coarse_finish(reduced):
        ordered = jnp.transpose(reduced, (0, 2, 1))
        ordered = ordered.reshape(rhs_count, ordered.shape[1] * comps).astype(jnp.bfloat16)
        own_rows = add_coarse(lax.all_gather(ordered, ("group", "sub"), axis=1, tiled=True))
        solution = jnp.transpose(own_rows.reshape(rhs_count, cl_dev, comps), (0, 2, 1))
        return add_clusters(lax.all_gather(solution, "sub", axis=2, tiled=True))

    residual = residual_in.reshape(line_count, own_cams)
    over_res = fetch(residual)
    reduced_res = coarse_reduce(residual)
    first = local_solve(residual, over_res) + coarse_finish(reduced_res)
    first_cube = first.reshape(rhs_count, comps, own_cams)
    part_rf = jnp.sum(residual_in * first_cube, axis=(1, 2))
    part_ff = jnp.sum(first_cube * first_cube, axis=(1, 2))
    inner_rf, inner_ff = lax.psum((part_rf, part_ff), ("group", "sub"))
    step_scale = inner_rf / (inner_ff + EPSILON)
    line_scale = jnp.repeat(step_scale, comps)[:, None]
    shifted = residual - line_scale * first
    over_shift = fetch(shifted)
    reduced_shift = coarse_reduce(shifted)
    second = local_solve(shifted, over_shift) + coarse_finish(reduced_shift)
    return (first_cube, second.reshape(rhs_count, comps, own_cams))


def solution(mesh):
    placed = (
        P(None, None, ("group", "sub")),
        P(("group", "sub"), None, None),
        P(("group", "sub"), None),
        P(("group", "sub")),
        P(("group", "sub"), None),
        P(("group", "sub")),
    )
    return jax.shard_map(
        body,
        mesh=mesh,
        in_specs=placed,
        out_specs=(P(None, None, ("group", "sub")), P(None, None, ("group", "sub"))),
        check_vma=False,
    )
```

profile of v0, /device:TPU:10, one launch (start us, length us, event | category | flops | bytes accessed | tf_op | source)
XLA Modules:
  0.0 907.1 jit_solution(15966489444424743444)
XLA Ops:
  14.4 3.0 copy.45
  17.4 218.1 %reduce-scatter.3.cloned.1.call-done = f32[128,9,5]{0,1,2:T(8,128)} async-done(((f32[128,9,160]{0,1,2:T(8,128)}), f32[128,9,5]{0,1,2:T(8,128)}) %reduce-scatter.3.cloned.1.call-update) | async-done | bytes 23056 | tf_op jit(solution)/shard_map/reduce_scatter | solution.py:78
  238.6 16.3 %all_to_all.51 = s32[32,8,1]{1,2,0:T(1,128)S(1)} all-to-all(s32[32,8,1]{1,2,0:T(1,128)S(1)} %bitcast.101), channel_id=1, replica_groups=mesh['group'=8,'sub'=32] {'sub'}, dimensions={0} | all-to-all | bytes 2048 | tf_op jit(solution)/shard_map/all_to_all | solution.py:40
  257.5 5.0 all-to-all-start.1
  262.6 13.4 %all-to-all-done.1 = bf16[1152,32,8]{0,2,1:T(8,128)(2,1)S(1)} async-done(((bf16[1152,32,8]{0,2,1:T(8,128)(2,1)}), bf16[1152,32,8]{0,2,1:T(8,128)(2,1)S(1)}, u32[]{:S(2)}, u32[]{:S(2)}) %all-to-all-start.1) | async-done | bytes 589856 | tf_op jit(solution)/shard_map/all_to_all | solution.py:52
  278.0 5.6 fusion.2
  288.3 5.7 all-to-all-start.2
  294.1 56.5 %all-gather.5.cloned.1.call-done = bf16[256,45,128]{2,1,0:T(8,128)(2,1)} async-done(((bf16[1,45,128]{2,1,0:T(8,128)(2,1)}), bf16[256,45,128]{2,1,0:T(8,128)(2,1)}) %all-gather.5.cloned.1.call-update) | async-done | bytes 2949136 | tf_op jit(solution)/shard_map/all_gather | solution.py:91
  350.6 5.5 reshape.214
  358.4 49.9 %all_gather.13 = f32[128,9,160]{0,1,2:T(8,128)S(1)} all-gather(f32[128,9,5]{0,1,2:T(8,128)S(1)} %bitcast.98), channel_id=1, replica_groups=mesh['group'=8,'sub'=32] {'sub'}, dimensions={2}, use_global_device_ids=true | all-gather | bytes 760320 | tf_op jit(solution)/shard_map/all_gather | solution.py:93
  414.2 4.0 scatter_custom_fusion.2
  421.9 72.7 %all-reduce = (f32[128]{0:T(128)S(1)}, f32[128]{0:T(128)S(1)}) all-reduce(f32[128]{0:T(128)S(1)} %multiply_reduce_fusion, f32[128]{0:T(128)S(1)} %reduce_sum.41), channel_id=1, replica_groups=mesh['group'=8,'sub'=32] {'group','sub'}, use_global_device_ids=true, to_apply=%region_7.10 | all-reduce | flops 256 | bytes 2048 | tf_op jit(solution)/shard_map/psum | solution.py:102
  498.8 2.5 copy.53
  501.3 2.6 reshape.130
  504.0 3.0 copy.54
  507.0 212.7 %reduce-scatter.5.cloned.1.call-done = f32[128,9,5]{0,1,2:T(8,128)} async-done(((f32[128,9,160]{0,1,2:T(8,128)}), f32[128,9,5]{0,1,2:T(8,128)}) %reduce-scatter.5.cloned.1.call-update) | async-done | bytes 23056 | tf_op jit(solution)/shard_map/reduce_scatter | solution.py:78
  724.8 21.0 %all_to_all.52 = bf16[1152,32,8]{0,2,1:T(8,128)(2,1)S(1)} all-to-all(bf16[1152,32,8]{0,2,1:T(8,128)(2,1)S(1)} %fusion.21), channel_id=1, replica_groups=mesh['group'=8,'sub'=32] {'sub'}, dimensions={1} | all-to-all | bytes 1179648 | tf_op jit(solution)/shard_map/all_to_all | solution.py:52
  747.8 6.6 fusion
  754.4 2.5 reshape.129
  760.4 5.9 all-to-all-start.4
  767.3 64.5 %all-gather.7.cloned.1.call-done = bf16[256,45,128]{2,1,0:T(8,128)(2,1)} async-done(((bf16[1,45,128]{2,1,0:T(8,128)(2,1)}), bf16[256,45,128]{2,1,0:T(8,128)(2,1)}) %all-gather.7.cloned.1.call-update) | async-done | bytes 2949136 | tf_op jit(solution)/shard_map/all_gather | solution.py:91
  831.8 5.5 reshape.216
  839.6 49.7 %all_gather.15 = f32[128,9,160]{0,1,2:T(8,128)S(1)} all-gather(f32[128,9,5]{0,1,2:T(8,128)S(1)} %bitcast.99), channel_id=1, replica_groups=mesh['group'=8,'sub'=32] {'sub'}, dimensions={2}, use_global_device_ids=true | all-gather | bytes 760320 | tf_op jit(solution)/shard_map/all_gather | solution.py:93
  895.2 4.0 scatter_custom_fusion.4
  (110 shorter events, 56.7 us)
Async XLA Ops:
  7.2 348.9 %copy-start = (bf16[45,11520]{1,0:T(8,128)(2,1)S(1)}, bf16[45,11520]{1,0:T(8,128)(2,1)}, u32[]{:S(2)}) copy-start(bf16[45,11520]{1,0:T(8,128)(2,1)} %param.12) | copy-start | bytes 3110404
  7.2 228.4 %reduce-scatter.3.cloned.1.call-start = ((), (), s32[]{:S(2)}) async-start(), calls=%async_computation.7 | async-start | bytes 1351680 | tf_op jit(solution)/shard_map/reduce_scatter | solution.py:78
  8.7 0.7 copy-start.6
  17.4 219.6 %copy-start.7 = (s32[128,1]{0,1:T(1,128)S(1)}, s32[128,1]{0,1:T(1,128)}, u32[]{:S(2)}) copy-start(s32[128,1]{0,1:T(1,128)} %param.14) | copy-start | bytes 1540
  17.4 333.2 %all-gather.5.cloned.1.call-start = ((), (), s32[]{:S(2)}) async-start(), calls=%async_computation.9 | async-start | bytes 3158016 | tf_op jit(solution)/shard_map/all_gather | solution.py:91
  257.5 18.5 %all-to-all-start.1 = ((bf16[1152,32,8]{0,2,1:T(8,128)(2,1)}), bf16[1152,32,8]{0,2,1:T(8,128)(2,1)S(1)}, u32[]{:S(2)}, u32[]{:S(2)}) async-start(bf16[1152,32,8]{0,2,1:T(8,128)(2,1)} %fusion.20), calls=%async_computation.1 | async-start | bytes 1179648 | tf_op jit(solution)/shard_map/all_to_all | solution.py:52
  288.3 125.9 %all-to-all-start.2 = ((f32[1152,32,8]{0,2,1:T(8,128)}), f32[1152,32,8]{0,2,1:T(8,128)}, u32[]{:S(2)}, u32[]{:S(2)}) async-start(f32[1152,32,8]{0,2,1:T(8,128)} %bitcast.16), calls=%async_computation.3 | async-start | bytes 2359296 | tf_op jit(solution)/shard_map/all_to_all | solution.py:70
  294.0 425.7 %reduce-scatter.5.cloned.1.call-start = ((), (), s32[]{:S(2)}) async-start(), calls=%async_computation.8 | async-start | bytes 1351680 | tf_op jit(solution)/shard_map/reduce_scatter | solution.py:78
  412.4 1.3 copy-start.2
  418.3 1.1 copy-start.1
  419.3 1.3 copy-start.4
  507.0 324.8 %all-gather.7.cloned.1.call-start = ((), (), s32[]{:S(2)}) async-start(), calls=%async_computation.10 | async-start | bytes 3158016 | tf_op jit(solution)/shard_map/all_gather | solution.py:91
  745.8 1.0 copy-start.5
  760.4 134.9 %all-to-all-start.4 = ((f32[1152,32,8]{0,2,1:T(8,128)}), f32[1152,32,8]{0,2,1:T(8,128)}, u32[]{:S(2)}, u32[]{:S(2)}) async-start(f32[1152,32,8]{0,2,1:T(8,128)} %bitcast.97), calls=%async_computation.6 | async-start | bytes 2359296 | tf_op jit(solution)/shard_map/all_to_all | solution.py:70
  893.4 1.3 copy-start.3
Sparse Core Ops, SparseCore 0:
  17.5 217.9 reduce-scatter.2
  239.7 110.8 all-gather.4
  507.1 212.5 reduce-scatter.4
  723.1 108.6 all-gather.6
where the time goes:
time: 909 us; the launch traced here: 907 us
  waiting for transfers between devices  565 us (62%)
  blocking collectives  210 us (23%)
  local copies, waits for them, and re-layouts  62.3 us (7%)
  matrix products  22.8 us (3%)
  starting transfers between devices  16.8 us (2%)
  other arithmetic  16.1 us (2%)
  between operations  14.2 us (2%)
    reduce_scatter x2, waiting for transfers between devices, coarse_reduce(): return lax.psum_scatter(local_sums, 'sub', scatter_dimension=2, tiled=True)  431 us
    all_gather x2, waiting for transfers between devices, coarse_finish(): lax.all_gather(ordered, ('group', 'sub'), axis=1, tiled=True)  121 us
    all_gather x2, blocking collectives, coarse_finish(): return add_clusters(lax.all_gather(solution, 'sub', axis=2, tiled=True))  99.7 us
    psum x1, blocking collectives, body(): inner_rf, inner_ff = lax.psum((part_rf, part_ff), ('group', 'sub'))  72.7 us
    all_to_all x1, blocking collectives, fetch(): lax.all_to_all(outgoing.astype(jnp.bfloat16), 'sub', split_axis=1, concat...  21 us
  transfers between devices with their start and end apart: 7, of which 5 were waited for; matrix products, arithmetic and copies ran while one was open for 7% of the time, Pallas kernels for 0%

commit v1 on v0

v1 whole, which is shorter than its diff:
```python
import jax
import jax.numpy as jnp
from jax import lax
from jax.sharding import PartitionSpec as P

EPSILON = 1e-06
F32 = jnp.float32
BF16 = jnp.bfloat16


def dot(left, right):
    return jnp.dot(left, right, preferred_element_type=F32)


def hot(ids, count):
    return (ids[:, None] == jnp.arange(count, dtype=jnp.int32)[None, :]).astype(BF16)


def hot_t(ids, count):
    return (jnp.arange(count, dtype=jnp.int32)[:, None] == ids[None, :]).astype(BF16)


def exchange(values, axis):
    return lax.all_to_all(values, axis, split_axis=0, concat_axis=0, tiled=True)


def body(residual_in, local_inverse, coarse_inverse, cluster_of, margin_peer, margin_row):
    rhs, comps, own = residual_in.shape
    over = margin_row.shape[0]
    subs = lax.axis_size("sub")
    groups = lax.axis_size("group")
    cap = max(2, 2 * over // subs)
    slots = subs * cap
    cl_rows = coarse_inverse.shape[0]
    cl_dev = cl_rows // comps
    cl_grp = cl_dev * subs
    grp_rows = cl_rows * subs
    width = local_inverse.shape[1]
    cams = width // comps
    lanes = comps * rhs
    inverse = local_inverse[0]

    def aux_row(values):
        return jnp.pad(values, ((0, 0), (0, lanes - values.shape[1])))[:, None, :].astype(BF16)

    def spread_out(values):
        return jnp.broadcast_to(values.astype(BF16)[None], (subs,) + values.shape)

    with jax.named_scope("coarse_block"):
        columns = coarse_inverse.reshape(cl_rows, groups, grp_rows).transpose(1, 0, 2)
        coarse_block = exchange(columns, "group").reshape(groups * cl_rows, grp_rows)

    with jax.named_scope("index"):
        peer = margin_peer[:, 0]
        place = jnp.arange(over, dtype=jnp.int32)
        earlier = (peer[:, None] == peer[None, :]) & (place[None, :] < place[:, None])
        dest = peer * cap + jnp.sum(earlier.astype(jnp.int32), axis=1)
        take = hot(dest, slots)
        take_t = hot_t(dest, slots)
        wanted = jnp.sum(
            jnp.where(jnp.arange(slots, dtype=jnp.int32)[:, None] == dest[None, :], margin_row[None, :] + 1, 0),
            axis=1,
        )
        own_hot = hot_t(cluster_of, cl_grp)
        own_back = hot(cluster_of, cl_grp)
        counts = jnp.sum(own_hot.astype(F32), axis=1)

    with jax.named_scope("restrict"):
        field = residual_in.transpose(2, 1, 0).reshape(own, lanes)
        field16 = field.astype(BF16)
        sums = dot(own_hot, field16).astype(BF16).reshape(subs, cl_dev, lanes)
        extra = aux_row(
            jnp.concatenate([wanted.reshape(subs, cap).astype(F32), counts.reshape(subs, cl_dev)], axis=1)
        )
        got = exchange(jnp.concatenate([sums, extra], axis=1), "sub")
        coarse_in = jnp.sum(got[:, :cl_dev].astype(F32), axis=0)
        asked = got[:, cl_dev, :cap].astype(jnp.int32).reshape(slots) - 1
        members = jnp.sum(got[:, cl_dev, cap : cap + cl_dev].astype(F32), axis=0)[:, None]
        give = hot(asked, own)
        give_t = hot_t(asked, own)

    def solve(own_part, over_part):
        joined = jnp.concatenate([own_part, over_part], axis=0).reshape(cams, comps, rhs)
        flat = joined.transpose(1, 0, 2).reshape(width, rhs)
        result = lax.dot_general(flat, inverse, (((0,), (0,)), ((), ())), preferred_element_type=F32)
        return result.reshape(rhs, comps, cams).transpose(2, 1, 0).reshape(cams, lanes)

    def coarse(gathered, inner):
        column = gathered.reshape(grp_rows, rhs)
        parts = dot(coarse_block, column).reshape(groups, cl_rows, rhs)
        if inner is not None:
            parts = jnp.concatenate([parts, jnp.broadcast_to(inner[None], (groups,) + inner.shape)], axis=1)
        total = jnp.sum(exchange(parts, "group"), axis=0)
        return total[:cl_rows].reshape(cl_dev, lanes), total[cl_rows:]

    with jax.named_scope("fetch_first"):
        clusters = jnp.sum(
            jnp.where(asked[:, None] == jnp.arange(own, dtype=jnp.int32)[None, :], cluster_of[None, :], 0), axis=1
        ).astype(F32)
        sent = jnp.concatenate(
            [
                dot(give, field16).astype(BF16).reshape(subs, cap, lanes),
                spread_out(coarse_in),
                aux_row(clusters.reshape(subs, cap)),
            ],
            axis=1,
        )
        got = exchange(sent, "sub")
        over_field = dot(take, got[:, :cap].reshape(slots, lanes)).astype(BF16)
        over_ids = dot(take, got[:, cap + cl_dev, :cap].reshape(slots, 1))[:, 0].astype(jnp.int32)
        over_hot = hot_t(over_ids, cl_grp)
        over_back = hot(over_ids, cl_grp)
    with jax.named_scope("coarse_first"):
        sol, _ = coarse(got[:, cap : cap + cl_dev].reshape(cl_grp, lanes), None)
    with jax.named_scope("solve_first"):
        result = solve(field16, over_field)
        result16 = result.astype(BF16)

    with jax.named_scope("return_first"):
        sums = dot(jnp.concatenate([own_hot, over_hot], axis=1), result16).astype(BF16)
        back = dot(take_t, result16[own:]).astype(BF16)
        sent = jnp.concatenate([back.reshape(subs, cap, lanes), sums.reshape(subs, cl_dev, lanes)], axis=1)
        got = exchange(sent, "sub")
        spread = result[:own] + dot(give_t, got[:, :cap].reshape(slots, lanes))
        coarse_in = jnp.sum(got[:, cap:].astype(F32), axis=0) + members * sol

    with jax.named_scope("fetch_second"):
        sent = jnp.concatenate(
            [
                dot(give, spread.astype(BF16)).astype(BF16).reshape(subs, cap, lanes),
                spread_out(coarse_in),
                spread_out(sol),
            ],
            axis=1,
        )
        got = exchange(sent, "sub")
        solution_all = got[:, cap + cl_dev :].reshape(cl_grp, lanes)
        first = spread + dot(own_back, solution_all)
        over_first = dot(take, got[:, :cap].reshape(slots, lanes)) + dot(over_back, solution_all)
        inner = jnp.stack(
            [
                jnp.sum((field * first).reshape(own * comps, rhs), axis=0),
                jnp.sum((first * first).reshape(own * comps, rhs), axis=0),
            ]
        )
    with jax.named_scope("coarse_second"):
        sol, inner = coarse(got[:, cap : cap + cl_dev].reshape(cl_grp, lanes), inner)
    with jax.named_scope("solve_second"):
        result = solve(first.astype(BF16), over_first.astype(BF16))

    with jax.named_scope("return_second"):
        back = dot(take_t, result[own:].astype(BF16)).astype(BF16)
        high = inner.astype(BF16)
        low = inner - high.astype(F32)
        pair = jnp.concatenate([high.astype(F32), low], axis=0).reshape(1, 4 * rhs)
        sent = jnp.concatenate(
            [
                back.reshape(subs, cap, lanes),
                spread_out(sol),
                aux_row(jnp.broadcast_to(pair, (subs, 4 * rhs))),
            ],
            axis=1,
        )
        got = exchange(sent, "sub")
        solution_all = got[:, cap : cap + cl_dev].reshape(cl_grp, lanes)
        applied = result[:own] + dot(give_t, got[:, :cap].reshape(slots, lanes)) + dot(own_back, solution_all)
        pair = jnp.sum(got[:, cap + cl_dev, : 4 * rhs].astype(F32), axis=0).reshape(2, 2, rhs)
        inner = pair[0] + pair[1]
        scale = inner[0] / (inner[1] + EPSILON)
        second = first - jnp.tile(scale, comps)[None, :] * applied

    def place_out(values):
        return values.reshape(own, comps, rhs).transpose(2, 1, 0)

    return place_out(first), place_out(second)


def solution(mesh):
    placed = (
        P(None, None, ("group", "sub")),
        P(("group", "sub"), None, None),
        P(("group", "sub"), None),
        P(("group", "sub")),
        P(("group", "sub"), None),
        P(("group", "sub")),
    )
    return jax.shard_map(
        body,
        mesh=mesh,
        in_specs=placed,
        out_specs=(P(None, None, ("group", "sub")), P(None, None, ("group", "sub"))),
        check_vma=False,
    )
```

time: 909 us -> 272 us (0.30)
  waiting for transfers between devices: 565 us -> 97 us
  blocking collectives: 210 us -> 47.9 us
  starting transfers between devices: 16.8 us -> 42.8 us
  local copies, waits for them, and re-layouts: 62.3 us -> 43.4 us
  between operations: 14.2 us -> 1.14 us
    reduce_scatter x2 -> x0, waiting for transfers between devices: 431 us -> none  [coarse_reduce(): return lax.psum_scatter(local_sums, 'sub', scatter_dimension=2, tiled=True)]
    all_gather x2 -> x0, waiting for transfers between devices: 121 us -> none  [coarse_finish(): lax.all_gather(ordered, ('group', 'sub'), axis=1, tiled=True)]
    all_gather x2 -> x0, blocking collectives: 99.7 us -> none  [coarse_finish(): return add_clusters(lax.all_gather(solution, 'sub', axis=2, tiled=True))]
    all_to_all x3 -> x7, waiting for transfers between devices: 13.4 us -> 97 us  [exchange(): return lax.all_to_all(values, axis, split_axis=0, concat_axis=0, tiled=True)]
    psum x1 -> x0, blocking collectives: 72.7 us -> none  [body(): inner_rf, inner_ff = lax.psum((part_rf, part_ff), ('group', 'sub'))]
    all_to_all x3 -> x7, starting transfers between devices: 16.6 us -> 42.8 us  [exchange(): return lax.all_to_all(values, axis, split_axis=0, concat_axis=0, tiled=True)]
    all_to_all x2 -> x1, blocking collectives: 37.4 us -> 47.9 us  [exchange(): return lax.all_to_all(values, axis, split_axis=0, concat_axis=0, tiled=True)]
    reshape x14 -> x16, local copies, waits for them, and re-layouts: 18.6 us -> 15.2 us  [the longest x2 4.23 us: body(): coarse_inverse.reshape(cl_rows, groups, grp_rows).transpose(1, 0, 2)]
  transfers between devices with their start and end apart: 7 -> 7, of which waited for: 5 -> 5; matrix products, arithmetic and copies ran while one was open for 7% -> 18% of each run, Pallas kernels for 0% -> 0%
where the time goes in v1:
time: 272 us; the launch traced here: 270 us
  waiting for transfers between devices  97 us (36%)
  blocking collectives  47.9 us (18%)
  local copies, waits for them, and re-layouts  43.4 us (16%)
  starting transfers between devices  42.8 us (16%)
  matrix products  25.2 us (9%)
  other arithmetic  13.1 us (5%)
    all_to_all x7, waiting for transfers between devices, exchange(): return lax.all_to_all(values, axis, split_axis=0, concat_axis=0, tiled=True)  97 us
    all_to_all x1, blocking collectives, exchange(): return lax.all_to_all(values, axis, split_axis=0, concat_axis=0, tiled=True)  47.9 us
    all_to_all x7, starting transfers between devices, exchange(): return lax.all_to_all(values, axis, split_axis=0, concat_axis=0, tiled=True)  42.8 us
    unnamed x29, local copies, waits for them, and re-layouts  18.3 us
    dot_general x2, matrix products, solve(): lax.dot_general(flat, inverse, (((0,), (0,)), ((), ())), preferred_elemen...  16.2 us
    dot_general x16, matrix products, dot(): return jnp.dot(left, right, preferred_element_type=F32)  8.93 us
  transfers between devices with their start and end apart: 7, of which 5 were waited for; matrix products, arithmetic and copies ran while one was open for 18% of the time, Pallas kernels for 0%

profile of v1, /device:TPU:10, one launch (start us, length us, event | category | flops | bytes accessed | tf_op | source)
XLA Modules:
  0.0 270.5 jit_solution(4852828058807806707)
XLA Ops:
  6.4 11.6 %all-to-all-start = ((bf16[32,6,1152]{2,1,0:T(8,128)(2,1)}), bf16[32,6,1152]{2,1,0:T(8,128)(2,1)S(1)}, u32[]{:S(2)}, u32[]{:S(2)}) async-start(bf16[32,6,1152]{2,1,0:T(8,128)(2,1)} %pad_maximum_fusion.4), calls=%async_computation | async-start | bytes 1179648 | tf_op jit(solution)/shard_map/restrict/all_to_all | solution.py:24
  18.0 2.9 %reshape.241 = bf16[45,8,1440]{2,1,0:T(8,128)(2,1)S(1)} reshape(bf16[45,11520]{1,0:T(8,128)(2,1)} %param.8) | data formatting | bytes 2073600 | tf_op jit(solution)/shard_map/coarse_block/reshape | solution.py:50
  22.3 14.0 %all-to-all-done = bf16[32,6,1152]{2,1,0:T(8,128)(2,1)S(1)} async-done(((bf16[32,6,1152]{2,1,0:T(8,128)(2,1)}), bf16[32,6,1152]{2,1,0:T(8,128)(2,1)S(1)}, u32[]{:S(2)}, u32[]{:S(2)}) %all-to-all-start) | async-done | bytes 442400 | tf_op jit(solution)/shard_map/restrict/all_to_all | solution.py:24
  36.3 4.9 %all-to-all-start.3 = ((bf16[8,45,1440]{2,1,0:T(8,128)(2,1)}), bf16[8,45,1440]{2,1,0:T(8,128)(2,1)S(1)}, u32[]{:S(2)}, u32[]{:S(2)}) async-start(bf16[8,45,1440]{2,1,0:T(8,128)(2,1)} %bitcast.100), calls=%async_computation.3 | async-start | bytes 2359296 | tf_op jit(solution)/shard_map/coarse_block/all_to_all | solution.py:24
  43.7 13.4 %all-to-all-done.3 = bf16[8,45,1440]{2,1,0:T(8,128)(2,1)S(1)} async-done(((bf16[8,45,1440]{2,1,0:T(8,128)(2,1)}), bf16[8,45,1440]{2,1,0:T(8,128)(2,1)S(1)}, u32[]{:S(2)}, u32[]{:S(2)}) %all-to-all-start.3) | async-done | bytes 1036832 | tf_op jit(solution)/shard_map/coarse_block/all_to_all | solution.py:24
  58.2 5.6 %all-to-all-start.1 = ((bf16[32,14,1152]{2,1,0:T(8,128)(2,1)}), bf16[32,14,1152]{2,1,0:T(8,128)(2,1)S(1)}, u32[]{:S(2)}, u32[]{:S(2)}) async-start(bf16[32,14,1152]{2,1,0:T(8,128)(2,1)} %pad_maximum_fusion.1), calls=%async_computation.1 | async-start | bytes 2359296 | tf_op jit(solution)/shard_map/fetch_first/all_to_all | solution.py:24
  63.7 14.5 %copy.38 = bf16[1,2304,2304]{1,2,0:T(8,128)(2,1)} copy(bf16[1,2304,2304]{2,1,0:T(8,128)(2,1)} %param.7) | data formatting | bytes 21233664 | tf_op args[1]
  78.8 1.8 reshape.242
  80.6 13.8 %all-to-all-done.1 = bf16[32,14,1152]{2,1,0:T(8,128)(2,1)S(1)} async-done(((bf16[32,14,1152]{2,1,0:T(8,128)(2,1)}), bf16[32,14,1152]{2,1,0:T(8,128)(2,1)S(1)}, u32[]{:S(2)}, u32[]{:S(2)}) %all-to-all-start.1) | async-done | bytes 1032224 | tf_op jit(solution)/shard_map/fetch_first/all_to_all | solution.py:24
  96.3 1.5 reshape.240
  99.8 4.8 %all-to-all-start.4 = ((f32[8,45,128]{2,1,0:T(8,128)}), f32[8,45,128]{2,1,0:T(8,128)S(1)}, u32[]{:S(2)}, u32[]{:S(2)}) async-start(f32[8,45,128]{2,1,0:T(8,128)} %reshape.243), calls=%async_computation.4 | async-start | bytes 393216 | tf_op jit(solution)/shard_map/coarse_first/all_to_all | solution.py:24
  104.6 8.7 %fusion.42 = (bf16[256,9,128]{0,2,1:T(8,128)(2,1)S(1)}, f32[256,9,128]{0,2,1:T(8,128)}) fusion(bf16[2304,128,1]{1,0,2:T(8,128)(2,1)S(1)} %bitcast.105, bf16[9,256,2304]{2,1,0:T(8,128)(2,1)} %bitcast.101), kind=kOutput, calls=%fused_computation.107 | convolution fusion | flops 1359249408 | bytes 12976128 | tf_op jit(solution)/shard_map/solve_first/dot_general | solution.py:85
  116.1 5.6 %all-to-all-start.2 = ((bf16[32,13,1152]{2,1,0:T(8,128)(2,1)}), bf16[32,13,1152]{2,1,0:T(8,128)(2,1)S(1)}, u32[]{:S(2)}, u32[]{:S(2)}) async-start(bf16[32,13,1152]{2,1,0:T(8,128)(2,1)} %pad_maximum_fusion.2), calls=%async_computation.2 | async-start | bytes 2359296 | tf_op jit(solution)/shard_map/return_first/all_to_all | solution.py:24
  122.6 1.9 slice.134
  126.8 26.0 %all-to-all-done.2 = bf16[32,13,1152]{2,1,0:T(8,128)(2,1)S(1)} async-done(((bf16[32,13,1152]{2,1,0:T(8,128)(2,1)}), bf16[32,13,1152]{2,1,0:T(8,128)(2,1)S(1)}, u32[]{:S(2)}, u32[]{:S(2)}) %all-to-all-start.2) | async-done | bytes 958496 | tf_op jit(solution)/shard_map/return_first/all_to_all | solution.py:24
  154.4 47.9 %all_to_all.40 = bf16[32,18,1152]{2,1,0:T(8,128)(2,1)S(1)} all-to-all(bf16[32,18,1152]{2,1,0:T(8,128)(2,1)S(1)} %pad_maximum_fusion), channel_id=1, replica_groups=mesh['group'=8,'sub'=32] {'sub'}, dimensions={0} | all-to-all | bytes 2654208 | tf_op jit(solution)/shard_map/fetch_second/all_to_all | solution.py:24
  203.4 2.2 reshape.251
  205.6 2.1 convolution_bitcast_fusion.2
  207.8 1.6 reshape.252
  210.6 2.5 fusion.41
  217.4 4.8 %all-to-all-start.6 = ((f32[8,47,128]{2,1,0:T(8,128)}), f32[8,47,128]{2,1,0:T(8,128)S(1)}, u32[]{:S(2)}, u32[]{:S(2)}) async-start(f32[8,47,128]{2,1,0:T(8,128)} %pad_maximum_fusion.7), calls=%async_computation.6 | async-start | bytes 393216 | tf_op jit(solution)/shard_map/coarse_second/all_to_all | solution.py:24
  222.2 7.6 %convolution_bitcast_fusion = f32[256,9,128]{0,2,1:T(8,128)S(1)} fusion(bf16[2304,128,1]{1,0,2:T(8,128)(2,1)S(1)} %bitcast.104, bf16[9,256,2304]{2,1,0:T(8,128)(2,1)} %bitcast.102), kind=kOutput, calls=%fused_computation.20 | convolution fusion | flops 1358954496 | bytes 12386304 | tf_op jit(solution)/shard_map/solve_second/dot_general | solution.py:85
  231.7 5.6 %all-to-all-start.7 = ((bf16[32,14,1152]{2,1,0:T(8,128)(2,1)}), bf16[32,14,1152]{2,1,0:T(8,128)(2,1)S(1)}, u32[]{:S(2)}, u32[]{:S(2)}) async-start(bf16[32,14,1152]{2,1,0:T(8,128)(2,1)} %pad_maximum_fusion.3), calls=%async_computation.7 | async-start | bytes 2359296 | tf_op jit(solution)/shard_map/return_second/all_to_all | solution.py:24
  238.7 29.9 %all-to-all-done.7 = bf16[32,14,1152]{2,1,0:T(8,128)(2,1)S(1)} async-done(((bf16[32,14,1152]{2,1,0:T(8,128)(2,1)}), bf16[32,14,1152]{2,1,0:T(8,128)(2,1)S(1)}, u32[]{:S(2)}, u32[]{:S(2)}) %all-to-all-start.7) | async-done | bytes 1032224 | tf_op jit(solution)/shard_map/return_second/all_to_all | solution.py:24
  (122 shorter events, 34.4 us)
Async XLA Ops:
  3.3 1.6 copy-start.10
  6.4 29.9 %all-to-all-start = ((bf16[32,6,1152]{2,1,0:T(8,128)(2,1)}), bf16[32,6,1152]{2,1,0:T(8,128)(2,1)S(1)}, u32[]{:S(2)}, u32[]{:S(2)}) async-start(bf16[32,6,1152]{2,1,0:T(8,128)(2,1)} %pad_maximum_fusion.4), calls=%async_computation | async-start | bytes 1179648 | tf_op jit(solution)/shard_map/restrict/all_to_all | solution.py:24
  36.3 5.9 %copy-start.2 = (bf16[32,6,1152]{2,1,0:T(8,128)(2,1)}, bf16[32,6,1152]{2,1,0:T(8,128)(2,1)S(1)}, u32[]{:S(2)}) copy-start(bf16[32,6,1152]{2,1,0:T(8,128)(2,1)S(1)} %all-to-all-done) | copy-start | bytes 1327108
  36.3 20.8 %all-to-all-start.3 = ((bf16[8,45,1440]{2,1,0:T(8,128)(2,1)}), bf16[8,45,1440]{2,1,0:T(8,128)(2,1)S(1)}, u32[]{:S(2)}, u32[]{:S(2)}) async-start(bf16[8,45,1440]{2,1,0:T(8,128)(2,1)} %bitcast.100), calls=%async_computation.3 | async-start | bytes 2359296 | tf_op jit(solution)/shard_map/coarse_block/all_to_all | solution.py:24
  57.1 1.1 copy-start.1
  58.2 36.2 %all-to-all-start.1 = ((bf16[32,14,1152]{2,1,0:T(8,128)(2,1)}), bf16[32,14,1152]{2,1,0:T(8,128)(2,1)S(1)}, u32[]{:S(2)}, u32[]{:S(2)}) async-start(bf16[32,14,1152]{2,1,0:T(8,128)(2,1)} %pad_maximum_fusion.1), calls=%async_computation.1 | async-start | bytes 2359296 | tf_op jit(solution)/shard_map/fetch_first/all_to_all | solution.py:24
  63.7 14.5 %copy-start.13 = (s32[128,1]{0,1:T(1,128)S(1)}, s32[128,1]{0,1:T(1,128)}, u32[]{:S(2)}) copy-start(s32[128,1]{0,1:T(1,128)} %param.10) | copy-start | bytes 1540
  94.8 0.6 copy-start.11
  99.8 15.5 %all-to-all-start.4 = ((f32[8,45,128]{2,1,0:T(8,128)}), f32[8,45,128]{2,1,0:T(8,128)S(1)}, u32[]{:S(2)}, u32[]{:S(2)}) async-start(f32[8,45,128]{2,1,0:T(8,128)} %reshape.243), calls=%async_computation.4 | async-start | bytes 393216 | tf_op jit(solution)/shard_map/coarse_first/all_to_all | solution.py:24
  104.6 8.7 %copy-start.8 = (bf16[160,128]{1,0:T(8,128)(2,1)S(1)}, bf16[160,128]{1,0:T(8,128)(2,1)}, u32[]{:S(2)}) copy-start(bf16[160,128]{1,0:T(8,128)(2,1)} %fusion.15) | copy-start | bytes 122884
  104.6 8.7 %copy-start.9 = (bf16[160,128]{1,0:T(8,128)(2,1)S(1)}, bf16[160,128]{1,0:T(8,128)(2,1)}, u32[]{:S(2)}) copy-start(bf16[160,128]{1,0:T(8,128)(2,1)} %fusion.16) | copy-start | bytes 122884
  115.4 0.7 copy-start.7
  116.1 36.8 %all-to-all-start.2 = ((bf16[32,13,1152]{2,1,0:T(8,128)(2,1)}), bf16[32,13,1152]{2,1,0:T(8,128)(2,1)S(1)}, u32[]{:S(2)}, u32[]{:S(2)}) async-start(bf16[32,13,1152]{2,1,0:T(8,128)(2,1)} %pad_maximum_fusion.2), calls=%async_computation.2 | async-start | bytes 2359296 | tf_op jit(solution)/shard_map/return_first/all_to_all | solution.py:24
  153.1 0.8 copy-start
  213.1 0.7 copy-start.12
  213.8 1.1 copy-start.4
  214.1 1.0 copy-start.5
  215.1 1.1 copy-start.3
  215.7 1.0 copy-start.6
  217.4 12.8 %all-to-all-start.6 = ((f32[8,47,128]{2,1,0:T(8,128)}), f32[8,47,128]{2,1,0:T(8,128)S(1)}, u32[]{:S(2)}, u32[]{:S(2)}) async-start(f32[8,47,128]{2,1,0:T(8,128)} %pad_maximum_fusion.7), calls=%async_computation.6 | async-start | bytes 393216 | tf_op jit(solution)/shard_map/coarse_second/all_to_all | solution.py:24
  231.7 36.8 %all-to-all-start.7 = ((bf16[32,14,1152]{2,1,0:T(8,128)(2,1)}), bf16[32,14,1152]{2,1,0:T(8,128)(2,1)S(1)}, u32[]{:S(2)}, u32[]{:S(2)}) async-start(bf16[32,14,1152]{2,1,0:T(8,128)(2,1)} %pad_maximum_fusion.3), calls=%async_computation.7 | async-start | bytes 2359296 | tf_op jit(solution)/shard_map/return_second/all_to_all | solution.py:24

commit v2 on v0

v2 whole, which is shorter than its diff:
```python
import functools

import jax
import jax.numpy as jnp
import numpy as np
from jax import lax
from jax.experimental import pallas as pl
from jax.experimental.pallas import tpu as pltpu
from jax.sharding import PartitionSpec as P

EPSILON = 1e-06
F32 = jnp.float32
BF16 = jnp.bfloat16
LANES = 128
ROWS = 8


def dot(left, right):
    return jnp.dot(left, right, preferred_element_type=F32)


def exchange(values, axis):
    return lax.all_to_all(values, axis, split_axis=0, concat_axis=0, tiled=True)


def tile(values, index):
    return values[:, index * LANES : (index + 1) * LANES]


def iota(shape, axis):
    return lax.broadcasted_iota(jnp.int32, shape, axis)


def over_rows(values, subs):
    cube = values.reshape(subs, ROWS, LANES)
    return jnp.broadcast_to(jnp.sum(cube, axis=1, keepdims=True), cube.shape).reshape(subs * ROWS, LANES)


def one_row(values, row, subs):
    cube = values.reshape(subs, ROWS, LANES)
    return jnp.broadcast_to(cube[:, row : row + 1, :], cube.shape).reshape(subs * ROWS, LANES)


def repeat_rows(values, subs):
    return jnp.broadcast_to(values[None], (subs,) + values.shape).reshape(subs * ROWS, values.shape[1])


def kernel_call(body, outs, *args, **kw):
    return pl.pallas_call(
        body,
        out_shape=[jax.ShapeDtypeStruct(shape, dtype) for shape, dtype in outs],
        compiler_params=pltpu.CompilerParams(vmem_limit_bytes=48 * 1024 * 1024),
        **kw,
    )(*args)


def make(rhs, comps, own, over, subs, groups, cl_dev):
    tail = ROWS - cl_dev
    main = comps - tail
    slots = subs * ROWS
    lanes = comps * LANES
    block = main * LANES
    aux = main - 1

    def pack(sums, extra, ref, offset):
        inner = iota((slots, LANES), 0) % ROWS
        for t in range(main):
            value = tile(sums, t)
            if t < cl_dev:
                for j in range(tail):
                    value = jnp.where(inner == cl_dev + j, one_row(tile(sums, main + j), t, subs), value)
            elif extra is not None:
                value = jnp.where(inner == cl_dev, extra, value)
            ref[:, offset + t * LANES : offset + (t + 1) * LANES] = value.astype(BF16)

    def prolong(tiles, own8t, own_tail, own_kind):
        head = dot(own8t, tiles)
        picked = dot(own_tail, tiles[:, : cl_dev * LANES])
        parts = [head]
        for j in range(tail):
            rows = picked[j * own : (j + 1) * own]
            value = jnp.zeros((own, LANES), F32)
            for t in range(cl_dev):
                value = jnp.where(own_kind == t, tile(rows, t), value)
            parts.append(value)
        return jnp.concatenate(parts, axis=1)

    def begin(res, cl, peer, row, field, field16, fieldr, send, own8, own8t, own_tail, own_kind, take, take_t):
        for k in range(comps):
            values = res[:, k, :]
            turned = values.T
            field[:, k * LANES : (k + 1) * LANES] = turned
            field16[:, k * LANES : (k + 1) * LANES] = turned.astype(BF16)
            fieldr[:, k * LANES : (k + 1) * LANES] = values.astype(BF16)
        number = cl[...]
        holder = ((number.astype(F32) + 0.5) * (1.0 / cl_dev)).astype(jnp.int32)
        kind = number - holder * cl_dev
        rows = iota((slots, own), 0)
        lane = iota((slots, LANES), 1)
        inner = rows % ROWS
        hot = (rows == holder * ROWS + kind).astype(F32)
        own8[...] = hot.astype(BF16)
        own8t[...] = hot.T.astype(BF16)
        for j in range(tail):
            hot_j = (rows == holder * ROWS + (cl_dev + j)).astype(F32)
            own_tail[j * own : (j + 1) * own, :] = hot_j.T.astype(BF16)
        own_kind[...] = jnp.broadcast_to(kind.astype(F32), (LANES, own)).T
        peers = jnp.broadcast_to(peer[...].astype(F32), (over, over))
        same = (peers == peers.T) & (iota((over, over), 0) < iota((over, over), 1))
        rank = jnp.sum(same.astype(F32), axis=0, keepdims=True).astype(jnp.int32)
        dest = peer[...] * ROWS + rank
        hot_dest = (iota((slots, over), 0) == dest).astype(F32)
        take_t[...] = hot_dest.astype(BF16)
        take[...] = hot_dest.T.astype(BF16)
        wanted = jnp.sum(hot_dest * (row[...] + 1).astype(F32), axis=1, keepdims=True)
        counts = jnp.sum(hot, axis=1, keepdims=True)
        extra = jnp.where(lane == inner, wanted, 0.0) + jnp.where(lane == inner + ROWS, counts, 0.0)
        pack(dot(own8[...], field16[...]), over_rows(extra, subs), send, 0)

    def answer(got, field16, cl, send, give, give_t, members):
        lane = iota((slots, LANES), 1)
        inner = iota((slots, LANES), 0) % ROWS
        total = jnp.sum(got[...].astype(F32).reshape(subs, ROWS, block), axis=0)
        asked = one_row(tile(got, aux).astype(F32), cl_dev, subs)
        asked = jnp.sum(jnp.where(lane == inner, asked, 0.0), axis=1, keepdims=True) - 1.0
        hot = (iota((slots, own), 1).astype(F32) == asked).astype(F32)
        give[...] = hot.astype(BF16)
        give_t[...] = hot.T.astype(BF16)
        send[:, :lanes] = dot(give[...], field16[...]).astype(BF16)
        ids = jnp.sum(hot * cl[...].astype(F32), axis=1, keepdims=True)
        ids = over_rows(jnp.where(lane == inner, ids, 0.0), subs)
        small = iota((ROWS, LANES), 0)
        small_lane = iota((ROWS, LANES), 1)
        numbers = [
            jnp.sum(
                jnp.where((small_lane == ROWS + c) & (small == cl_dev), tile(total, aux), 0.0),
                axis=(0, 1),
                keepdims=True,
            )
            for c in range(cl_dev)
        ]
        base = jnp.zeros((ROWS, LANES), F32)
        for c in range(cl_dev):
            base = jnp.where(small == c, numbers[c], base)
        for t in range(main):
            value = repeat_rows(tile(total, t), subs)
            count = base
            if t < cl_dev:
                count = jnp.where(small < cl_dev, base, numbers[t])
            else:
                value = jnp.where(inner == cl_dev, ids, value)
            send[:, lanes + t * LANES : lanes + (t + 1) * LANES] = value.astype(BF16)
            members[:, t * LANES : (t + 1) * LANES] = count

    def coarse(offset, rows, matrix, got, *refs):
        out = refs[-1]
        total = jnp.zeros((matrix.shape[0], LANES), F32)
        for t in range(main):
            total += dot(matrix[:, t * slots : (t + 1) * slots], got[:, offset + t * LANES : offset + (t + 1) * LANES])
        each = main * ROWS
        for g in range(groups):
            out[g, :each, :] = total[g * each : (g + 1) * each].astype(BF16)
        if rows > each:
            inner = refs[0][...]
            high = inner.astype(BF16).astype(F32)
            last = jnp.concatenate([high, inner - high, jnp.zeros((rows - each - 4, LANES), F32)], axis=0)
            for g in range(groups):
                out[g, each:, :] = last.astype(BF16)

    def group_total(got):
        total = jnp.sum(got[...].astype(F32), axis=0)
        return total, [total[t * ROWS : (t + 1) * ROWS] for t in range(main)]

    def half(fieldr, inverse, out):
        step = pl.program_id(0)
        columns = pl.ds(pl.multiple_of(step * fieldr.shape[1] // 3, LANES), fieldr.shape[1] // 3)
        product = dot(fieldr[:, columns], inverse[...].reshape(fieldr.shape[1] // 3, inverse.shape[-1]))

        @pl.when(step == 0)
        def _():
            out[...] = product

        @pl.when(step > 0)
        def _():
            out[...] += product

    def half_first(values, field, inverse, first_out, inner, out, turned):
        @pl.when(pl.program_id(0) == 0)
        def _():
            rf = jnp.zeros((1, LANES), F32)
            ff = jnp.zeros((1, LANES), F32)
            for k in range(comps):
                mine = tile(values, k)
                flipped = mine.T
                first_out[:, k, :] = flipped
                turned[:, k * LANES : (k + 1) * LANES] = flipped.astype(BF16)
                rf += jnp.sum(tile(field, k) * mine, axis=0, keepdims=True)
                ff += jnp.sum(mine * mine, axis=0, keepdims=True)
            inner[...] = jnp.concatenate([rf, ff], axis=0)

        half(turned, inverse, out)

    def finish(full, got, part, inverse, take, take_t, own8, res_own, send, turned, total, own16, over16):
        step = pl.program_id(0)

        @pl.when(step == 0)
        def _():
            arrived = dot(take[...], got[:, :lanes])
            for k in range(comps):
                turned[:, k * LANES : (k + 1) * LANES] = tile(arrived, k).T.astype(BF16)
            total[...] = part[...]

        third = lanes // 3
        columns = pl.ds(pl.multiple_of(step * third, LANES), third)
        total[...] += dot(turned[:, columns], inverse[...].reshape(third, inverse.shape[-1]))

        @pl.when(step == 2)
        def _():
            cams = own + over
            for k in range(comps):
                flipped = total[:, k * cams : (k + 1) * cams].T
                res_own[:, k * LANES : (k + 1) * LANES] = flipped[:own]
                if full:
                    own16[:, k * LANES : (k + 1) * LANES] = flipped[:own].astype(BF16)
                over16[:, k * LANES : (k + 1) * LANES] = flipped[own:].astype(BF16)
            send[:, :lanes] = dot(take_t[...], over16[...]).astype(BF16)
            if full:
                lane = iota((slots, LANES), 1)
                inner = iota((slots, LANES), 0) % ROWS
                ids = one_row(got[:, lanes + aux * LANES : lanes + (aux + 1) * LANES].astype(F32), cl_dev, subs)
                ids = jnp.sum(jnp.where(lane == inner, ids, 0.0), axis=1, keepdims=True)
                number = jnp.sum(take_t[...].astype(F32) * ids, axis=0, keepdims=True)
                holder = ((number + 0.5) * (1.0 / cl_dev)).astype(jnp.int32)
                kind = number.astype(jnp.int32) - holder * cl_dev
                over8 = (iota((slots, over), 0) == holder * ROWS + kind).astype(F32).astype(BF16)
                sums = dot(own8[...], own16[...]) + dot(over8, over16[...])
                pack(sums, None, send, lanes)

    def join_first(sent, got, send, sol):
        send[:, : lanes + block] = sent[...]
        _, tiles = group_total(got)
        for t in range(main):
            sol[:, t * LANES : (t + 1) * LANES] = tiles[t]
            send[:, lanes + block + t * LANES : lanes + block + (t + 1) * LANES] = repeat_rows(tiles[t], subs).astype(BF16)

    def join_second(sent, got, send):
        send[:, :lanes] = sent[...]
        total, tiles = group_total(got)
        each = main * ROWS
        inner = total[each : each + 2] + total[each + 2 : each + 4]
        small = iota((ROWS, LANES), 0)
        for t in range(main):
            value = tiles[t]
            if t == aux:
                value = jnp.where(small == cl_dev, inner[0:1], value)
                value = jnp.where(small == cl_dev + 1, inner[1:2], value)
            send[:, lanes + t * LANES : lanes + (t + 1) * LANES] = repeat_rows(value, subs).astype(BF16)

    def combine(got, res_own, give, give_t, own8t, own_tail, own_kind, members, sol, first, send):
        values = res_own[...] + dot(give_t[...], got[:, :lanes])
        values += prolong(got[:, lanes + block :], own8t[...], own_tail[...], own_kind[...])
        first[...] = values
        send[:, :lanes] = dot(give[...], values.astype(BF16)).astype(BF16)
        total = jnp.sum(got[:, lanes : lanes + block].astype(F32).reshape(subs, ROWS, block), axis=0)
        total += members[...] * sol[...]
        send[:, lanes:] = repeat_rows(total, subs).astype(BF16)

    def end(got, res_own, first, give_t, own8t, own_tail, own_kind, out):
        applied = res_own[...] + dot(give_t[...], got[:, :lanes])
        applied += prolong(got[:, lanes:], own8t[...], own_tail[...], own_kind[...])
        sums = got[:, lanes + aux * LANES :].astype(F32).reshape(subs, ROWS, LANES)
        sums = jnp.sum(sums, axis=0)
        scale = sums[cl_dev : cl_dev + 1] / (sums[cl_dev + 1 : cl_dev + 2] + EPSILON)
        for k in range(comps):
            out[:, k, :] = (tile(first, k) - scale * tile(applied, k)).T

    return dict(locals())


def block_order(cl_dev, comps, count):
    tail = ROWS - cl_dev
    main = comps - tail
    order = np.full((main, count, ROWS), -1, np.int32)
    for t in range(main):
        for i in range(ROWS):
            if i < cl_dev:
                order[t, :, i] = np.arange(count) * cl_dev * comps + i * comps + t
            elif t < cl_dev:
                order[t, :, i] = np.arange(count) * cl_dev * comps + t * comps + main + i - cl_dev
    return order.reshape(-1)


def regroup(coarse_inverse, groups, subs, cl_dev, comps):
    cl_rows = cl_dev * comps
    grp_rows = cl_rows * subs
    row_order = block_order(cl_dev, comps, 1)
    col_order = block_order(cl_dev, comps, subs)
    pick_rows = jnp.asarray(row_order[:, None] == np.arange(cl_rows)[None, :]).astype(BF16)
    pick_cols = (jnp.asarray(col_order)[None, :] == jnp.arange(grp_rows, dtype=jnp.int32)[:, None]).astype(BF16)
    values = coarse_inverse.reshape(cl_rows, groups, grp_rows)
    values = lax.dot_general(pick_rows, values, (((1,), (0,)), ((), ())), preferred_element_type=F32).astype(BF16)
    values = values.transpose(1, 0, 2).reshape(groups * row_order.size, grp_rows)
    values = dot(values, pick_cols).astype(BF16).reshape(groups, row_order.size, col_order.size)
    if groups == 1:
        return values.reshape(-1, col_order.size)
    turns = groups // 2
    index = lax.axis_index("group")
    core, turn = index % 2, index // 2
    pairs = values.reshape(turns, 2, row_order.size, col_order.size)
    kept = lax.dynamic_index_in_dim(pairs, core, 1, keepdims=False)
    given = lax.dynamic_index_in_dim(pairs, 1 - core, 1, keepdims=False)
    other = lax.ppermute(given, "group", [(i, i ^ 1) for i in range(groups)])
    both = jnp.where(core == 0, jnp.stack([kept, other], axis=1), jnp.stack([other, kept], axis=1))
    arrived = [lax.dynamic_index_in_dim(both, turn, 0, keepdims=False)]
    for step in range(1, turns):
        target = lax.dynamic_index_in_dim(both, (turn - step) % turns, 0, keepdims=False)
        arrived.append(lax.ppermute(target, "group", [(i, (i - 2 * step) % groups) for i in range(groups)]))
    ring = jnp.stack(arrived + arrived[:-1], axis=0)
    ring = lax.dynamic_slice_in_dim(ring, (turns - turn) % turns, turns, 0)
    return ring.reshape(groups * row_order.size, col_order.size)


def body(residual_in, local_inverse, coarse_inverse, cluster_of, margin_peer, margin_row):
    rhs, comps, own = residual_in.shape
    over = margin_row.shape[0]
    subs = lax.axis_size("sub")
    groups = lax.axis_size("group")
    cl_dev = coarse_inverse.shape[0] // comps
    width = local_inverse.shape[1]
    m = make(rhs, comps, own, over, subs, groups, cl_dev)
    slots, lanes, block, main, tail = m["slots"], m["lanes"], m["block"], m["main"], m["tail"]
    each = main * ROWS
    inverse = local_inverse.reshape(comps, 2, own, width)
    row_of = lambda values: values.reshape(1, -1)

    def swap(send):
        return exchange(send.reshape(subs, ROWS, send.shape[1]), "sub").reshape(send.shape)

    whole = lambda shape: pl.BlockSpec(shape, lambda step: (0,) * len(shape))
    part_of = lambda which: pl.BlockSpec((comps // 3, 1, own, width), lambda step: (step, which, 0, 0))
    vmem = lambda shape, dtype: pltpu.VMEM(shape, dtype)

    with jax.named_scope("begin"):
        field, field16, fieldr, send, own8, own8t, own_tail, own_kind, take, take_t = kernel_call(
            m["begin"],
            [
                ((own, lanes), F32),
                ((own, lanes), BF16),
                ((rhs, lanes), BF16),
                ((slots, block), BF16),
                ((slots, own), BF16),
                ((own, slots), BF16),
                ((tail * own, slots), BF16),
                ((own, LANES), F32),
                ((over, slots), BF16),
                ((slots, over), BF16),
            ],
            residual_in,
            row_of(cluster_of),
            row_of(margin_peer),
            row_of(margin_row),
        )
    with jax.named_scope("regroup"):
        coarse_inverse, send = lax.optimization_barrier((coarse_inverse, send))
        matrix = regroup(coarse_inverse, groups, subs, cl_dev, comps)
    with jax.named_scope("answer"):
        got = swap(send)
        send, give, give_t, members = kernel_call(
            m["answer"],
            [((slots, lanes + block), BF16), ((slots, own), BF16), ((own, slots), BF16), ((ROWS, block), F32)],
            got,
            field16,
            row_of(cluster_of),
        )
    with jax.named_scope("own_half_first"):
        fieldr, send = lax.optimization_barrier((fieldr, send))
        part = kernel_call(
            m["half"],
            [((rhs, width), F32)],
            fieldr,
            inverse,
            grid=(3,),
            in_specs=[whole((rhs, lanes)), part_of(0)],
            out_specs=[whole((rhs, width))],
        )[0]
    got = swap(send)

    def coarse_parts(got, offset, rows, inner):
        return exchange(
            kernel_call(
                functools.partial(m["coarse"], offset, rows), [((groups, rows, LANES), BF16)], matrix, got, *inner
            )[0],
            "group",
        )

    def finish(full, got, part):
        sent = lanes + block if full else lanes
        return kernel_call(
            functools.partial(m["finish"], full),
            [((own, lanes), F32), ((slots, sent), BF16)],
            got,
            part,
            inverse,
            take,
            take_t,
            own8,
            grid=(3,),
            in_specs=[
                whole(got.shape),
                whole((rhs, width)),
                part_of(1),
                whole((over, slots)),
                whole((slots, over)),
                whole((slots, own)),
            ],
            out_specs=[whole((own, lanes)), whole((slots, sent))],
            scratch_shapes=[
                vmem((rhs, lanes), BF16),
                vmem((rhs, width), F32),
                vmem((own, lanes), BF16),
                vmem((over, lanes), BF16),
            ],
        )

    with jax.named_scope("coarse_first"):
        parts = coarse_parts(got, lanes, each, [])
    with jax.named_scope("solve_first"):
        res_own, sent = finish(True, got, part)
    with jax.named_scope("return_first"):
        send, sol = kernel_call(
            m["join_first"], [((slots, lanes + 2 * block), BF16), ((ROWS, block), F32)], sent, parts
        )
        got = swap(send)
    with jax.named_scope("combine"):
        first, send = kernel_call(
            m["combine"],
            [((own, lanes), F32), ((slots, lanes + block), BF16)],
            got, res_own, give, give_t, own8t, own_tail, own_kind, members, sol,
        )
    with jax.named_scope("own_half_second"):
        got = swap(send)
        first_out, inner, part = kernel_call(
            m["half_first"],
            [((rhs, comps, own), F32), ((2, LANES), F32), ((rhs, width), F32)],
            first,
            field,
            inverse,
            grid=(3,),
            in_specs=[whole((own, lanes)), whole((own, lanes)), part_of(0)],
            out_specs=[whole((rhs, comps, own)), whole((2, LANES)), whole((rhs, width))],
            scratch_shapes=[vmem((rhs, lanes), BF16)],
        )
    with jax.named_scope("coarse_second"):
        parts = coarse_parts(got, lanes, each + 16, [inner])
    with jax.named_scope("solve_second"):
        res_own, sent = finish(False, got, part)
    with jax.named_scope("return_second"):
        send = kernel_call(m["join_second"], [((slots, lanes + block), BF16)], sent, parts)[0]
        got = swap(send)
    with jax.named_scope("end"):
        second = kernel_call(
            m["end"], [((rhs, comps, own), F32)], got, res_own, first, give_t, own8t, own_tail, own_kind
        )[0]
    return first_out, second


def solution(mesh):
    placed = (
        P(None, None, ("group", "sub")),
        P(("group", "sub"), None, None),
        P(("group", "sub"), None),
        P(("group", "sub")),
        P(("group", "sub"), None),
        P(("group", "sub")),
    )
    return jax.shard_map(
        body,
        mesh=mesh,
        in_specs=placed,
        out_specs=(P(None, None, ("group", "sub")), P(None, None, ("group", "sub"))),
        check_vma=False,
    )
```

time: 909 us -> 213 us (0.23)
  waiting for transfers between devices: 565 us -> 67.6 us
  blocking collectives: 210 us -> 40.9 us
  local copies, waits for them, and re-layouts: 62.3 us -> 28.1 us
  Pallas kernels: 0 us -> 27 us
  starting transfers between devices: 16.8 us -> 43.2 us
  matrix products: 22.8 us -> 2.62 us
  other arithmetic: 16.1 us -> 1.41 us
  between operations: 14.2 us -> 1.16 us
    reduce_scatter x2 -> x0, waiting for transfers between devices: 431 us -> none  [coarse_reduce(): return lax.psum_scatter(local_sums, 'sub', scatter_dimension=2, tiled=True)]
    all_gather x2 -> x0, waiting for transfers between devices: 121 us -> none  [coarse_finish(): lax.all_gather(ordered, ('group', 'sub'), axis=1, tiled=True)]
    all_gather x2 -> x0, blocking collectives: 99.7 us -> none  [coarse_finish(): return add_clusters(lax.all_gather(solution, 'sub', axis=2, tiled=True))]
    psum x1 -> x0, blocking collectives: 72.7 us -> none  [body(): inner_rf, inner_ff = lax.psum((part_rf, part_ff), ('group', 'sub'))]
    all_to_all x3 -> x6, waiting for transfers between devices: 13.4 us -> 67.6 us  [exchange(): return lax.all_to_all(values, axis, split_axis=0, concat_axis=0, tiled=True)]
    pallas_call x0 -> x12, Pallas kernels: none -> 27 us  [kernel_call(): pl.pallas_call(body, out_shape=[jax.ShapeDtypeStruct(shape, dtype) for sh...]
    all_to_all x3 -> x6, starting transfers between devices: 16.6 us -> 38.2 us  [exchange(): return lax.all_to_all(values, axis, split_axis=0, concat_axis=0, tiled=True)]
    dot_general x16 -> x2, matrix products: 22.8 us -> 2.62 us  [the longest x1 2.11 us: dot(): return jnp.dot(left, right, preferred_element_type=F32)]
  transfers between devices with their start and end apart: 7 -> 10, of which waited for: 5 -> 4; matrix products, arithmetic and copies ran while one was open for 7% -> 6% of each run, Pallas kernels for 0% -> 9%
where the time goes in v2:
time: 213 us; the launch traced here: 212 us
  waiting for transfers between devices  67.6 us (32%)
  starting transfers between devices  43.2 us (20%)
  blocking collectives  40.9 us (19%)
  local copies, waits for them, and re-layouts  28.1 us (13%)
  Pallas kernels  27 us (13%)
  matrix products  2.62 us (1%)
    all_to_all x6, waiting for transfers between devices, exchange(): return lax.all_to_all(values, axis, split_axis=0, concat_axis=0, tiled=True)  67.6 us
    all_to_all x1, blocking collectives, exchange(): return lax.all_to_all(values, axis, split_axis=0, concat_axis=0, tiled=True)  40.9 us
    all_to_all x6, starting transfers between devices, exchange(): return lax.all_to_all(values, axis, split_axis=0, concat_axis=0, tiled=True)  38.2 us
    pallas_call x12, Pallas kernels, kernel_call(): pl.pallas_call(body, out_shape=[jax.ShapeDtypeStruct(shape, dtype) for sh...  27 us
    unnamed x70, local copies, waits for them, and re-layouts  20.9 us
    ppermute x3, starting transfers between devices, regroup(): lax.ppermute(target, 'group', [(i, (i - 2 * step) % groups) for i in rang...  4.93 us
  transfers between devices with their start and end apart: 10, of which 4 were waited for; matrix products, arithmetic and copies ran while one was open for 6% of the time, Pallas kernels for 9%

profile of v2, /device:TPU:10, one launch (start us, length us, event | category | flops | bytes accessed | tf_op | source)
XLA Modules:
  0.0 212.0 jit_solution(13751771867337192591)
XLA Ops:
  2.2 2.2 %begin.1 = (f32[128,1152]{1,0:T(8,128)S(1)}, bf16[128,1152]{1,0:T(8,128)(2,1)S(1)}, bf16[128,1152]{1,0:T(8,128)(2,1)S(1)}, bf16[256,768]{1,0:T(8,128)(2,1)}, bf1...) custom-call(f32[128,9,128]{2,1,0:T(8,128)S(1)} %copy.10.res, ...), custom_call_target="tpu_custom_call" | custom-call | tf_op jit(solution)/shard_map/begin/pallas_call | solution.py:49
  6.4 2.9 %reshape.68 = bf16[45,8,1440]{2,1,0:T(8,128)(2,1)S(1)} reshape(bf16[45,11520]{1,0:T(8,128)(2,1)} %param.10) | data formatting | bytes 2073600 | tf_op jit(solution)/shard_map/regroup/reshape | solution.py:300
  10.1 2.1 fusion.2
  12.4 11.6 %all-to-all-start = ((bf16[32,8,768]{2,1,0:T(8,128)(2,1)}), bf16[32,8,768]{2,1,0:T(8,128)(2,1)S(1)}, u32[]{:S(2)}, u32[]{:S(2)}) async-start(bf16[32,8,768]{2,1,0:T(8,128)(2,1)} %bitcast.3), calls=%async_computation | async-start | bytes 786432 | tf_op jit(solution)/shard_map/answer/all_to_all | solution.py:23
  27.2 2.6 %collective-permute-start.2 = (bf16[2,48,1536]{2,1,0:T(8,128)(2,1)}, bf16[2,48,1536]{2,1,0:T(8,128)(2,1)}, u32[]{:S(2)}, u32[]{:S(2)}) collective-permute-start(bf16[2,48,1536]{2,1,0:T(8,128)(2,1)} %get-tuple-element.64), channel_id=1, source_target_pairs={{0,128},{32,160},{64,192},{96,224},{128,0},{160,32},{192,64},{224,... | collective-permute-start | bytes 884744 | tf_op jit(solution)/shard_map/regroup/ppermute | solution.py:317
  29.8 1.9 collective-permute-start.3
  31.7 7.0 %all-to-all-done = bf16[32,8,768]{2,1,0:T(8,128)(2,1)S(1)} async-done(((bf16[32,8,768]{2,1,0:T(8,128)(2,1)}), bf16[32,8,768]{2,1,0:T(8,128)(2,1)S(1)}, u32[]{:S(2)}, u32[]{:S(2)}) %all-to-all-start) | async-done | bytes 393248 | tf_op jit(solution)/shard_map/answer/all_to_all | solution.py:23
  40.7 5.6 %all-to-all-start.1 = ((bf16[32,8,1920]{2,1,0:T(8,128)(2,1)}), bf16[32,8,1920]{2,1,0:T(8,128)(2,1)S(1)}, u32[]{:S(2)}, u32[]{:S(2)}) async-start(bf16[32,8,1920]{2,1,0:T(8,128)(2,1)} %bitcast.5), calls=%async_computation.1 | async-start | bytes 1966080 | tf_op jit(solution)/shard_map/all_to_all | solution.py:23
  47.0 1.7 bitcast_dynamic-update-slice_fusion.1
  48.7 1.7 bitcast_dynamic-update-slice_fusion
  50.4 1.7 dynamic-slice_dynamic-update-slice_fusion.1
  52.9 1.7 bitcast_dynamic-update-slice_fusion.2
  55.9 16.3 %all-to-all-done.1 = bf16[32,8,1920]{2,1,0:T(8,128)(2,1)S(1)} async-done(((bf16[32,8,1920]{2,1,0:T(8,128)(2,1)}), bf16[32,8,1920]{2,1,0:T(8,128)(2,1)S(1)}, u32[]{:S(2)}, u32[]{:S(2)}) %all-to-all-start.1) | async-done | bytes 983072 | tf_op jit(solution)/shard_map/all_to_all | solution.py:23
  73.3 4.9 %all-to-all-start.2 = ((bf16[8,48,128]{2,1,0:T(8,128)(2,1)}), bf16[8,48,128]{2,1,0:T(8,128)(2,1)S(1)}, u32[]{:S(2)}, u32[]{:S(2)}) async-start(bf16[8,48,128]{2,1,0:T(8,128)(2,1)} %coarse_first.1), calls=%async_computation.2 | async-start | bytes 196608 | tf_op jit(solution)/shard_map/coarse_first/all_to_all | solution.py:23
  78.2 4.1 %own_half_first.1.part = f32[128,2304]{1,0:T(8,128)S(1)} custom-call(bf16[128,1152]{1,0:T(8,128)(2,1)S(1)} %get-tuple-element.37.fieldr, bf16[9,2,128,2304]{3,2,1,0:T(8,128)(2,1)} %bitcast.54), custom_call_target="tpu_custom_call" | custom-call | tf_op jit(solution)/shard_map/own_half_first/pallas_call | solution.py:49
  82.4 5.2 %solve_first.1 = (f32[128,1152]{1,0:T(8,128)S(1)}, bf16[256,1920]{1,0:T(8,128)(2,1)S(1)}) custom-call(bf16[256,1920]{1,0:T(8,128)(2,1)S(1)} %bitcast.42, f32[128,2304]{1,0:T(8,128)S(1)} %own_half_first.1.part, bf16[9,2,128,2304]{3,2,1,0:T(8,128)(2,1)} %bitcast.55, bf16[128,256]{1,0:T(8,128)(2,1)S(1)} %copy-done.12, bf16[256,128]{1,0:T(8,128)(2,1)S(1)} %copy-done.15, ...), custom_call_target="tpu_custom_call" | custom-call | tf_op jit(solution)/shard_map/solve_first/pallas_call | solution.py:49
  88.6 40.9 %all_to_all.35 = bf16[32,8,2688]{2,1,0:T(8,128)(2,1)S(1)} all-to-all(bf16[32,8,2688]{2,1,0:T(8,128)(2,1)S(1)} %bitcast.48), channel_id=1, replica_groups=mesh['group'=8,'sub'=32] {'sub'}, dimensions={0} | all-to-all | bytes 2752512 | tf_op jit(solution)/shard_map/return_first/all_to_all | solution.py:23
  131.2 5.6 %all-to-all-start.4 = ((bf16[32,8,1920]{2,1,0:T(8,128)(2,1)}), bf16[32,8,1920]{2,1,0:T(8,128)(2,1)S(1)}, u32[]{:S(2)}, u32[]{:S(2)}) async-start(bf16[32,8,1920]{2,1,0:T(8,128)(2,1)} %bitcast.49), calls=%async_computation.4 | async-start | bytes 1966080 | tf_op jit(solution)/shard_map/own_half_second/all_to_all | solution.py:23
  137.8 4.5 %own_half_second.1 = (f32[128,9,128]{2,1,0:T(8,128)S(1)}, f32[2,128]{1,0:T(2,128)S(1)}, f32[128,2304]{1,0:T(8,128)S(1)}) custom-call(f32[128,1152]{1,0:T(8,128)S(1)} %get-tuple-element.52.values.first, f32[128,1152]{1,0:T(8,128)S(1)} %copy-done.6, bf16[9,2,128,2304]{3,2,1,0:T(8,128)(2,1)} %bitcast.56), custom_call_target="tpu_custom_call" | custom-call | tf_op jit(solution)/shard_map/own_half_second/pallas_call | solution.py:49
  144.4 18.3 %all-to-all-done.4 = bf16[32,8,1920]{2,1,0:T(8,128)(2,1)S(1)} async-done(((bf16[32,8,1920]{2,1,0:T(8,128)(2,1)}), bf16[32,8,1920]{2,1,0:T(8,128)(2,1)S(1)}, u32[]{:S(2)}, u32[]{:S(2)}) %all-to-all-start.4) | async-done | bytes 983072 | tf_op jit(solution)/shard_map/own_half_second/all_to_all | solution.py:23
  163.8 4.8 %all-to-all-start.5 = ((bf16[8,64,128]{2,1,0:T(8,128)(2,1)}), bf16[8,64,128]{2,1,0:T(8,128)(2,1)S(1)}, u32[]{:S(2)}, u32[]{:S(2)}) async-start(bf16[8,64,128]{2,1,0:T(8,128)(2,1)} %coarse_second.1), calls=%async_computation.5 | async-start | bytes 262144 | tf_op jit(solution)/shard_map/coarse_second/all_to_all | solution.py:23
  169.9 4.7 %solve_second.1 = (f32[128,1152]{1,0:T(8,128)S(1)}, bf16[256,1152]{1,0:T(8,128)(2,1)S(1)}) custom-call(bf16[256,1920]{1,0:T(8,128)(2,1)S(1)} %bitcast.44, f32[128,2304]{1,0:T(8,128)S(1)} %copy-done.1, bf16[9,2,128,2304]{3,2,1,0:T(8,128)(2,1)} %bitcast.57, bf16[128,256]{1,0:T(8,128)(2,1)S(1)} %copy-done.13, bf16[256,128]{1,0:T(8,128)(2,1)S(1)} %copy-done.16, ...), custom_call_target="tpu_custom_call" | custom-call | tf_op jit(solution)/shard_map/solve_second/pallas_call | solution.py:49
  176.5 5.7 %all-to-all-start.6 = ((bf16[32,8,1920]{2,1,0:T(8,128)(2,1)}), bf16[32,8,1920]{2,1,0:T(8,128)(2,1)S(1)}, u32[]{:S(2)}, u32[]{:S(2)}) async-start(bf16[32,8,1920]{2,1,0:T(8,128)(2,1)} %bitcast.25), calls=%async_computation.6 | async-start | bytes 1966080 | tf_op jit(solution)/shard_map/return_second/all_to_all | solution.py:23
  183.2 26.0 %all-to-all-done.6 = bf16[32,8,1920]{2,1,0:T(8,128)(2,1)S(1)} async-done(((bf16[32,8,1920]{2,1,0:T(8,128)(2,1)}), bf16[32,8,1920]{2,1,0:T(8,128)(2,1)S(1)}, u32[]{:S(2)}, u32[]{:S(2)}) %all-to-all-start.6) | async-done | bytes 983072 | tf_op jit(solution)/shard_map/return_second/all_to_all | solution.py:23
  (87 shorter events, 27.0 us)
Async XLA Ops:
  2.1 7.3 %copy-start.29 = (pred[48,45,1]{1,0,2:T(8,128)(4,1)S(1)}, pred[48,45,1]{1,0,2:T(8,128)(4,1)}, u32[]{:S(2)}) copy-start(pred[48,45,1]{1,0,2:T(8,128)(4,1)} %constant.91) | copy-start | bytes 6484
  6.4 3.5 %copy-start.19 = (f32[128,128]{1,0:T(8,128)}, f32[128,128]{1,0:T(8,128)S(1)}, u32[]{:S(2)}) copy-start(f32[128,128]{1,0:T(8,128)S(1)} %get-tuple-element.49.own_kind) | copy-start | bytes 196612
  12.3 11.8 %collective-permute-start = (bf16[4,48,1536]{2,1,0:T(8,128)(2,1)S(1)}, bf16[4,48,1536]{2,1,0:T(8,128)(2,1)}, u32[]{:S(2)}, u32[]{:S(2)}) collective-permute-start(bf16[4,48,1536]{2,1,0:T(8,128)(2,1)S(1)} %get-tuple-element.67), channel_id=1, source_target_pairs={{0,32},{32,0},{64,96},{96,64},{128,160},{160,128},{192,224},{224,1... | collective-permute-start | bytes 1769480 | tf_op jit(solution)/shard_map/regroup/ppermute | solution.py:312
  12.4 26.3 %all-to-all-start = ((bf16[32,8,768]{2,1,0:T(8,128)(2,1)}), bf16[32,8,768]{2,1,0:T(8,128)(2,1)S(1)}, u32[]{:S(2)}, u32[]{:S(2)}) async-start(bf16[32,8,768]{2,1,0:T(8,128)(2,1)} %bitcast.3), calls=%async_computation | async-start | bytes 786432 | tf_op jit(solution)/shard_map/answer/all_to_all | solution.py:23
  25.5 14.5 %copy-start.28 = (bf16[4,2,48,1536]{3,2,1,0:T(8,128)(2,1)}, bf16[4,2,48,1536]{3,2,1,0:T(8,128)(2,1)S(1)}, u32[]{:S(2)}) copy-start(bf16[4,2,48,1536]{3,2,1,0:T(8,128)(2,1)S(1)} %maximum_select_fusion) | copy-start | bytes 3538948
  26.7 19.5 %collective-permute-start.1 = (bf16[2,48,1536]{2,1,0:T(8,128)(2,1)}, bf16[2,48,1536]{2,1,0:T(8,128)(2,1)S(1)}, u32[]{:S(2)}, u32[]{:S(2)}) collective-permute-start(bf16[2,48,1536]{2,1,0:T(8,128)(2,1)} %get-tuple-element.65), channel_id=1, source_target_pairs={{0,192},{32,224},{64,0},{96,32},{128,64},{160,96},{192,128},{224,1... | collective-permute-start | bytes 884744 | tf_op jit(solution)/shard_map/regroup/ppermute | solution.py:317
  27.2 19.8 %collective-permute-start.2 = (bf16[2,48,1536]{2,1,0:T(8,128)(2,1)}, bf16[2,48,1536]{2,1,0:T(8,128)(2,1)}, u32[]{:S(2)}, u32[]{:S(2)}) collective-permute-start(bf16[2,48,1536]{2,1,0:T(8,128)(2,1)} %get-tuple-element.64), channel_id=1, source_target_pairs={{0,128},{32,160},{64,192},{96,224},{128,0},{160,32},{192,64},{224,... | collective-permute-start | bytes 884744 | tf_op jit(solution)/shard_map/regroup/ppermute | solution.py:317
  29.8 18.9 %collective-permute-start.3 = (bf16[2,48,1536]{2,1,0:T(8,128)(2,1)}, bf16[2,48,1536]{2,1,0:T(8,128)(2,1)}, u32[]{:S(2)}, u32[]{:S(2)}) collective-permute-start(bf16[2,48,1536]{2,1,0:T(8,128)(2,1)} %get-tuple-element.62), channel_id=1, source_target_pairs={{0,64},{32,96},{64,128},{96,160},{128,192},{160,224},{192,0},{224,... | collective-permute-start | bytes 884744 | tf_op jit(solution)/shard_map/regroup/ppermute | solution.py:317
  40.7 8.0 %copy-start.23 = (bf16[256,128]{1,0:T(8,128)(2,1)}, bf16[256,128]{1,0:T(8,128)(2,1)S(1)}, u32[]{:S(2)}) copy-start(bf16[256,128]{1,0:T(8,128)(2,1)S(1)} %get-tuple-element.45.give) | copy-start | bytes 196612
  40.7 31.5 %all-to-all-start.1 = ((bf16[32,8,1920]{2,1,0:T(8,128)(2,1)}), bf16[32,8,1920]{2,1,0:T(8,128)(2,1)S(1)}, u32[]{:S(2)}, u32[]{:S(2)}) async-start(bf16[32,8,1920]{2,1,0:T(8,128)(2,1)} %bitcast.5), calls=%async_computation.1 | async-start | bytes 1966080 | tf_op jit(solution)/shard_map/all_to_all | solution.py:23
  73.3 15.1 %all-to-all-start.2 = ((bf16[8,48,128]{2,1,0:T(8,128)(2,1)}), bf16[8,48,128]{2,1,0:T(8,128)(2,1)S(1)}, u32[]{:S(2)}, u32[]{:S(2)}) async-start(bf16[8,48,128]{2,1,0:T(8,128)(2,1)} %coarse_first.1), calls=%async_computation.2 | async-start | bytes 196608 | tf_op jit(solution)/shard_map/coarse_first/all_to_all | solution.py:23
  78.2 4.2 %copy-start.12 = (bf16[128,256]{1,0:T(8,128)(2,1)S(1)}, bf16[128,256]{1,0:T(8,128)(2,1)}, u32[]{:S(2)}) copy-start(bf16[128,256]{1,0:T(8,128)(2,1)} %copy-done.11) | copy-start | bytes 196612
  78.2 4.2 %copy-start.15 = (bf16[256,128]{1,0:T(8,128)(2,1)S(1)}, bf16[256,128]{1,0:T(8,128)(2,1)}, u32[]{:S(2)}) copy-start(bf16[256,128]{1,0:T(8,128)(2,1)} %copy-done.14) | copy-start | bytes 196612
  88.6 41.0 %copy-start.10 = (f32[128,1152]{1,0:T(8,128)S(1)}, f32[128,1152]{1,0:T(8,128)}, u32[]{:S(2)}) copy-start(f32[128,1152]{1,0:T(8,128)} %copy-done.9) | copy-start | bytes 1769476
  88.6 40.9 %copy-start.18 = (bf16[128,256]{1,0:T(8,128)(2,1)S(1)}, bf16[128,256]{1,0:T(8,128)(2,1)}, u32[]{:S(2)}) copy-start(bf16[128,256]{1,0:T(8,128)(2,1)} %copy-done.17) | copy-start | bytes 196612
  88.6 40.9 %copy-start.20 = (f32[128,128]{1,0:T(8,128)S(1)}, f32[128,128]{1,0:T(8,128)}, u32[]{:S(2)}) copy-start(f32[128,128]{1,0:T(8,128)} %copy-done.19) | copy-start | bytes 196612
  88.6 40.9 %copy-start.22 = (bf16[128,256]{1,0:T(8,128)(2,1)S(1)}, bf16[128,256]{1,0:T(8,128)(2,1)}, u32[]{:S(2)}) copy-start(bf16[128,256]{1,0:T(8,128)(2,1)} %copy-done.21) | copy-start | bytes 196612
  88.6 40.9 %copy-start.24 = (bf16[256,128]{1,0:T(8,128)(2,1)S(1)}, bf16[256,128]{1,0:T(8,128)(2,1)}, u32[]{:S(2)}) copy-start(bf16[256,128]{1,0:T(8,128)(2,1)} %copy-done.23) | copy-start | bytes 196612
  131.2 31.5 %all-to-all-start.4 = ((bf16[32,8,1920]{2,1,0:T(8,128)(2,1)}), bf16[32,8,1920]{2,1,0:T(8,128)(2,1)S(1)}, u32[]{:S(2)}, u32[]{:S(2)}) async-start(bf16[32,8,1920]{2,1,0:T(8,128)(2,1)} %bitcast.49), calls=%async_computation.4 | async-start | bytes 1966080 | tf_op jit(solution)/shard_map/own_half_second/all_to_all | solution.py:23
  144.4 24.2 %copy-start.13 = (bf16[128,256]{1,0:T(8,128)(2,1)S(1)}, bf16[128,256]{1,0:T(8,128)(2,1)}, u32[]{:S(2)}) copy-start(bf16[128,256]{1,0:T(8,128)(2,1)} %copy-done.11) | copy-start | bytes 196612
  144.4 24.2 %copy-start.16 = (bf16[256,128]{1,0:T(8,128)(2,1)S(1)}, bf16[256,128]{1,0:T(8,128)(2,1)}, u32[]{:S(2)}) copy-start(bf16[256,128]{1,0:T(8,128)(2,1)} %copy-done.14) | copy-start | bytes 196612
  163.8 11.6 %all-to-all-start.5 = ((bf16[8,64,128]{2,1,0:T(8,128)(2,1)}), bf16[8,64,128]{2,1,0:T(8,128)(2,1)S(1)}, u32[]{:S(2)}, u32[]{:S(2)}) async-start(bf16[8,64,128]{2,1,0:T(8,128)(2,1)} %coarse_second.1), calls=%async_computation.5 | async-start | bytes 262144 | tf_op jit(solution)/shard_map/coarse_second/all_to_all | solution.py:23
  176.5 5.7 %copy-start.3 = (f32[128,9,128]{2,1,0:T(8,128)S(1)}, f32[128,9,128]{2,1,0:T(8,128)}, u32[]{:S(2)}) copy-start(f32[128,9,128]{2,1,0:T(8,128)} %copy-done.2) | copy-start | bytes 1769476
  176.5 32.7 %all-to-all-start.6 = ((bf16[32,8,1920]{2,1,0:T(8,128)(2,1)}), bf16[32,8,1920]{2,1,0:T(8,128)(2,1)S(1)}, u32[]{:S(2)}, u32[]{:S(2)}) async-start(bf16[32,8,1920]{2,1,0:T(8,128)(2,1)} %bitcast.25), calls=%async_computation.6 | async-start | bytes 1966080 | tf_op jit(solution)/shard_map/return_second/all_to_all | solution.py:23
  (17 other events, 19.4 us)

commit v3 on v2

v3 whole, which is shorter than its diff:
```python
import functools

import jax
import jax.numpy as jnp
import numpy as np
from jax import lax
from jax.experimental import pallas as pl
from jax.experimental.pallas import tpu as pltpu
from jax.sharding import PartitionSpec as P

EPSILON = 1e-06
F32 = jnp.float32
BF16 = jnp.bfloat16
LANES = 128
ROWS = 8
RING = 4


def dot(left, right):
    return jnp.dot(left, right, preferred_element_type=F32)


def exchange(values, axis):
    return lax.all_to_all(values, axis, split_axis=0, concat_axis=0, tiled=True)


def tile(values, index):
    return values[:, index * LANES : (index + 1) * LANES]


def iota(shape, axis):
    return lax.broadcasted_iota(jnp.int32, shape, axis)


def over_rows(values, subs):
    cube = values.reshape(subs, ROWS, LANES)
    return jnp.broadcast_to(jnp.sum(cube, axis=1, keepdims=True), cube.shape).reshape(subs * ROWS, LANES)


def one_row(values, row, subs):
    cube = values.reshape(subs, ROWS, LANES)
    return jnp.broadcast_to(cube[:, row : row + 1, :], cube.shape).reshape(subs * ROWS, LANES)


def repeat_rows(values, subs):
    return jnp.broadcast_to(values[None], (subs,) + values.shape).reshape(subs * ROWS, values.shape[1])


def kernel_call(body, outs, *args, flops=0, moved=0, limit=48, after=(), in_specs=None, **kw):
    count = len(after)
    specs = in_specs or [pl.BlockSpec(memory_space=pltpu.VMEM)] * len(args)
    return pl.pallas_call(
        lambda *refs: body(*refs[count:]),
        out_shape=[jax.ShapeDtypeStruct(shape, dtype) for shape, dtype in outs],
        in_specs=[pl.BlockSpec(memory_space=pl.ANY)] * count + list(specs),
        compiler_params=pltpu.CompilerParams(vmem_limit_bytes=limit * 1024 * 1024),
        cost_estimate=pl.CostEstimate(flops=flops, bytes_accessed=moved, transcendentals=0),
        **kw,
    )(*after, *args)


def make(rhs, comps, own, over, subs, groups, cl_dev):
    tail = ROWS - cl_dev
    main = comps - tail
    slots = subs * ROWS
    lanes = comps * LANES
    block = main * LANES
    share = -(-main // RING) * LANES
    aux = main - 1
    at_take, at_own, at_tail = 0, over, over + own
    at_kind = at_tail + tail * own
    at_rows = at_kind + own
    map_rows = at_rows + slots

    def pack(sums, extra, ref, offset):
        inner = iota((slots, LANES), 0) % ROWS
        for t in range(main):
            value = tile(sums, t)
            if t < cl_dev:
                for j in range(tail):
                    value = jnp.where(inner == cl_dev + j, one_row(tile(sums, main + j), t, subs), value)
            elif extra is not None:
                value = jnp.where(inner == cl_dev, extra, value)
            ref[:, offset + t * LANES : offset + (t + 1) * LANES] = value.astype(BF16)

    def prolong(tiles, own8t, own_tail, own_kind):
        head = dot(own8t, tiles)
        picked = dot(own_tail, tiles[:, : cl_dev * LANES])
        parts = [head]
        for j in range(tail):
            rows = picked[j * own : (j + 1) * own]
            value = jnp.zeros((own, LANES), F32)
            for t in range(cl_dev):
                value = jnp.where(own_kind == t, tile(rows, t), value)
            parts.append(value)
        return jnp.concatenate(parts, axis=1)

    def places(cl, peer):
        number = cl[...]
        holder = ((number.astype(F32) + 0.5) * (1.0 / cl_dev)).astype(jnp.int32)
        kind = number - holder * cl_dev
        rows = iota((slots, own), 0)
        hot = (rows == holder * ROWS + kind).astype(F32)
        peers = jnp.broadcast_to(peer[...].astype(F32), (over, over))
        same = (peers == peers.T) & (iota((over, over), 0) < iota((over, over), 1))
        rank = jnp.sum(same.astype(F32), axis=0, keepdims=True).astype(jnp.int32)
        dest = peer[...] * ROWS + rank
        hot_dest = (iota((slots, over), 0) == dest).astype(F32)
        return rows, holder, kind, hot, hot_dest

    def begin(res_hbm, cl_hbm, peer_hbm, row_hbm, send, token, res, cl, peer, row, field16, sems):
        token[...] = jnp.zeros((ROWS, LANES), F32)
        pairs = [(peer_hbm, peer), (row_hbm, row), (cl_hbm, cl), (res_hbm, res)]
        copies = [pltpu.make_async_copy(src, dst, sems.at[i]) for i, (src, dst) in enumerate(pairs)]
        for copy in copies:
            copy.start()
        for copy in copies[:3]:
            copy.wait()
        rows, holder, kind, hot, hot_dest = places(cl, peer)
        inner = rows % ROWS
        lane = iota((slots, LANES), 1)
        wanted = jnp.sum(hot_dest * (row[...] + 1).astype(F32), axis=1, keepdims=True)
        counts = jnp.sum(hot, axis=1, keepdims=True)
        extra = jnp.where(lane == inner, wanted, 0.0) + jnp.where(lane == inner + ROWS, counts, 0.0)
        copies[3].wait()
        for k in range(comps):
            field16[:, k * LANES : (k + 1) * LANES] = res[k].T.astype(BF16)
        pack(dot(hot.astype(BF16), field16[...]), over_rows(extra, subs), send, 0)

    def keep_maps(res, cl, peer, field16, maps):
        for k in range(comps):
            field16[:, k * LANES : (k + 1) * LANES] = res[k].T.astype(BF16)
        rows, holder, kind, hot, hot_dest = places(cl, peer)
        maps[at_take : at_take + over, :] = hot_dest.T.astype(BF16)
        cluster_maps(holder, kind, maps, at_own)
        maps[at_rows : at_rows + slots, :over] = hot_dest.astype(BF16)
        maps[at_rows : at_rows + slots, over : over + own] = hot.astype(BF16)

    def asking(got):
        lane = iota((slots, LANES), 1)
        inner = iota((slots, LANES), 0) % ROWS
        asked = one_row(tile(got, aux).astype(F32), cl_dev, subs)
        asked = jnp.sum(jnp.where(lane == inner, asked, 0.0), axis=1, keepdims=True) - 1.0
        hot = (iota((slots, own), 1).astype(F32) == asked).astype(F32)
        return lane, inner, hot

    def answer(got, field16, cl, send, token):
        token[...] = jnp.zeros((ROWS, LANES), F32)
        total = jnp.sum(got[...].astype(F32).reshape(subs, ROWS, block), axis=0)
        lane, inner, hot = asking(got)
        send[:, :lanes] = dot(hot.astype(BF16), field16[...]).astype(BF16)
        ids = jnp.sum(hot * cl[...].astype(F32), axis=1, keepdims=True)
        ids = over_rows(jnp.where(lane == inner, ids, 0.0), subs)
        for t in range(main):
            value = repeat_rows(tile(total, t), subs)
            if t >= cl_dev:
                value = jnp.where(inner == cl_dev, ids, value)
            send[:, lanes + t * LANES : lanes + (t + 1) * LANES] = value.astype(BF16)

    def keep_answer(got, gives, gives_late, members):
        lane, inner, hot = asking(got)
        gives_late[...] = hot.T.astype(BF16)
        gives[:own, :] = hot.T.astype(BF16)
        gives[own:, :own] = hot.astype(BF16)
        gives[own:, own:] = jnp.zeros((slots, slots - own), BF16)
        total = jnp.sum(tile(got, aux).astype(F32).reshape(subs, ROWS, LANES), axis=0)
        small = iota((ROWS, LANES), 0)
        small_lane = iota((ROWS, LANES), 1)
        numbers = [
            jnp.sum(jnp.where((small_lane == ROWS + c) & (small == cl_dev), total, 0.0), axis=(0, 1), keepdims=True)
            for c in range(cl_dev)
        ]
        base = jnp.zeros((ROWS, LANES), F32)
        for c in range(cl_dev):
            base = jnp.where(small == c, numbers[c], base)
        for t in range(main):
            count = jnp.where(small < cl_dev, base, numbers[t]) if t < cl_dev else base
            members[:, t * LANES : (t + 1) * LANES] = count

    def gather(place, *refs):
        pieces, outs = refs[:-2], refs[-2:]
        turns = len(pieces)
        sides = pieces[0].shape[0]
        for step, piece in enumerate(pieces):
            turn = place[0, 1] + step
            turn = jnp.where(turn >= turns, turn - turns, turn)
            for side in range(sides):
                core = place[0, 0] if side == 0 else 1 - place[0, 0]
                for out in outs:
                    out[sides * turn + core] = piece[side]

    def coarse(offset, rows, matrix, got, *refs):
        out = refs[-1]
        each = main * ROWS
        total = jnp.zeros((groups * each, LANES), F32)
        for t in range(main):
            columns = matrix[:, :, t * slots : (t + 1) * slots].reshape(groups * each, slots)
            total += dot(columns, got[:, offset + t * LANES : offset + (t + 1) * LANES])
        for g in range(groups):
            out[g, :each, :] = total[g * each : (g + 1) * each].astype(BF16)
        if rows > each:
            inner = refs[0][...]
            high = inner.astype(BF16).astype(F32)
            last = jnp.concatenate([high, inner - high, jnp.zeros((rows - each - 4, LANES), F32)], axis=0)
            for g in range(groups):
                out[g, each:, :] = last.astype(BF16)

    def group_total(got):
        total = jnp.sum(got[...].astype(F32), axis=0)
        return total, [total[t * ROWS : (t + 1) * ROWS] for t in range(main)]

    def loads(inverse, which, buffer, sems):
        copies = [pltpu.make_async_copy(inverse.at[k, which], buffer.at[k], sems.at[k]) for k in range(comps)]
        for copy in copies:
            copy.start()
        return copies

    def product(copies, turned, buffer, part, out):
        third = comps // 3
        for step in range(3):
            for copy in copies[step * third : (step + 1) * third]:
                copy.wait()
            rows = buffer[step * third : (step + 1) * third].reshape(third * own, out.shape[1])
            value = dot(turned[:, step * third * LANES : (step + 1) * third * LANES], rows)
            if step:
                out[...] += value
            elif part is None:
                out[...] = value
            else:
                out[...] = part[...] + value

    def half(res, inverse, out, token, turned, buffer, sems):
        token[...] = jnp.zeros((ROWS, LANES), F32)
        copies = loads(inverse, 0, buffer, sems)
        for k in range(comps):
            turned[:, k * LANES : (k + 1) * LANES] = res[k].astype(BF16)
        product(copies, turned, buffer, None, out)

    def half_first(place, spread, maps, over_maps, res, inverse, *refs):
        pieces, refs = refs[:RING], refs[RING:]
        first_out, inner, out, over_add, turned, buffer, sems, tiles = refs
        copies = loads(inverse, 0, buffer, sems)
        for step, piece in enumerate(pieces):
            member = place[0, 2] + step
            member = jnp.where(member >= RING, member - RING, member)

            @pl.when(member * share < block)
            def _(piece=piece, member=member):
                tiles[:, pl.ds(pl.multiple_of(member * share, LANES), share)] = piece[...]

        everything = tiles[...]
        values = spread[...] + prolong_maps(everything, maps, at_own)
        over_add[...] = prolong_maps(everything, over_maps, 0)
        rf = jnp.zeros((rhs, own), F32)
        ff = jnp.zeros((rhs, own), F32)
        for k in range(comps):
            flipped = tile(values, k).T
            first_out[k] = flipped
            turned[:, k * LANES : (k + 1) * LANES] = flipped.astype(BF16)
            rf += res[k] * flipped
            ff += flipped * flipped
        inner[0:1, :] = jnp.sum(rf.T, axis=0, keepdims=True)
        inner[1:2, :] = jnp.sum(ff.T, axis=0, keepdims=True)
        product(copies, turned, buffer, None, out)

    def solve(got, part, maps, inverse, *refs):
        extra, (out, turned, buffer, sems) = refs[:-4], refs[-4:]
        copies = loads(inverse, 1, buffer, sems)
        arrived = dot(maps[at_take : at_take + over, :], got[:, :lanes])
        for each_extra in extra:
            arrived += each_extra[...]
        for k in range(comps):
            turned[:, k * LANES : (k + 1) * LANES] = tile(arrived, k).T.astype(BF16)
        product(copies, turned, buffer, part, out)

    def finish_first(got, total, parts, maps, send, res_own, over_maps, sol, token, own16, over16):
        token[...] = jnp.zeros((ROWS, LANES), F32)
        cams = own + over
        for k in range(comps):
            flipped = total[:, k * cams : (k + 1) * cams].T
            res_own[:, k * LANES : (k + 1) * LANES] = flipped[:own]
            flipped = flipped.astype(BF16)
            own16[:, k * LANES : (k + 1) * LANES] = flipped[:own]
            over16[:, k * LANES : (k + 1) * LANES] = flipped[own:]
        rows = maps[at_rows : at_rows + slots, :]
        take_t, own8 = rows[:, :over], rows[:, over : over + own]
        send[:, :lanes] = dot(take_t, over16[...]).astype(BF16)
        holder, kind = margin_places(got, take_t)
        cluster_maps(holder, kind, over_maps, 0)
        over8 = (iota((slots, over), 0) == holder * ROWS + kind).astype(F32).astype(BF16)
        pack(dot(own8, own16[...]) + dot(over8, over16[...]), None, send, lanes)
        _, tiles = group_total(parts)
        each_share = share // LANES
        for t in range(main):
            sol[:, t * LANES : (t + 1) * LANES] = tiles[t]
        member = iota((slots, LANES), 0) // ROWS % RING
        for j in range(each_share):
            value = jnp.zeros((slots, LANES), F32)
            for q in range(RING):
                if q * each_share + j < main:
                    value = jnp.where(member == q, repeat_rows(tiles[q * each_share + j], subs), value)
            at = lanes + block + j * LANES
            send[:, at : at + LANES] = value.astype(BF16)

    def margin_places(got, take_t):
        lane = iota((slots, LANES), 1)
        inner = iota((slots, LANES), 0) % ROWS
        ids = one_row(got[:, lanes + aux * LANES : lanes + (aux + 1) * LANES].astype(F32), cl_dev, subs)
        ids = jnp.sum(jnp.where(lane == inner, ids, 0.0), axis=1, keepdims=True)
        number = jnp.sum(take_t.astype(F32) * ids, axis=0, keepdims=True)
        holder = ((number + 0.5) * (1.0 / cl_dev)).astype(jnp.int32)
        return holder, number.astype(jnp.int32) - holder * cl_dev

    def cluster_maps(holder, kind, maps, base):
        rows = iota((slots, own), 0)
        hot = (rows == holder * ROWS + kind).astype(F32)
        maps[base : base + own, :] = hot.T.astype(BF16)
        for j in range(tail):
            hot_j = (rows == holder * ROWS + (cl_dev + j)).astype(F32)
            maps[base + (1 + j) * own : base + (2 + j) * own, :] = hot_j.T.astype(BF16)
        at = base + (1 + tail) * own
        maps[at : at + own, :] = jnp.broadcast_to(kind.astype(F32), (slots, own)).T.astype(BF16)

    def finish_second(total, parts, maps, send, res_own, over16):
        cams = own + over
        for k in range(comps):
            flipped = total[:, k * cams : (k + 1) * cams].T
            res_own[:, k * LANES : (k + 1) * LANES] = flipped[:own]
            over16[:, k * LANES : (k + 1) * LANES] = flipped[own:].astype(BF16)
        send[:, :lanes] = dot(maps[at_rows : at_rows + slots, :over], over16[...]).astype(BF16)
        summed, tiles = group_total(parts)
        each = main * ROWS
        inner = summed[each : each + 2] + summed[each + 2 : each + 4]
        small = iota((ROWS, LANES), 0)
        for t in range(main):
            value = tiles[t]
            if t == aux:
                value = jnp.where(small == cl_dev, inner[0:1], value)
                value = jnp.where(small == cl_dev + 1, inner[1:2], value)
            send[:, lanes + t * LANES : lanes + (t + 1) * LANES] = repeat_rows(value, subs).astype(BF16)

    def prolong_maps(tiles, maps, base):
        kind = maps[base + (1 + tail) * own : base + (2 + tail) * own, :LANES].astype(F32)
        return prolong(tiles, maps[base : base + own, :], maps[base + own : base + (1 + tail) * own, :], kind)

    def combine(got, res_own, gives, members, sol, send, third, spread, token):
        token[...] = jnp.zeros((ROWS, LANES), F32)
        values = res_own[...] + dot(gives[:own, :], got[:, :lanes])
        spread[...] = values
        send[:, :lanes] = dot(gives[own:, :own], values.astype(BF16)).astype(BF16)
        total = jnp.sum(got[:, lanes : lanes + block].astype(F32).reshape(subs, ROWS, block), axis=0)
        for t in range(main):
            columns = slice(t * LANES, (t + 1) * LANES)
            value = tile(total, t) + members[:, columns] * sol[:, columns]
            send[:, lanes + t * LANES : lanes + (t + 1) * LANES] = repeat_rows(value, subs).astype(BF16)
        third[...] = got[:, lanes + block :]

    def end(got, res_own, first, gives, maps, out):
        applied = res_own[...] + dot(gives[...], got[:, :lanes])
        applied += prolong_maps(got[:, lanes:], maps, at_own)
        sums = got[:, lanes + aux * LANES :].astype(F32).reshape(subs, ROWS, LANES)
        sums = jnp.sum(sums, axis=0)
        scale = sums[cl_dev : cl_dev + 1] / (sums[cl_dev + 1 : cl_dev + 2] + EPSILON)
        for k in range(comps):
            out[k] = first[k] - (scale * tile(applied, k)).T

    return dict(locals())


def block_order(cl_dev, comps, count):
    tail = ROWS - cl_dev
    main = comps - tail
    order = np.full((main, count, ROWS), -1, np.int32)
    for t in range(main):
        for i in range(ROWS):
            if i < cl_dev:
                order[t, :, i] = np.arange(count) * cl_dev * comps + i * comps + t
            elif t < cl_dev:
                order[t, :, i] = np.arange(count) * cl_dev * comps + t * comps + main + i - cl_dev
    return order.reshape(-1)


def regroup(coarse_inverse, groups, subs, cl_dev, comps):
    cl_rows = cl_dev * comps
    grp_rows = cl_rows * subs
    row_order = block_order(cl_dev, comps, 1)
    col_order = block_order(cl_dev, comps, subs)
    pick_rows = jnp.asarray(row_order[:, None] == np.arange(cl_rows)[None, :]).astype(BF16)
    pick_cols = (jnp.asarray(col_order)[None, :] == jnp.arange(grp_rows, dtype=jnp.int32)[:, None]).astype(BF16)
    values = coarse_inverse.reshape(cl_rows, groups, grp_rows)
    values = lax.dot_general(pick_rows, values, (((1,), (0,)), ((), ())), preferred_element_type=F32).astype(BF16)
    values = values.transpose(1, 0, 2).reshape(groups * row_order.size, grp_rows)
    return dot(values, pick_cols).astype(BF16).reshape(groups, row_order.size, col_order.size)


def place_of():
    index = lax.axis_index("group")
    return index % 2, index // 2


def pass_round(values, after):
    groups = values.shape[0]
    if groups == 1:
        return [values]
    turns = groups // 2
    core, turn = place_of()
    pairs = values.reshape((turns, 2) + values.shape[1:])
    kept = lax.dynamic_index_in_dim(pairs, core, 1, keepdims=False)
    given = lax.dynamic_index_in_dim(pairs, 1 - core, 1, keepdims=False)
    given, after = lax.optimization_barrier((given, after))
    other = lax.ppermute(given, "group", [(i, i ^ 1) for i in range(groups)])
    pieces = []
    for step in range(turns):
        target = (turn - step) % turns
        piece = jnp.stack([lax.dynamic_index_in_dim(part, target, 0, keepdims=False) for part in (kept, other)])
        if step:
            piece = lax.ppermute(piece, "group", [(i, (i - 2 * step) % groups) for i in range(groups)])
        pieces.append(piece)
    return pieces


def body(residual_in, local_inverse, coarse_inverse, cluster_of, margin_peer, margin_row):
    rhs, comps, own = residual_in.shape
    over = margin_row.shape[0]
    subs = lax.axis_size("sub")
    groups = lax.axis_size("group")
    cl_dev = coarse_inverse.shape[0] // comps
    width = local_inverse.shape[1]
    m = make(rhs, comps, own, over, subs, groups, cl_dev)
    slots, lanes, block, main, tail = m["slots"], m["lanes"], m["block"], m["main"], m["tail"]
    share = m["share"]
    each = main * ROWS
    inverse = local_inverse.reshape(comps, 2, own, width)
    residual = residual_in.transpose(1, 0, 2)
    cluster, peer, row = [values.reshape(1, -1) for values in (cluster_of, margin_peer, margin_row)]
    hbm = pl.BlockSpec(memory_space=pltpu.HBM)
    here = pl.BlockSpec(memory_space=pltpu.VMEM)
    vmem = pltpu.VMEM
    half_cost = dict(flops=rhs * width * width, moved=width * width)
    mark = ((ROWS, LANES), F32)
    half_scratch = [
        vmem((rhs, lanes), BF16),
        vmem((comps, own, width), BF16),
        pltpu.SemaphoreType.DMA((comps,)),
    ]

    def swap(send):
        return exchange(send.reshape(subs, ROWS, send.shape[1]), "sub").reshape(send.shape)

    def coarse_parts(matrix, got, rows, inner, after=()):
        parts = kernel_call(
            functools.partial(m["coarse"], lanes, rows),
            [((groups, rows, LANES), BF16)],
            matrix,
            got,
            *inner,
            after=after,
        )[0]
        return exchange(parts, "group")

    def solve(got, part, *extra):
        return kernel_call(
            m["solve"],
            [((rhs, width), F32)],
            got,
            part,
            maps,
            inverse,
            *extra,
            in_specs=[here, here, here, hbm] + [here] * len(extra),
            scratch_shapes=half_scratch,
            limit=48,
            **half_cost,
        )[0]

    with jax.named_scope("begin"):
        send, token = kernel_call(
            m["begin"],
            [((slots, block), BF16), mark],
            residual,
            cluster,
            peer,
            row,
            in_specs=[hbm] * 4,
            limit=60,
            scratch_shapes=[
                vmem((comps, rhs, own), F32),
                vmem((1, own), jnp.int32),
                vmem((1, over), jnp.int32),
                vmem((1, over), jnp.int32),
                vmem((own, lanes), BF16),
                pltpu.SemaphoreType.DMA((4,)),
            ],
        )
    with jax.named_scope("maps"):
        field16, maps = kernel_call(
            m["keep_maps"],
            [((own, lanes), BF16), ((m["map_rows"], slots), BF16)],
            residual,
            cluster,
            peer,
            after=[token],
        )
    with jax.named_scope("regroup"):
        matrix = regroup(coarse_inverse, groups, subs, cl_dev, comps)
        member = lax.axis_index("sub") % RING
        place = jnp.stack((place_of() if groups > 1 else (0, 0)) + (member,)).astype(jnp.int32).reshape(1, 3)
    with jax.named_scope("answer"):
        got = swap(send)
        send, token = kernel_call(
            m["answer"], [((slots, lanes + block), BF16), mark], got, field16, cluster
        )
        gives, gives_late, members = kernel_call(
            m["keep_answer"],
            [((own + slots, slots), BF16), ((own, slots), BF16), ((ROWS, block), F32)],
            got,
            after=[token],
        )
    with jax.named_scope("own_half_first"):
        part, half_token = kernel_call(
            m["half"],
            [((rhs, width), F32), mark],
            residual,
            inverse,
            after=[token],
            in_specs=[here, hbm],
            scratch_shapes=half_scratch,
            **half_cost,
        )
    with jax.named_scope("regroup"):
        pieces = pass_round(matrix, token)
        matrix, matrix_late = kernel_call(
            m["gather"],
            [(matrix.shape, BF16)] * 2,
            place,
            *pieces,
            after=[half_token],
            in_specs=[pl.BlockSpec(memory_space=pltpu.SMEM)] + [here] * len(pieces),
        )
    got = swap(send)

    with jax.named_scope("coarse_first"):
        parts = coarse_parts(matrix, got, each, [], [half_token, members])
    with jax.named_scope("solve_first"):
        total = solve(got, part)
    with jax.named_scope("return_first"):
        send, res_own, over_maps, sol, token = kernel_call(
            m["finish_first"],
            [
                ((slots, lanes + block + share), BF16),
                ((own, lanes), F32),
                (((2 + tail) * own, slots), BF16),
                ((ROWS, block), F32),
                mark,
            ],
            got,
            total,
            parts,
            maps,
            scratch_shapes=[vmem((own, lanes), BF16), vmem((over, lanes), BF16)],
        )
        got = swap(send)
    with jax.named_scope("combine"):
        send, third, spread, token = kernel_call(
            m["combine"],
            [((slots, lanes + block), BF16), ((slots, share), BF16), ((own, lanes), F32), mark],
            got,
            res_own,
            gives,
            members,
            sol,
        )
    with jax.named_scope("own_half_second"):
        pieces_x = [third]
        for step in range(1, RING):
            turn = [(i, i // RING * RING + (i - step) % RING) for i in range(subs)]
            pieces_x.append(lax.ppermute(third, "sub", turn))
        first, inner, part, over_add = kernel_call(
            m["half_first"],
            [((comps, rhs, own), F32), ((2, LANES), F32), ((rhs, width), F32), ((over, lanes), F32)],
            place,
            spread,
            maps,
            over_maps,
            residual,
            inverse,
            *pieces_x,
            after=[token],
            in_specs=[pl.BlockSpec(memory_space=pltpu.SMEM)] + [here] * 4 + [hbm] + [here] * RING,
            scratch_shapes=half_scratch + [vmem((slots, block), BF16)],
            limit=48,
            **half_cost,
        )
    got = swap(send)
    with jax.named_scope("coarse_second"):
        parts = coarse_parts(matrix_late, got, each + 16, [inner])
    with jax.named_scope("solve_second"):
        total = solve(got, part, over_add)
    with jax.named_scope("return_second"):
        send, res_own = kernel_call(
            m["finish_second"],
            [((slots, lanes + block), BF16), ((own, lanes), F32)],
            total,
            parts,
            maps,
            scratch_shapes=[vmem((over, lanes), BF16)],
        )
        got = swap(send)
    with jax.named_scope("end"):
        second = kernel_call(m["end"], [((comps, rhs, own), F32)], got, res_own, first, gives_late, maps)[0]
    return first.transpose(1, 0, 2), second.transpose(1, 0, 2)


def solution(mesh):
    placed = (
        P(None, None, ("group", "sub")),
        P(("group", "sub"), None, None),
        P(("group", "sub"), None),
        P(("group", "sub")),
        P(("group", "sub"), None),
        P(("group", "sub")),
    )
    return jax.shard_map(
        body,
        mesh=mesh,
        in_specs=placed,
        out_specs=(P(None, None, ("group", "sub")), P(None, None, ("group", "sub"))),
        check_vma=False,
    )
```

time: 213 us -> 194 us (0.911)
  waiting for transfers between devices: 67.6 us -> 28.5 us
  blocking collectives: 40.9 us -> 72 us
  local copies, waits for them, and re-layouts: 28.1 us -> 17.9 us
  matrix products: 2.62 us -> 5.41 us
    all_to_all x6 -> x5, waiting for transfers between devices: 67.6 us -> 9.59 us  [exchange(): return lax.all_to_all(values, axis, split_axis=0, concat_axis=0, tiled=True)]
    all_to_all x1 -> x2, blocking collectives: 40.9 us -> 72 us  [exchange(): return lax.all_to_all(values, axis, split_axis=0, concat_axis=0, tiled=True)]
    ppermute x4 -> x7, waiting for transfers between devices: 0.01 us -> 18.9 us  [the longest x3 10.2 us: body(): pieces_x.append(lax.ppermute(third, 'sub', turn))]
    unnamed x70 -> x42, local copies, waits for them, and re-layouts: 20.9 us -> 11.1 us
    all_to_all x6 -> x5, starting transfers between devices: 38.2 us -> 33 us  [exchange(): return lax.all_to_all(values, axis, split_axis=0, concat_axis=0, tiled=True)]
    ppermute x4 -> x7, starting transfers between devices: 5.02 us -> 9.96 us  [the longest x3 5.17 us: pass_round(): lax.ppermute(piece, 'group', [(i, (i - 2 * step) % groups) for i in range...]
    pallas_call x12 -> x15, Pallas kernels: 27 us -> 24.9 us  [kernel_call(): pl.pallas_call(lambda *refs: body(*refs[count:]), out_shape=[jax.ShapeDty...]
  transfers between devices with their start and end apart: 10 -> 12, of which waited for: 4 -> 9; matrix products, arithmetic and copies ran while one was open for 6% -> 6% of each run, Pallas kernels for 9% -> 8%
where the time goes in v3:
time: 194 us; the launch traced here: 193 us
  blocking collectives  72 us (37%)
  starting transfers between devices  42.9 us (22%)
  waiting for transfers between devices  28.5 us (15%)
  Pallas kernels  24.9 us (13%)
  local copies, waits for them, and re-layouts  17.9 us (9%)
  matrix products  5.41 us (3%)
    all_to_all x2, blocking collectives, exchange(): return lax.all_to_all(values, axis, split_axis=0, concat_axis=0, tiled=True)  72 us
    all_to_all x5, starting transfers between devices, exchange(): return lax.all_to_all(values, axis, split_axis=0, concat_axis=0, tiled=True)  33 us
    pallas_call x15, Pallas kernels, kernel_call(): pl.pallas_call(lambda *refs: body(*refs[count:]), out_shape=[jax.ShapeDty...  24.9 us
    unnamed x42, local copies, waits for them, and re-layouts  11.1 us
    ppermute x3, waiting for transfers between devices, body(): pieces_x.append(lax.ppermute(third, 'sub', turn))  10.2 us
    all_to_all x5, waiting for transfers between devices, exchange(): return lax.all_to_all(values, axis, split_axis=0, concat_axis=0, tiled=True)  9.59 us
    ppermute x3, waiting for transfers between devices, pass_round(): lax.ppermute(piece, 'group', [(i, (i - 2 * step) % groups) for i in range...  8.03 us
    ppermute x3, starting transfers between devices, pass_round(): lax.ppermute(piece, 'group', [(i, (i - 2 * step) % groups) for i in range...  5.17 us
  transfers between devices with their start and end apart: 12, of which 9 were waited for; matrix products, arithmetic and copies ran while one was open for 6% of the time, Pallas kernels for 8%

profile of v3, /device:TPU:10, one launch (start us, length us, event | category | flops | bytes accessed | tf_op | source)
XLA Modules:
  0.0 192.9 jit_solution(2940729251518920119)
XLA Ops:
  0.7 2.5 %begin.1 = (bf16[256,768]{1,0:T(8,128)(2,1)}, f32[8,128]{1,0:T(8,128)}) custom-call(f32[9,128,128]{2,1,0:T(8,128)} %bitcast.42, s32[1,128]{1,0:T(1,128)} %bitcast.55, s32[1,128]{1,0:T(1,128)} %bitcast.58, s32[1,128]{1,0:T(1,128)} %bitcast.69), custom_call_target="tpu_custom_call" | custom-call | tf_op jit(solution)/shard_map/begin/pallas_call | solution.py:52
  3.2 11.6 %all-to-all-start = ((bf16[32,8,768]{2,1,0:T(8,128)(2,1)}), bf16[32,8,768]{2,1,0:T(8,128)(2,1)S(1)}, u32[]{:S(2)}, u32[]{:S(2)}) async-start(bf16[32,8,768]{2,1,0:T(8,128)(2,1)} %bitcast.68), calls=%async_computation | async-start | bytes 786432 | tf_op jit(solution)/shard_map/answer/all_to_all | solution.py:24
  15.9 3.7 %reshape.72 = bf16[45,8,1440]{2,1,0:T(8,128)(2,1)} reshape(bf16[45,11520]{1,0:T(8,128)(2,1)} %param.10) | data formatting | bytes 2073600 | tf_op jit(solution)/shard_map/regroup/reshape | solution.py:390
  19.6 2.2 %convolution_convert_fusion = bf16[48,8,1440]{2,0,1:T(8,128)(2,1)S(1)} fusion(pred[48,45,1]{1,0,2:T(8,128)(4,1)S(1)} %copy-done.19, bf16[45,8,1440]{2,1,0:T(8,128)(2,1)} %reshape.72), kind=kOutput, calls=%fused_computation.4 | convolution fusion | flops 50319360 | bytes 2144880 | tf_op jit(solution)/shard_map/regroup/dot_general | solution.py:391
  21.9 3.2 %fusion.2 = bf16[384,1536]{1,0:T(8,128)(2,1)} fusion(bf16[384,1440]{1,0:T(8,128)(2,1)S(1)} %bitcast.66, s32[1536]{0:T(1024)S(1)} %copy-done.20), kind=kOutput, calls=%fused_computation.3 | convolution fusion | flops 1701494784 | bytes 2291712 | tf_op jit(solution)/shard_map/regroup/dot_general | solution.py:20
  25.0 3.8 %all-to-all-done = bf16[32,8,768]{2,1,0:T(8,128)(2,1)S(1)} async-done(((bf16[32,8,768]{2,1,0:T(8,128)(2,1)}), bf16[32,8,768]{2,1,0:T(8,128)(2,1)S(1)}, u32[]{:S(2)}, u32[]{:S(2)}) %all-to-all-start) | async-done | bytes 393248 | tf_op jit(solution)/shard_map/answer/all_to_all | solution.py:24
  30.2 6.0 %all-to-all-start.1 = ((bf16[32,8,1920]{2,1,0:T(8,128)(2,1)}), bf16[32,8,1920]{2,1,0:T(8,128)(2,1)S(1)}, u32[]{:S(2)}, u32[]{:S(2)}) async-start(bf16[32,8,1920]{2,1,0:T(8,128)(2,1)} %bitcast.6), calls=%async_computation.1 | async-start | bytes 1966080 | tf_op jit(solution)/shard_map/all_to_all | solution.py:24
  41.0 2.7 %collective-permute-start.2 = (bf16[2,48,1536]{2,1,0:T(8,128)(2,1)S(1)}, bf16[2,48,1536]{2,1,0:T(8,128)(2,1)S(1)}, u32[]{:S(2)}, u32[]{:S(2)}) collective-permute-start(bf16[2,48,1536]{2,1,0:T(8,128)(2,1)S(1)} %pad_maximum_fusion.2), channel_id=1, source_target_pairs={{0,128},{32,160},{64,192},{96,224},{128,0},{160,32},{192,64},{224,... | collective-permute-start | bytes 884744 | tf_op jit(solution)/shard_map/regroup/ppermute | solution.py:417
  45.6 3.1 %own_half_first.1 = (f32[128,2304]{1,0:T(8,128)S(1)}, f32[8,128]{1,0:T(8,128)S(1)}) custom-call(f32[8,128]{1,0:T(8,128)S(1)} %get-tuple-element.34.refs_0_, f32[9,128,128]{2,1,0:T(8,128)S(1)} %bitcast.44, bf16[9,2,128,2304]{3,2,1,0:T(8,128)(2,1)} %bitcast.60), custom_call_target="tpu_custom_call" | custom-call | flops 679477248 | bytes 5308416 | tf_op jit(solution)/shard_map/own_half_first/pallas_call | solution.py:52
  49.8 7.1 %collective-permute-done.2.refs_4_ = bf16[2,48,1536]{2,1,0:T(8,128)(2,1)S(1)} collective-permute-done((bf16[2,48,1536]{2,1,0:T(8,128)(2,1)S(1)}, bf16[2,48,1536]{2,1,0:T(8,128)(2,1)S(1)}, u32[]{:S(2)}, u32[]{:S(2)}) %collective-permute-start.2) | collective-permute-done | bytes 294944 | tf_op jit(solution)/shard_map/regroup/ppermute | solution.py:417
  59.6 2.7 %all-to-all-done.1 = bf16[32,8,1920]{2,1,0:T(8,128)(2,1)S(1)} async-done(((bf16[32,8,1920]{2,1,0:T(8,128)(2,1)}), bf16[32,8,1920]{2,1,0:T(8,128)(2,1)S(1)}, u32[]{:S(2)}, u32[]{:S(2)}) %all-to-all-start.1) | async-done | bytes 983072 | tf_op jit(solution)/shard_map/all_to_all | solution.py:24
  63.4 4.9 %all-to-all-start.2 = ((bf16[8,48,128]{2,1,0:T(8,128)(2,1)}), bf16[8,48,128]{2,1,0:T(8,128)(2,1)S(1)}, u32[]{:S(2)}, u32[]{:S(2)}) async-start(bf16[8,48,128]{2,1,0:T(8,128)(2,1)} %coarse_first.1), calls=%async_computation.2 | async-start | bytes 196608 | tf_op jit(solution)/shard_map/coarse_first/all_to_all | solution.py:24
  69.6 3.2 %solve_first.1.refs_1_ = f32[128,2304]{1,0:T(8,128)S(1)} custom-call(bf16[256,1920]{1,0:T(8,128)(2,1)S(1)} %bitcast.40, f32[128,2304]{1,0:T(8,128)S(1)} %copy-done.2, bf16[1024,256]{1,0:T(8,128)(2,1)S(1)} %get-tuple-element.36.refs_2_.refs_3_.refs_4_, bf16[9,2,128,2304]{3,2,1,0:T(8,128)(2,1)} %bitcast.61), custom_call_target="tpu_custom_call" | custom-call | flops 679477248 | bytes 5308416 | tf_op jit(solution)/shard_map/solve_first/pallas_call | solution.py:52
  73.7 38.4 %all_to_all.35 = bf16[32,8,2176]{2,1,0:T(8,128)(2,1)S(1)} all-to-all(bf16[32,8,2176]{2,1,0:T(8,128)(2,1)S(1)} %bitcast.52), channel_id=1, replica_groups=mesh['group'=8,'sub'=32] {'sub'}, dimensions={0} | all-to-all | bytes 2228224 | tf_op jit(solution)/shard_map/return_first/all_to_all | solution.py:24
  114.5 5.6 %all-to-all-start.4 = ((bf16[32,8,1920]{2,1,0:T(8,128)(2,1)}), bf16[32,8,1920]{2,1,0:T(8,128)(2,1)S(1)}, u32[]{:S(2)}, u32[]{:S(2)}) async-start(bf16[32,8,1920]{2,1,0:T(8,128)(2,1)} %bitcast.25), calls=%async_computation.4 | async-start | bytes 1966080 | tf_op jit(solution)/shard_map/all_to_all | solution.py:24
  122.6 2.3 %collective-permute-start.4 = (bf16[256,256]{1,0:T(8,128)(2,1)S(1)}, bf16[256,256]{1,0:T(8,128)(2,1)S(1)}, u32[]{:S(2)}, u32[]{:S(2)}) collective-permute-start(bf16[256,256]{1,0:T(8,128)(2,1)S(1)} %get-tuple-element.48.refs_7_), channel_id=1, source_target_pairs={{0,3},{1,0},{2,1},{3,2},{4,7},{5,4},{6,5},{7,6},{8,11},{9,8},{10,9... | collective-permute-start | bytes 393224 | tf_op jit(solution)/shard_map/own_half_second/ppermute | solution.py:577
  124.9 3.9 %collective-permute-done.6.refs_10_ = bf16[256,256]{1,0:T(8,128)(2,1)S(1)} collective-permute-done((bf16[256,256]{1,0:T(8,128)(2,1)S(1)}, bf16[256,256]{1,0:T(8,128)(2,1)S(1)}, u32[]{:S(2)}, u32[]{:S(2)}) %collective-permute-start.6) | collective-permute-done | bytes 131104 | tf_op jit(solution)/shard_map/own_half_second/ppermute | solution.py:577
  128.8 3.7 %collective-permute-done.5.refs_9_ = bf16[256,256]{1,0:T(8,128)(2,1)S(1)} collective-permute-done((bf16[256,256]{1,0:T(8,128)(2,1)S(1)}, bf16[256,256]{1,0:T(8,128)(2,1)S(1)}, u32[]{:S(2)}, u32[]{:S(2)}) %collective-permute-start.5) | collective-permute-done | bytes 131104 | tf_op jit(solution)/shard_map/own_half_second/ppermute | solution.py:577
  132.5 2.6 %collective-permute-done.4.refs_8_ = bf16[256,256]{1,0:T(8,128)(2,1)S(1)} collective-permute-done((bf16[256,256]{1,0:T(8,128)(2,1)S(1)}, bf16[256,256]{1,0:T(8,128)(2,1)S(1)}, u32[]{:S(2)}, u32[]{:S(2)}) %collective-permute-start.4) | collective-permute-done | bytes 131104 | tf_op jit(solution)/shard_map/own_half_second/ppermute | solution.py:577
  137.1 3.9 %own_half_second.1 = (f32[9,128,128]{2,1,0:T(8,128)}, f32[2,128]{1,0:T(2,128)S(1)}, f32[128,2304]{1,0:T(8,128)S(1)}, f32[128,1152]{1,0:T(8,128)S(1)}) custom-call(f32[8,128]{1,0:T(8,128)S(1)} %get-tuple-element.45.refs_0_, s32[1,3]{1,0:T(1,128)S(1)} %add_bitcast_fusion.refs_1_, f32[128,1152]{1,0:T(8,128)S(1)} %copy-done.8, ...), custom_call_target="tpu_custom_call" | custom-call | flops 679477248 | bytes 5308416 | tf_op jit(solution)/shard_map/own_half_second/pallas_call | solution.py:52
  142.9 3.1 %all-to-all-done.4 = bf16[32,8,1920]{2,1,0:T(8,128)(2,1)S(1)} async-done(((bf16[32,8,1920]{2,1,0:T(8,128)(2,1)}), bf16[32,8,1920]{2,1,0:T(8,128)(2,1)S(1)}, u32[]{:S(2)}, u32[]{:S(2)}) %all-to-all-start.4) | async-done | bytes 983072 | tf_op jit(solution)/shard_map/all_to_all | solution.py:24
  147.1 4.8 %all-to-all-start.5 = ((bf16[8,64,128]{2,1,0:T(8,128)(2,1)}), bf16[8,64,128]{2,1,0:T(8,128)(2,1)S(1)}, u32[]{:S(2)}, u32[]{:S(2)}) async-start(bf16[8,64,128]{2,1,0:T(8,128)(2,1)} %coarse_second.1), calls=%async_computation.5 | async-start | bytes 262144 | tf_op jit(solution)/shard_map/coarse_second/all_to_all | solution.py:24
  154.3 3.1 %solve_second.1.refs_0_ = f32[128,2304]{1,0:T(8,128)S(1)} custom-call(bf16[256,1920]{1,0:T(8,128)(2,1)S(1)} %bitcast.47, f32[128,2304]{1,0:T(8,128)S(1)} %copy-done.4, bf16[1024,256]{1,0:T(8,128)(2,1)S(1)} %get-tuple-element.36.refs_2_.refs_3_.refs_4_, bf16[9,2,128,2304]{3,2,1,0:T(8,128)(2,1)} %bitcast.63, f32[128,1152]{1,0:T(8,128)S(1)} %copy-done.10), custom_call_target="tpu_custom_call" | custom-call | flops 679477248 | bytes 5308416 | tf_op jit(solution)/shard_map/solve_second/pallas_call | solution.py:52
  157.9 33.6 %all_to_all.36 = bf16[32,8,1920]{2,1,0:T(8,128)(2,1)S(1)} all-to-all(bf16[32,8,1920]{2,1,0:T(8,128)(2,1)S(1)} %bitcast.53), channel_id=1, replica_groups=mesh['group'=8,'sub'=32] {'sub'}, dimensions={0} | all-to-all | bytes 1966080 | tf_op jit(solution)/shard_map/return_second/all_to_all | solution.py:24
  (70 shorter events, 30.2 us)
Async XLA Ops:
  0.6 14.2 %copy-start.18 = (s32[128,1]{0,1:T(1,128)S(1)}, s32[128,1]{0,1:T(1,128)}, u32[]{:S(2)}) copy-start(s32[128,1]{0,1:T(1,128)} %param.12) | copy-start | bytes 1540
  0.6 14.2 %copy-start.16 = (s32[128]{0:T(128)S(1)}, s32[128]{0:T(128)}, u32[]{:S(2)}) copy-start(s32[128]{0:T(128)} %param.11) | copy-start | bytes 1540
  0.7 14.2 %copy-start = (f32[128,9,128]{2,0,1:T(8,128)S(1)}, f32[128,9,128]{2,0,1:T(8,128)}, u32[]{:S(2)}) copy-start(f32[128,9,128]{2,0,1:T(8,128)} %param.8) | copy-start | bytes 1769476
  3.2 25.7 %all-to-all-start = ((bf16[32,8,768]{2,1,0:T(8,128)(2,1)}), bf16[32,8,768]{2,1,0:T(8,128)(2,1)S(1)}, u32[]{:S(2)}, u32[]{:S(2)}) async-start(bf16[32,8,768]{2,1,0:T(8,128)(2,1)} %bitcast.68), calls=%async_computation | async-start | bytes 786432 | tf_op jit(solution)/shard_map/answer/all_to_all | solution.py:24
  15.9 3.7 %copy-start.19 = (pred[48,45,1]{1,0,2:T(8,128)(4,1)S(1)}, pred[48,45,1]{1,0,2:T(8,128)(4,1)}, u32[]{:S(2)}) copy-start(pred[48,45,1]{1,0,2:T(8,128)(4,1)} %constant.187) | copy-start | bytes 6484
  19.6 2.2 %copy-start.20 = (s32[1536]{0:T(1024)S(1)}, s32[1536]{0:T(1024)}, u32[]{:S(2)}) copy-start(s32[1536]{0:T(1024)} %constant.180.clone) | copy-start | bytes 18436
  30.2 32.1 %all-to-all-start.1 = ((bf16[32,8,1920]{2,1,0:T(8,128)(2,1)}), bf16[32,8,1920]{2,1,0:T(8,128)(2,1)S(1)}, u32[]{:S(2)}, u32[]{:S(2)}) async-start(bf16[32,8,1920]{2,1,0:T(8,128)(2,1)} %bitcast.6), calls=%async_computation.1 | async-start | bytes 1966080 | tf_op jit(solution)/shard_map/all_to_all | solution.py:24
  38.1 2.2 %collective-permute-start = (bf16[4,48,1536]{2,1,0:T(8,128)(2,1)}, bf16[4,48,1536]{2,1,0:T(8,128)(2,1)S(1)}, u32[]{:S(2)}, u32[]{:S(2)}) collective-permute-start(bf16[4,48,1536]{2,1,0:T(8,128)(2,1)} %dynamic-slice_bitcast_fusion), channel_id=1, source_target_pairs={{0,32},{32,0},{64,96},{96,64},{128,160},{160,128},{192,224},{224,1... | collective-permute-start | bytes 1769480 | tf_op jit(solution)/shard_map/regroup/ppermute | solution.py:411
  39.5 1.4 copy-start.14
  40.4 9.4 %collective-permute-start.1 = (bf16[2,48,1536]{2,1,0:T(8,128)(2,1)S(1)}, bf16[2,48,1536]{2,1,0:T(8,128)(2,1)S(1)}, u32[]{:S(2)}, u32[]{:S(2)}) collective-permute-start(bf16[2,48,1536]{2,1,0:T(8,128)(2,1)S(1)} %pad_maximum_fusion.1), channel_id=1, source_target_pairs={{0,192},{32,224},{64,0},{96,32},{128,64},{160,96},{192,128},{224,1... | collective-permute-start | bytes 884744 | tf_op jit(solution)/shard_map/regroup/ppermute | solution.py:417
  41.0 15.9 %collective-permute-start.2 = (bf16[2,48,1536]{2,1,0:T(8,128)(2,1)S(1)}, bf16[2,48,1536]{2,1,0:T(8,128)(2,1)S(1)}, u32[]{:S(2)}, u32[]{:S(2)}) collective-permute-start(bf16[2,48,1536]{2,1,0:T(8,128)(2,1)S(1)} %pad_maximum_fusion.2), channel_id=1, source_target_pairs={{0,128},{32,160},{64,192},{96,224},{128,0},{160,32},{192,64},{224,... | collective-permute-start | bytes 884744 | tf_op jit(solution)/shard_map/regroup/ppermute | solution.py:417
  43.7 14.1 %collective-permute-start.3 = (bf16[2,48,1536]{2,1,0:T(8,128)(2,1)S(1)}, bf16[2,48,1536]{2,1,0:T(8,128)(2,1)S(1)}, u32[]{:S(2)}, u32[]{:S(2)}) collective-permute-start(bf16[2,48,1536]{2,1,0:T(8,128)(2,1)S(1)} %pad_maximum_fusion.3), channel_id=1, source_target_pairs={{0,64},{32,96},{64,128},{96,160},{128,192},{160,224},{192,0},{224,... | collective-permute-start | bytes 884744 | tf_op jit(solution)/shard_map/regroup/ppermute | solution.py:417
  63.4 9.4 %all-to-all-start.2 = ((bf16[8,48,128]{2,1,0:T(8,128)(2,1)}), bf16[8,48,128]{2,1,0:T(8,128)(2,1)S(1)}, u32[]{:S(2)}, u32[]{:S(2)}) async-start(bf16[8,48,128]{2,1,0:T(8,128)(2,1)} %coarse_first.1), calls=%async_computation.2 | async-start | bytes 196608 | tf_op jit(solution)/shard_map/coarse_first/all_to_all | solution.py:24
  68.3 1.3 copy-start.2
  73.7 40.0 %copy-start.12 = (bf16[640,256]{1,0:T(8,128)(2,1)}, bf16[640,256]{1,0:T(8,128)(2,1)S(1)}, u32[]{:S(2)}) copy-start(bf16[640,256]{1,0:T(8,128)(2,1)S(1)} %get-tuple-element.47.refs_4_) | copy-start | bytes 983044
  73.7 38.5 %copy-start.15 = (bf16[384,256]{1,0:T(8,128)(2,1)S(1)}, bf16[384,256]{1,0:T(8,128)(2,1)}, u32[]{:S(2)}) copy-start(bf16[384,256]{1,0:T(8,128)(2,1)} %copy-done.14) | copy-start | bytes 589828
  114.5 31.5 %all-to-all-start.4 = ((bf16[32,8,1920]{2,1,0:T(8,128)(2,1)}), bf16[32,8,1920]{2,1,0:T(8,128)(2,1)S(1)}, u32[]{:S(2)}, u32[]{:S(2)}) async-start(bf16[32,8,1920]{2,1,0:T(8,128)(2,1)} %bitcast.25), calls=%async_computation.4 | async-start | bytes 1966080 | tf_op jit(solution)/shard_map/all_to_all | solution.py:24
  120.1 8.7 %collective-permute-start.6 = (bf16[256,256]{1,0:T(8,128)(2,1)S(1)}, bf16[256,256]{1,0:T(8,128)(2,1)S(1)}, u32[]{:S(2)}, u32[]{:S(2)}) collective-permute-start(bf16[256,256]{1,0:T(8,128)(2,1)S(1)} %get-tuple-element.48.refs_7_), channel_id=1, source_target_pairs={{0,1},{1,2},{2,3},{3,0},{4,5},{5,6},{6,7},{7,4},{8,9},{9,10},{10,1... | collective-permute-start | bytes 393224 | tf_op jit(solution)/shard_map/own_half_second/ppermute | solution.py:577
  121.7 10.8 %collective-permute-start.5 = (bf16[256,256]{1,0:T(8,128)(2,1)S(1)}, bf16[256,256]{1,0:T(8,128)(2,1)S(1)}, u32[]{:S(2)}, u32[]{:S(2)}) collective-permute-start(bf16[256,256]{1,0:T(8,128)(2,1)S(1)} %get-tuple-element.48.refs_7_), channel_id=1, source_target_pairs={{0,2},{1,3},{2,0},{3,1},{4,6},{5,7},{6,4},{7,5},{8,10},{9,11},{10,... | collective-permute-start | bytes 393224 | tf_op jit(solution)/shard_map/own_half_second/ppermute | solution.py:577
  122.6 12.5 %collective-permute-start.4 = (bf16[256,256]{1,0:T(8,128)(2,1)S(1)}, bf16[256,256]{1,0:T(8,128)(2,1)S(1)}, u32[]{:S(2)}, u32[]{:S(2)}) collective-permute-start(bf16[256,256]{1,0:T(8,128)(2,1)S(1)} %get-tuple-element.48.refs_7_), channel_id=1, source_target_pairs={{0,3},{1,0},{2,1},{3,2},{4,7},{5,4},{6,5},{7,6},{8,11},{9,8},{10,9... | collective-permute-start | bytes 393224 | tf_op jit(solution)/shard_map/own_half_second/ppermute | solution.py:577
  137.1 8.9 %copy-start.6 = (bf16[8,48,1536]{2,1,0:T(8,128)(2,1)S(1)}, bf16[8,48,1536]{2,1,0:T(8,128)(2,1)}, u32[]{:S(2)}) copy-start(bf16[8,48,1536]{2,1,0:T(8,128)(2,1)} %copy-done.5) | copy-start | bytes 3538948
  147.1 10.3 %all-to-all-start.5 = ((bf16[8,64,128]{2,1,0:T(8,128)(2,1)}), bf16[8,64,128]{2,1,0:T(8,128)(2,1)S(1)}, u32[]{:S(2)}, u32[]{:S(2)}) async-start(bf16[8,64,128]{2,1,0:T(8,128)(2,1)} %coarse_second.1), calls=%async_computation.5 | async-start | bytes 262144 | tf_op jit(solution)/shard_map/coarse_second/all_to_all | solution.py:24
  151.9 1.3 copy-start.4
  157.9 33.6 %copy-start.11 = (f32[9,128,128]{2,1,0:T(8,128)S(1)}, f32[9,128,128]{2,1,0:T(8,128)}, u32[]{:S(2)}) copy-start(f32[9,128,128]{2,1,0:T(8,128)} %get-tuple-element.49.refs_2_) | copy-start | bytes 1769476
  (9 other events, 8.5 us)

commit v4 on v3

--- a/solution.py
+++ b/solution.py
@@ -2,7 +2,6 @@
 
 import jax
 import jax.numpy as jnp
-import numpy as np
 from jax import lax
 from jax.experimental import pallas as pl
 from jax.experimental.pallas import tpu as pltpu
@@ -177,17 +176,58 @@
             count = jnp.where(small < cl_dev, base, numbers[t]) if t < cl_dev else base
             members[:, t * LANES : (t + 1) * LANES] = count
 
-    def gather(place, *refs):
+    def prepare(place, rows, kept, given, lined):
+        cl_rows = cl_dev * comps
+        grp_rows = cl_rows * subs
+        each = main * ROWS
+        window = main * slots
+        turns = groups // 2
+        at = iota((each, cl_rows), 0)
+        t, i = at // ROWS, at % ROWS
+        source = jnp.where(i < cl_dev, i * comps + t, t * comps + main + i - cl_dev)
+        source = jnp.where((i < cl_dev) | (t < cl_dev), source, -1)
+        pick = (source == iota((each, cl_rows), 1)).astype(F32).astype(BF16)
+        for g in range(groups):
+            start = g * grp_rows // LANES * LANES
+            values = dot(pick, rows[:, start : start + window])
+            shift = g * grp_rows - start
+            if shift:
+                values = pltpu.roll(values, window - shift, 1)
+            lined[g] = values.astype(BF16)
+        turned = []
+        for side in range(2):
+            parts = []
+            for step in range(turns):
+                turn = place[0, 1] - step
+                turn = jnp.where(turn < 0, turn + turns, turn)
+                core = place[0, 0] if side == 0 else 1 - place[0, 0]
+                parts.append(lined[2 * turn + core])
+            turned.append(jnp.concatenate(parts, axis=0))
+        lane = iota((window, slots), 1)
+        row = iota((window, slots), 0)
+        holder, i = lane // ROWS, lane % ROWS
+        for t in range(main):
+            if t < cl_dev:
+                source = holder * cl_rows + jnp.where(i < cl_dev, i * comps + t, t * comps + main + i - cl_dev)
+            else:
+                source = jnp.where(i < cl_dev, holder * cl_rows + i * comps + t, -1)
+            moved = (source == row).astype(F32).astype(BF16)
+            for values, out in zip(turned, (kept, given)):
+                value = dot(values, moved).astype(BF16)
+                for step in range(turns):
+                    out[step, :, t * slots : (t + 1) * slots] = value[step * each : (step + 1) * each]
+
+    def gather(place, own_piece, other_piece, *refs):
         pieces, outs = refs[:-2], refs[-2:]
-        turns = len(pieces)
-        sides = pieces[0].shape[0]
-        for step, piece in enumerate(pieces):
+        turns = len(pieces) + 1
+        for step in range(turns):
             turn = place[0, 1] + step
             turn = jnp.where(turn >= turns, turn - turns, turn)
-            for side in range(sides):
+            for side in range(2):
                 core = place[0, 0] if side == 0 else 1 - place[0, 0]
+                value = pieces[step - 1][side] if step else (own_piece, other_piece)[side][...]
                 for out in outs:
-                    out[sides * turn + core] = piece[side]
+                    out[2 * turn + core] = value
 
     def coarse(offset, rows, matrix, got, *refs):
         out = refs[-1]
@@ -367,55 +407,19 @@
     return dict(locals())
 
 
-def block_order(cl_dev, comps, count):
-    tail = ROWS - cl_dev
-    main = comps - tail
-    order = np.full((main, count, ROWS), -1, np.int32)
-    for t in range(main):
-        for i in range(ROWS):
-            if i < cl_dev:
-                order[t, :, i] = np.arange(count) * cl_dev * comps + i * comps + t
-            elif t < cl_dev:
-                order[t, :, i] = np.arange(count) * cl_dev * comps + t * comps + main + i - cl_dev
-    return order.reshape(-1)
-
-
-def regroup(coarse_inverse, groups, subs, cl_dev, comps):
-    cl_rows = cl_dev * comps
-    grp_rows = cl_rows * subs
-    row_order = block_order(cl_dev, comps, 1)
-    col_order = block_order(cl_dev, comps, subs)
-    pick_rows = jnp.asarray(row_order[:, None] == np.arange(cl_rows)[None, :]).astype(BF16)
-    pick_cols = (jnp.asarray(col_order)[None, :] == jnp.arange(grp_rows, dtype=jnp.int32)[:, None]).astype(BF16)
-    values = coarse_inverse.reshape(cl_rows, groups, grp_rows)
-    values = lax.dot_general(pick_rows, values, (((1,), (0,)), ((), ())), preferred_element_type=F32).astype(BF16)
-    values = values.transpose(1, 0, 2).reshape(groups * row_order.size, grp_rows)
-    return dot(values, pick_cols).astype(BF16).reshape(groups, row_order.size, col_order.size)
-
-
 def place_of():
     index = lax.axis_index("group")
     return index % 2, index // 2
 
 
-def pass_round(values, after):
-    groups = values.shape[0]
-    if groups == 1:
-        return [values]
-    turns = groups // 2
-    core, turn = place_of()
-    pairs = values.reshape((turns, 2) + values.shape[1:])
-    kept = lax.dynamic_index_in_dim(pairs, core, 1, keepdims=False)
-    given = lax.dynamic_index_in_dim(pairs, 1 - core, 1, keepdims=False)
-    given, after = lax.optimization_barrier((given, after))
+def pass_round(kept, given):
+    turns = kept.shape[0]
+    groups = 2 * turns
     other = lax.ppermute(given, "group", [(i, i ^ 1) for i in range(groups)])
-    pieces = []
-    for step in range(turns):
-        target = (turn - step) % turns
-        piece = jnp.stack([lax.dynamic_index_in_dim(part, target, 0, keepdims=False) for part in (kept, other)])
-        if step:
-            piece = lax.ppermute(piece, "group", [(i, (i - 2 * step) % groups) for i in range(groups)])
-        pieces.append(piece)
+    pieces = [kept[0], other[0]]
+    for step in range(1, turns):
+        piece = jnp.stack([kept[step], other[step]])
+        pieces.append(lax.ppermute(piece, "group", [(i, (i - 2 * step) % groups) for i in range(groups)]))
     return pieces
 
 
@@ -502,9 +506,19 @@
             after=[token],
         )
     with jax.named_scope("regroup"):
-        matrix = regroup(coarse_inverse, groups, subs, cl_dev, comps)
         member = lax.axis_index("sub") % RING
-        place = jnp.stack((place_of() if groups > 1 else (0, 0)) + (member,)).astype(jnp.int32).reshape(1, 3)
+        place = jnp.stack(place_of() + (member,)).astype(jnp.int32).reshape(1, 3)
+        columns = main * slots
+        kept, given = kernel_call(
+            m["prepare"],
+            [((groups // 2, each, columns), BF16)] * 2,
+            place,
+            coarse_inverse,
+            after=[token],
+            in_specs=[pl.BlockSpec(memory_space=pltpu.SMEM), here],
+            scratch_shapes=[vmem((groups, each, columns), BF16)],
+            flops=2 * groups * each * columns * columns,
+        )
     with jax.named_scope("answer"):
         got = swap(send)
         send, token = kernel_call(
@@ -528,10 +542,10 @@
             **half_cost,
         )
     with jax.named_scope("regroup"):
-        pieces = pass_round(matrix, token)
+        pieces = pass_round(kept, given)
         matrix, matrix_late = kernel_call(
             m["gather"],
-            [(matrix.shape, BF16)] * 2,
+            [((groups, each, columns), BF16)] * 2,
             place,
             *pieces,
             after=[half_token],

time: 194 us -> 190 us (0.979)
  waiting for transfers between devices: 28.5 us -> 34.8 us
  matrix products: 5.41 us -> 0 us
  local copies, waits for them, and re-layouts: 17.9 us -> 13 us
  Pallas kernels: 24.9 us -> 28.9 us
  blocking collectives: 72 us -> 69.3 us
    all_to_all x5, waiting for transfers between devices: 9.59 us -> 19.1 us  [exchange(): return lax.all_to_all(values, axis, split_axis=0, concat_axis=0, tiled=True)]
    dot_general x2 -> x0, matrix products: 5.41 us -> none  [the longest x1 3.17 us: dot(): return jnp.dot(left, right, preferred_element_type=F32)]
    pallas_call x15 -> x16, Pallas kernels: 24.9 us -> 28.9 us  [kernel_call(): pl.pallas_call(lambda *refs: body(*refs[count:]), out_shape=[jax.ShapeDty...]
    reshape x1 -> x0, local copies, waits for them, and re-layouts: 3.69 us -> none  [regroup(): values = coarse_inverse.reshape(cl_rows, groups, grp_rows)]
    all_to_all x2, blocking collectives: 72 us -> 69.3 us  [exchange(): return lax.all_to_all(values, axis, split_axis=0, concat_axis=0, tiled=True)]
    ppermute x3, waiting for transfers between devices: 8.03 us -> 5.55 us  [pass_round(): lax.ppermute(piece, 'group', [(i, (i - 2 * step) % groups) for i in range...]
    unnamed x42 -> x40, local copies, waits for them, and re-layouts: 11.1 us -> 11.8 us
  transfers between devices with their start and end apart: 12 -> 12, of which waited for: 9 -> 8; matrix products, arithmetic and copies ran while one was open for 6% -> 1% of each run, Pallas kernels for 8% -> 10%
where the time goes in v4:
time: 190 us
  blocking collectives  69.3 us (36%)
  starting transfers between devices  42.5 us (22%)
  waiting for transfers between devices  34.8 us (18%)
  Pallas kernels  28.9 us (15%)
  local copies, waits for them, and re-layouts  13 us (7%)
    all_to_all x2, blocking collectives, exchange(): return lax.all_to_all(values, axis, split_axis=0, concat_axis=0, tiled=True)  69.3 us
    all_to_all x5, starting transfers between devices, exchange(): return lax.all_to_all(values, axis, split_axis=0, concat_axis=0, tiled=True)  32.5 us
    pallas_call x16, Pallas kernels, kernel_call(): pl.pallas_call(lambda *refs: body(*refs[count:]), out_shape=[jax.ShapeDty...  28.9 us
    all_to_all x5, waiting for transfers between devices, exchange(): return lax.all_to_all(values, axis, split_axis=0, concat_axis=0, tiled=True)  19.1 us
    unnamed x40, local copies, waits for them, and re-layouts  11.8 us
    ppermute x3, waiting for transfers between devices, body(): pieces_x.append(lax.ppermute(third, 'sub', turn))  10.2 us
    ppermute x3, waiting for transfers between devices, pass_round(): lax.ppermute(piece, 'group', [(i, (i - 2 * step) % groups) for i in range...  5.55 us
    ppermute x3, starting transfers between devices, pass_round(): lax.ppermute(piece, 'group', [(i, (i - 2 * step) % groups) for i in range...  5.17 us
  transfers between devices with their start and end apart: 12, of which 8 were waited for; matrix products, arithmetic and copies ran while one was open for 1% of the time, Pallas kernels for 10%

profile of v4, /device:TPU:10, one launch (start us, length us, event | category | flops | bytes accessed | tf_op | source)
XLA Modules:
  0.0 189.5 jit_solution(15268881463989603453)
XLA Ops:
  0.6 2.5 %begin.1 = (bf16[256,768]{1,0:T(8,128)(2,1)}, f32[8,128]{1,0:T(8,128)}) custom-call(f32[9,128,128]{2,1,0:T(8,128)} %bitcast.29, s32[1,128]{1,0:T(1,128)} %bitcast.42, s32[1,128]{1,0:T(1,128)} %bitcast.45, s32[1,128]{1,0:T(1,128)} %bitcast.53), custom_call_target="tpu_custom_call" | custom-call | tf_op jit(solution)/shard_map/begin/pallas_call | solution.py:51
  3.2 11.6 %all-to-all-start = ((bf16[32,8,768]{2,1,0:T(8,128)(2,1)}), bf16[32,8,768]{2,1,0:T(8,128)(2,1)S(1)}, u32[]{:S(2)}, u32[]{:S(2)}) async-start(bf16[32,8,768]{2,1,0:T(8,128)(2,1)} %bitcast.52), calls=%async_computation | async-start | bytes 786432 | tf_op jit(solution)/shard_map/answer/all_to_all | solution.py:23
  15.6 3.9 %regroup.2 = (bf16[4,48,1536]{2,1,0:T(8,128)(2,1)S(1)}, bf16[4,48,1536]{2,1,0:T(8,128)(2,1)}) custom-call(f32[8,128]{1,0:T(8,128)S(1)} %copy-done.17, s32[1,3]{1,0:T(1,128)S(1)} %add_bitcast_fusion.refs_1_, bf16[45,11520]{1,0:T(8,128)(2,1)S(1)} %copy-done.19), custom_call_target="tpu_custom_call" | custom-call | flops 1811939328 | tf_op jit(solution)/shard_map/regroup/pallas_call | solution.py:51
  19.9 8.9 %all-to-all-done = bf16[32,8,768]{2,1,0:T(8,128)(2,1)S(1)} async-done(((bf16[32,8,768]{2,1,0:T(8,128)(2,1)}), bf16[32,8,768]{2,1,0:T(8,128)(2,1)S(1)}, u32[]{:S(2)}, u32[]{:S(2)}) %all-to-all-start) | async-done | bytes 393248 | tf_op jit(solution)/shard_map/answer/all_to_all | solution.py:23
  30.2 5.6 %all-to-all-start.1 = ((bf16[32,8,1920]{2,1,0:T(8,128)(2,1)}), bf16[32,8,1920]{2,1,0:T(8,128)(2,1)S(1)}, u32[]{:S(2)}, u32[]{:S(2)}) async-start(bf16[32,8,1920]{2,1,0:T(8,128)(2,1)} %bitcast.6), calls=%async_computation.1 | async-start | bytes 1966080 | tf_op jit(solution)/shard_map/all_to_all | solution.py:23
  37.6 2.7 %collective-permute-start.2 = (bf16[2,48,1536]{2,1,0:T(8,128)(2,1)S(1)}, bf16[2,48,1536]{2,1,0:T(8,128)(2,1)S(1)}, u32[]{:S(2)}, u32[]{:S(2)}) collective-permute-start(bf16[2,48,1536]{2,1,0:T(8,128)(2,1)S(1)} %pad_maximum_fusion.1), channel_id=1, source_target_pairs={{0,128},{32,160},{64,192},{96,224},{128,0},{160,32},{192,64},{224,... | collective-permute-start | bytes 884744 | tf_op jit(solution)/shard_map/regroup/ppermute | solution.py:422
  40.3 2.0 %collective-permute-start.3 = (bf16[2,48,1536]{2,1,0:T(8,128)(2,1)S(1)}, bf16[2,48,1536]{2,1,0:T(8,128)(2,1)S(1)}, u32[]{:S(2)}, u32[]{:S(2)}) collective-permute-start(bf16[2,48,1536]{2,1,0:T(8,128)(2,1)S(1)} %pad_maximum_fusion.2), channel_id=1, source_target_pairs={{0,64},{32,96},{64,128},{96,160},{128,192},{160,224},{192,0},{224,... | collective-permute-start | bytes 884744 | tf_op jit(solution)/shard_map/regroup/ppermute | solution.py:422
  43.1 3.1 %own_half_first.1 = (f32[128,2304]{1,0:T(8,128)S(1)}, f32[8,128]{1,0:T(8,128)S(1)}) custom-call(f32[8,128]{1,0:T(8,128)S(1)} %get-tuple-element.35.refs_0_, f32[9,128,128]{2,1,0:T(8,128)S(1)} %bitcast.31, bf16[9,2,128,2304]{3,2,1,0:T(8,128)(2,1)} %bitcast.47), custom_call_target="tpu_custom_call" | custom-call | flops 679477248 | bytes 5308416 | tf_op jit(solution)/shard_map/own_half_first/pallas_call | solution.py:51
  47.2 4.6 %collective-permute-done.2.refs_5_ = bf16[2,48,1536]{2,1,0:T(8,128)(2,1)S(1)} collective-permute-done((bf16[2,48,1536]{2,1,0:T(8,128)(2,1)S(1)}, bf16[2,48,1536]{2,1,0:T(8,128)(2,1)S(1)}, u32[]{:S(2)}, u32[]{:S(2)}) %collective-permute-start.2) | collective-permute-done | bytes 294944 | tf_op jit(solution)/shard_map/regroup/ppermute | solution.py:422
  54.5 7.1 %all-to-all-done.1 = bf16[32,8,1920]{2,1,0:T(8,128)(2,1)S(1)} async-done(((bf16[32,8,1920]{2,1,0:T(8,128)(2,1)}), bf16[32,8,1920]{2,1,0:T(8,128)(2,1)S(1)}, u32[]{:S(2)}, u32[]{:S(2)}) %all-to-all-start.1) | async-done | bytes 983072 | tf_op jit(solution)/shard_map/all_to_all | solution.py:23
  62.7 4.9 %all-to-all-start.2 = ((bf16[8,48,128]{2,1,0:T(8,128)(2,1)}), bf16[8,48,128]{2,1,0:T(8,128)(2,1)S(1)}, u32[]{:S(2)}, u32[]{:S(2)}) async-start(bf16[8,48,128]{2,1,0:T(8,128)(2,1)} %coarse_first.1), calls=%async_computation.2 | async-start | bytes 196608 | tf_op jit(solution)/shard_map/coarse_first/all_to_all | solution.py:23
  68.9 3.2 %solve_first.1.refs_1_ = f32[128,2304]{1,0:T(8,128)S(1)} custom-call(bf16[256,1920]{1,0:T(8,128)(2,1)S(1)} %bitcast.27, f32[128,2304]{1,0:T(8,128)S(1)} %copy-done.2, bf16[1024,256]{1,0:T(8,128)(2,1)S(1)} %get-tuple-element.37.refs_2_.refs_3_.refs_4_, bf16[9,2,128,2304]{3,2,1,0:T(8,128)(2,1)} %bitcast.48), custom_call_target="tpu_custom_call" | custom-call | flops 679477248 | bytes 5308416 | tf_op jit(solution)/shard_map/solve_first/pallas_call | solution.py:51
  73.1 35.7 %all_to_all.35 = bf16[32,8,2176]{2,1,0:T(8,128)(2,1)S(1)} all-to-all(bf16[32,8,2176]{2,1,0:T(8,128)(2,1)S(1)} %bitcast.39), channel_id=1, replica_groups=mesh['group'=8,'sub'=32] {'sub'}, dimensions={0} | all-to-all | bytes 2228224 | tf_op jit(solution)/shard_map/return_first/all_to_all | solution.py:23
  111.1 5.6 %all-to-all-start.4 = ((bf16[32,8,1920]{2,1,0:T(8,128)(2,1)}), bf16[32,8,1920]{2,1,0:T(8,128)(2,1)S(1)}, u32[]{:S(2)}, u32[]{:S(2)}) async-start(bf16[32,8,1920]{2,1,0:T(8,128)(2,1)} %bitcast.18), calls=%async_computation.4 | async-start | bytes 1966080 | tf_op jit(solution)/shard_map/all_to_all | solution.py:23
  116.8 1.5 collective-permute-start.6
  119.3 2.3 %collective-permute-start.4 = (bf16[256,256]{1,0:T(8,128)(2,1)S(1)}, bf16[256,256]{1,0:T(8,128)(2,1)S(1)}, u32[]{:S(2)}, u32[]{:S(2)}) collective-permute-start(bf16[256,256]{1,0:T(8,128)(2,1)S(1)} %get-tuple-element.50.refs_7_), channel_id=1, source_target_pairs={{0,3},{1,0},{2,1},{3,2},{4,7},{5,4},{6,5},{7,6},{8,11},{9,8},{10,9... | collective-permute-start | bytes 393224 | tf_op jit(solution)/shard_map/own_half_second/ppermute | solution.py:591
  121.6 3.9 %collective-permute-done.6.refs_10_ = bf16[256,256]{1,0:T(8,128)(2,1)S(1)} collective-permute-done((bf16[256,256]{1,0:T(8,128)(2,1)S(1)}, bf16[256,256]{1,0:T(8,128)(2,1)S(1)}, u32[]{:S(2)}, u32[]{:S(2)}) %collective-permute-start.6) | collective-permute-done | bytes 131104 | tf_op jit(solution)/shard_map/own_half_second/ppermute | solution.py:591
  125.5 3.7 %collective-permute-done.5.refs_9_ = bf16[256,256]{1,0:T(8,128)(2,1)S(1)} collective-permute-done((bf16[256,256]{1,0:T(8,128)(2,1)S(1)}, bf16[256,256]{1,0:T(8,128)(2,1)S(1)}, u32[]{:S(2)}, u32[]{:S(2)}) %collective-permute-start.5) | collective-permute-done | bytes 131104 | tf_op jit(solution)/shard_map/own_half_second/ppermute | solution.py:591
  129.1 2.6 %collective-permute-done.4.refs_8_ = bf16[256,256]{1,0:T(8,128)(2,1)S(1)} collective-permute-done((bf16[256,256]{1,0:T(8,128)(2,1)S(1)}, bf16[256,256]{1,0:T(8,128)(2,1)S(1)}, u32[]{:S(2)}, u32[]{:S(2)}) %collective-permute-start.4) | collective-permute-done | bytes 131104 | tf_op jit(solution)/shard_map/own_half_second/ppermute | solution.py:591
  133.8 3.9 %own_half_second.1 = (f32[9,128,128]{2,1,0:T(8,128)}, f32[2,128]{1,0:T(2,128)S(1)}, f32[128,2304]{1,0:T(8,128)S(1)}, f32[128,1152]{1,0:T(8,128)S(1)}) custom-call(f32[8,128]{1,0:T(8,128)S(1)} %get-tuple-element.47.refs_0_, s32[1,3]{1,0:T(1,128)S(1)} %add_bitcast_fusion.refs_1_, f32[128,1152]{1,0:T(8,128)S(1)} %copy-done.8, ...), custom_call_target="tpu_custom_call" | custom-call | flops 679477248 | bytes 5308416 | tf_op jit(solution)/shard_map/own_half_second/pallas_call | solution.py:51
  139.6 3.1 %all-to-all-done.4 = bf16[32,8,1920]{2,1,0:T(8,128)(2,1)S(1)} async-done(((bf16[32,8,1920]{2,1,0:T(8,128)(2,1)}), bf16[32,8,1920]{2,1,0:T(8,128)(2,1)S(1)}, u32[]{:S(2)}, u32[]{:S(2)}) %all-to-all-start.4) | async-done | bytes 983072 | tf_op jit(solution)/shard_map/all_to_all | solution.py:23
  143.8 4.8 %all-to-all-start.5 = ((bf16[8,64,128]{2,1,0:T(8,128)(2,1)}), bf16[8,64,128]{2,1,0:T(8,128)(2,1)S(1)}, u32[]{:S(2)}, u32[]{:S(2)}) async-start(bf16[8,64,128]{2,1,0:T(8,128)(2,1)} %coarse_second.1), calls=%async_computation.5 | async-start | bytes 262144 | tf_op jit(solution)/shard_map/coarse_second/all_to_all | solution.py:23
  150.9 3.1 %solve_second.1.refs_0_ = f32[128,2304]{1,0:T(8,128)S(1)} custom-call(bf16[256,1920]{1,0:T(8,128)(2,1)S(1)} %bitcast.34, f32[128,2304]{1,0:T(8,128)S(1)} %copy-done.4, bf16[1024,256]{1,0:T(8,128)(2,1)S(1)} %get-tuple-element.37.refs_2_.refs_3_.refs_4_, bf16[9,2,128,2304]{3,2,1,0:T(8,128)(2,1)} %bitcast.50, f32[128,1152]{1,0:T(8,128)S(1)} %copy-done.10), custom_call_target="tpu_custom_call" | custom-call | flops 679477248 | bytes 5308416 | tf_op jit(solution)/shard_map/solve_second/pallas_call | solution.py:51
  154.5 33.6 %all_to_all.36 = bf16[32,8,1920]{2,1,0:T(8,128)(2,1)S(1)} all-to-all(bf16[32,8,1920]{2,1,0:T(8,128)(2,1)S(1)} %bitcast.40), channel_id=1, replica_groups=mesh['group'=8,'sub'=32] {'sub'}, dimensions={0} | all-to-all | bytes 1966080 | tf_op jit(solution)/shard_map/return_second/all_to_all | solution.py:23
  (64 shorter events, 24.7 us)
Async XLA Ops:
  0.6 14.3 %copy-start.19 = (bf16[45,11520]{1,0:T(8,128)(2,1)S(1)}, bf16[45,11520]{1,0:T(8,128)(2,1)}, u32[]{:S(2)}) copy-start(bf16[45,11520]{1,0:T(8,128)(2,1)} %refs_2_.1) | copy-start | bytes 3110404
  3.2 25.7 %all-to-all-start = ((bf16[32,8,768]{2,1,0:T(8,128)(2,1)}), bf16[32,8,768]{2,1,0:T(8,128)(2,1)S(1)}, u32[]{:S(2)}, u32[]{:S(2)}) async-start(bf16[32,8,768]{2,1,0:T(8,128)(2,1)} %bitcast.52), calls=%async_computation | async-start | bytes 786432 | tf_op jit(solution)/shard_map/answer/all_to_all | solution.py:23
  15.6 3.9 %copy-start = (f32[128,9,128]{2,0,1:T(8,128)S(1)}, f32[128,9,128]{2,0,1:T(8,128)}, u32[]{:S(2)}) copy-start(f32[128,9,128]{2,0,1:T(8,128)} %param.6) | copy-start | bytes 1769476
  15.6 3.9 %copy-start.16 = (s32[128]{0:T(128)S(1)}, s32[128]{0:T(128)}, u32[]{:S(2)}) copy-start(s32[128]{0:T(128)} %param.9) | copy-start | bytes 1540
  15.6 3.9 %copy-start.18 = (s32[128,1]{0,1:T(1,128)S(1)}, s32[128,1]{0,1:T(1,128)}, u32[]{:S(2)}) copy-start(s32[128,1]{0,1:T(1,128)} %param.10) | copy-start | bytes 1540
  19.5 16.3 %collective-permute-start = (bf16[4,48,1536]{2,1,0:T(8,128)(2,1)}, bf16[4,48,1536]{2,1,0:T(8,128)(2,1)}, u32[]{:S(2)}, u32[]{:S(2)}) collective-permute-start(bf16[4,48,1536]{2,1,0:T(8,128)(2,1)} %get-tuple-element.41), channel_id=1, source_target_pairs={{0,32},{32,0},{64,96},{96,64},{128,160},{160,128},{192,224},{224,1... | collective-permute-start | bytes 1769480 | tf_op jit(solution)/shard_map/regroup/ppermute | solution.py:418
  30.2 31.4 %all-to-all-start.1 = ((bf16[32,8,1920]{2,1,0:T(8,128)(2,1)}), bf16[32,8,1920]{2,1,0:T(8,128)(2,1)S(1)}, u32[]{:S(2)}, u32[]{:S(2)}) async-start(bf16[32,8,1920]{2,1,0:T(8,128)(2,1)} %bitcast.6), calls=%async_computation.1 | async-start | bytes 1966080 | tf_op jit(solution)/shard_map/all_to_all | solution.py:23
  37.0 10.2 %collective-permute-start.1 = (bf16[2,48,1536]{2,1,0:T(8,128)(2,1)S(1)}, bf16[2,48,1536]{2,1,0:T(8,128)(2,1)S(1)}, u32[]{:S(2)}, u32[]{:S(2)}) collective-permute-start(bf16[2,48,1536]{2,1,0:T(8,128)(2,1)S(1)} %pad_maximum_fusion), channel_id=1, source_target_pairs={{0,192},{32,224},{64,0},{96,32},{128,64},{160,96},{192,128},{224,1... | collective-permute-start | bytes 884744 | tf_op jit(solution)/shard_map/regroup/ppermute | solution.py:422
  37.6 14.3 %collective-permute-start.2 = (bf16[2,48,1536]{2,1,0:T(8,128)(2,1)S(1)}, bf16[2,48,1536]{2,1,0:T(8,128)(2,1)S(1)}, u32[]{:S(2)}, u32[]{:S(2)}) collective-permute-start(bf16[2,48,1536]{2,1,0:T(8,128)(2,1)S(1)} %pad_maximum_fusion.1), channel_id=1, source_target_pairs={{0,128},{32,160},{64,192},{96,224},{128,0},{160,32},{192,64},{224,... | collective-permute-start | bytes 884744 | tf_op jit(solution)/shard_map/regroup/ppermute | solution.py:422
  40.3 12.5 %collective-permute-start.3 = (bf16[2,48,1536]{2,1,0:T(8,128)(2,1)S(1)}, bf16[2,48,1536]{2,1,0:T(8,128)(2,1)S(1)}, u32[]{:S(2)}, u32[]{:S(2)}) collective-permute-start(bf16[2,48,1536]{2,1,0:T(8,128)(2,1)S(1)} %pad_maximum_fusion.2), channel_id=1, source_target_pairs={{0,64},{32,96},{64,128},{96,160},{128,192},{160,224},{192,0},{224,... | collective-permute-start | bytes 884744 | tf_op jit(solution)/shard_map/regroup/ppermute | solution.py:422
  62.7 9.4 %all-to-all-start.2 = ((bf16[8,48,128]{2,1,0:T(8,128)(2,1)}), bf16[8,48,128]{2,1,0:T(8,128)(2,1)S(1)}, u32[]{:S(2)}, u32[]{:S(2)}) async-start(bf16[8,48,128]{2,1,0:T(8,128)(2,1)} %coarse_first.1), calls=%async_computation.2 | async-start | bytes 196608 | tf_op jit(solution)/shard_map/coarse_first/all_to_all | solution.py:23
  67.7 1.3 copy-start.2
  73.1 37.3 %copy-start.12 = (bf16[640,256]{1,0:T(8,128)(2,1)}, bf16[640,256]{1,0:T(8,128)(2,1)S(1)}, u32[]{:S(2)}) copy-start(bf16[640,256]{1,0:T(8,128)(2,1)S(1)} %get-tuple-element.49.refs_4_) | copy-start | bytes 983044
  73.1 35.8 %copy-start.15 = (bf16[384,256]{1,0:T(8,128)(2,1)S(1)}, bf16[384,256]{1,0:T(8,128)(2,1)}, u32[]{:S(2)}) copy-start(bf16[384,256]{1,0:T(8,128)(2,1)} %copy-done.14) | copy-start | bytes 589828
  111.1 31.5 %all-to-all-start.4 = ((bf16[32,8,1920]{2,1,0:T(8,128)(2,1)}), bf16[32,8,1920]{2,1,0:T(8,128)(2,1)S(1)}, u32[]{:S(2)}, u32[]{:S(2)}) async-start(bf16[32,8,1920]{2,1,0:T(8,128)(2,1)} %bitcast.18), calls=%async_computation.4 | async-start | bytes 1966080 | tf_op jit(solution)/shard_map/all_to_all | solution.py:23
  116.8 8.7 %collective-permute-start.6 = (bf16[256,256]{1,0:T(8,128)(2,1)S(1)}, bf16[256,256]{1,0:T(8,128)(2,1)S(1)}, u32[]{:S(2)}, u32[]{:S(2)}) collective-permute-start(bf16[256,256]{1,0:T(8,128)(2,1)S(1)} %get-tuple-element.50.refs_7_), channel_id=1, source_target_pairs={{0,1},{1,2},{2,3},{3,0},{4,5},{5,6},{6,7},{7,4},{8,9},{9,10},{10,1... | collective-permute-start | bytes 393224 | tf_op jit(solution)/shard_map/own_half_second/ppermute | solution.py:591
  118.3 10.8 %collective-permute-start.5 = (bf16[256,256]{1,0:T(8,128)(2,1)S(1)}, bf16[256,256]{1,0:T(8,128)(2,1)S(1)}, u32[]{:S(2)}, u32[]{:S(2)}) collective-permute-start(bf16[256,256]{1,0:T(8,128)(2,1)S(1)} %get-tuple-element.50.refs_7_), channel_id=1, source_target_pairs={{0,2},{1,3},{2,0},{3,1},{4,6},{5,7},{6,4},{7,5},{8,10},{9,11},{10,... | collective-permute-start | bytes 393224 | tf_op jit(solution)/shard_map/own_half_second/ppermute | solution.py:591
  119.3 12.5 %collective-permute-start.4 = (bf16[256,256]{1,0:T(8,128)(2,1)S(1)}, bf16[256,256]{1,0:T(8,128)(2,1)S(1)}, u32[]{:S(2)}, u32[]{:S(2)}) collective-permute-start(bf16[256,256]{1,0:T(8,128)(2,1)S(1)} %get-tuple-element.50.refs_7_), channel_id=1, source_target_pairs={{0,3},{1,0},{2,1},{3,2},{4,7},{5,4},{6,5},{7,6},{8,11},{9,8},{10,9... | collective-permute-start | bytes 393224 | tf_op jit(solution)/shard_map/own_half_second/ppermute | solution.py:591
  131.7 1.1 copy-start.8
  133.8 8.9 %copy-start.6 = (bf16[8,48,1536]{2,1,0:T(8,128)(2,1)S(1)}, bf16[8,48,1536]{2,1,0:T(8,128)(2,1)}, u32[]{:S(2)}) copy-start(bf16[8,48,1536]{2,1,0:T(8,128)(2,1)} %copy-done.5) | copy-start | bytes 3538948
  143.8 10.3 %all-to-all-start.5 = ((bf16[8,64,128]{2,1,0:T(8,128)(2,1)}), bf16[8,64,128]{2,1,0:T(8,128)(2,1)S(1)}, u32[]{:S(2)}, u32[]{:S(2)}) async-start(bf16[8,64,128]{2,1,0:T(8,128)(2,1)} %coarse_second.1), calls=%async_computation.5 | async-start | bytes 262144 | tf_op jit(solution)/shard_map/coarse_second/all_to_all | solution.py:23
  148.6 1.3 copy-start.4
  149.8 1.1 copy-start.10
  154.5 33.6 %copy-start.11 = (f32[9,128,128]{2,1,0:T(8,128)S(1)}, f32[9,128,128]{2,1,0:T(8,128)}, u32[]{:S(2)}) copy-start(f32[9,128,128]{2,1,0:T(8,128)} %get-tuple-element.51.refs_2_) | copy-start | bytes 1769476
  (8 other events, 7.1 us)

commit v5 on v4

--- a/solution.py
+++ b/solution.py
@@ -109,7 +109,9 @@
 
     def begin(res_hbm, cl_hbm, peer_hbm, row_hbm, send, token, res, cl, peer, row, field16, sems):
         token[...] = jnp.zeros((ROWS, LANES), F32)
-        pairs = [(peer_hbm, peer), (row_hbm, row), (cl_hbm, cl), (res_hbm, res)]
+        third = comps // 3
+        pairs = [(peer_hbm, peer), (row_hbm, row), (cl_hbm, cl)]
+        pairs += [(res_hbm.at[pl.ds(j * third, third)], res.at[pl.ds(j * third, third)]) for j in range(3)]
         copies = [pltpu.make_async_copy(src, dst, sems.at[i]) for i, (src, dst) in enumerate(pairs)]
         for copy in copies:
             copy.start()
@@ -121,8 +123,9 @@
         wanted = jnp.sum(hot_dest * (row[...] + 1).astype(F32), axis=1, keepdims=True)
         counts = jnp.sum(hot, axis=1, keepdims=True)
         extra = jnp.where(lane == inner, wanted, 0.0) + jnp.where(lane == inner + ROWS, counts, 0.0)
-        copies[3].wait()
-        for k in range(comps):
+        for k in range(comps):
+            if k % third == 0:
+                copies[3 + k // third].wait()
             field16[:, k * LANES : (k + 1) * LANES] = res[k].T.astype(BF16)
         pack(dot(hot.astype(BF16), field16[...]), over_rows(extra, subs), send, 0)
 
@@ -278,7 +281,8 @@
 
     def half_first(place, spread, maps, over_maps, res, inverse, *refs):
         pieces, refs = refs[:RING], refs[RING:]
-        first_out, inner, out, over_add, turned, buffer, sems, tiles = refs
+        first_out, inner, both, turned, buffer, sems, tiles = refs
+        out = both.at[:, : (own + over) * comps]
         copies = loads(inverse, 0, buffer, sems)
         for step, piece in enumerate(pieces):
             member = place[0, 2] + step
@@ -290,7 +294,7 @@
 
         everything = tiles[...]
         values = spread[...] + prolong_maps(everything, maps, at_own)
-        over_add[...] = prolong_maps(everything, over_maps, 0)
+        both[:, (own + over) * comps :] = prolong_maps(everything, over_maps, 0)
         rf = jnp.zeros((rhs, own), F32)
         ff = jnp.zeros((rhs, own), F32)
         for k in range(comps):
@@ -304,14 +308,15 @@
         product(copies, turned, buffer, None, out)
 
     def solve(got, part, maps, inverse, *refs):
-        extra, (out, turned, buffer, sems) = refs[:-4], refs[-4:]
+        out, turned, buffer, sems = refs
+        size = out.shape[1]
         copies = loads(inverse, 1, buffer, sems)
         arrived = dot(maps[at_take : at_take + over, :], got[:, :lanes])
-        for each_extra in extra:
-            arrived += each_extra[...]
+        if part.shape[1] > size:
+            arrived += part[:, size:]
         for k in range(comps):
             turned[:, k * LANES : (k + 1) * LANES] = tile(arrived, k).T.astype(BF16)
-        product(copies, turned, buffer, part, out)
+        product(copies, turned, buffer, part.at[:, :size], out)
 
     def finish_first(got, total, parts, maps, send, res_own, over_maps, sol, token, own16, over16):
         token[...] = jnp.zeros((ROWS, LANES), F32)
@@ -371,12 +376,15 @@
         summed, tiles = group_total(parts)
         each = main * ROWS
         inner = summed[each : each + 2] + summed[each + 2 : each + 4]
+        low = inner - inner.astype(BF16).astype(F32)
+        rest = low[0:1] - inner[0:1] / (inner[1:2] + EPSILON) * low[1:2]
         small = iota((ROWS, LANES), 0)
         for t in range(main):
             value = tiles[t]
             if t == aux:
                 value = jnp.where(small == cl_dev, inner[0:1], value)
                 value = jnp.where(small == cl_dev + 1, inner[1:2], value)
+                value = jnp.where(small == cl_dev + 2, rest, value)
             send[:, lanes + t * LANES : lanes + (t + 1) * LANES] = repeat_rows(value, subs).astype(BF16)
 
     def prolong_maps(tiles, maps, base):
@@ -400,7 +408,7 @@
         applied += prolong_maps(got[:, lanes:], maps, at_own)
         sums = got[:, lanes + aux * LANES :].astype(F32).reshape(subs, ROWS, LANES)
         sums = jnp.sum(sums, axis=0)
-        scale = sums[cl_dev : cl_dev + 1] / (sums[cl_dev + 1 : cl_dev + 2] + EPSILON)
+        scale = (sums[cl_dev : cl_dev + 1] + sums[cl_dev + 2 : cl_dev + 3]) / (sums[cl_dev + 1 : cl_dev + 2] + EPSILON)
         for k in range(comps):
             out[k] = first[k] - (scale * tile(applied, k)).T
 
@@ -462,7 +470,7 @@
         )[0]
         return exchange(parts, "group")
 
-    def solve(got, part, *extra):
+    def solve(got, part):
         return kernel_call(
             m["solve"],
             [((rhs, width), F32)],
@@ -470,8 +478,7 @@
             part,
             maps,
             inverse,
-            *extra,
-            in_specs=[here, here, here, hbm] + [here] * len(extra),
+            in_specs=[here, here, here, hbm],
             scratch_shapes=half_scratch,
             limit=48,
             **half_cost,
@@ -493,7 +500,7 @@
                 vmem((1, over), jnp.int32),
                 vmem((1, over), jnp.int32),
                 vmem((own, lanes), BF16),
-                pltpu.SemaphoreType.DMA((4,)),
+                pltpu.SemaphoreType.DMA((6,)),
             ],
         )
     with jax.named_scope("maps"):
@@ -589,9 +596,9 @@
         for step in range(1, RING):
             turn = [(i, i // RING * RING + (i - step) % RING) for i in range(subs)]
             pieces_x.append(lax.ppermute(third, "sub", turn))
-        first, inner, part, over_add = kernel_call(
+        first, inner, part = kernel_call(
             m["half_first"],
-            [((comps, rhs, own), F32), ((2, LANES), F32), ((rhs, width), F32), ((over, lanes), F32)],
+            [((comps, rhs, own), F32), ((2, LANES), F32), ((rhs, width + lanes), F32)],
             place,
             spread,
             maps,
@@ -609,7 +616,7 @@
     with jax.named_scope("coarse_second"):
         parts = coarse_parts(matrix_late, got, each + 16, [inner])
     with jax.named_scope("solve_second"):
-        total = solve(got, part, over_add)
+        total = solve(got, part)
     with jax.named_scope("return_second"):
         send, res_own = kernel_call(
             m["finish_second"],

time: 190 us -> 189 us (level)
    unnamed x40 -> x36, local copies, waits for them, and re-layouts: 11.8 us -> 10.3 us
  transfers between devices with their start and end apart: 12 -> 12, of which waited for: 8 -> 9; matrix products, arithmetic and copies ran while one was open for 1% -> 1% of each run, Pallas kernels for 10% -> 10%
where the time goes in v5:
time: 189 us; the launch traced here: 188 us
  blocking collectives  68.6 us (36%)
  starting transfers between devices  42.5 us (22%)
  waiting for transfers between devices  35.6 us (19%)
  Pallas kernels  28.7 us (15%)
  local copies, waits for them, and re-layouts  11.5 us (6%)
    all_to_all x2, blocking collectives, exchange(): return lax.all_to_all(values, axis, split_axis=0, concat_axis=0, tiled=True)  68.6 us
    all_to_all x5, starting transfers between devices, exchange(): return lax.all_to_all(values, axis, split_axis=0, concat_axis=0, tiled=True)  32.5 us
    pallas_call x16, Pallas kernels, kernel_call(): pl.pallas_call(lambda *refs: body(*refs[count:]), out_shape=[jax.ShapeDty...  28.7 us
    all_to_all x5, waiting for transfers between devices, exchange(): return lax.all_to_all(values, axis, split_axis=0, concat_axis=0, tiled=True)  19.9 us
    unnamed x36, local copies, waits for them, and re-layouts  10.3 us
    ppermute x3, waiting for transfers between devices, body(): pieces_x.append(lax.ppermute(third, 'sub', turn))  10.2 us
    ppermute x3, waiting for transfers between devices, pass_round(): lax.ppermute(piece, 'group', [(i, (i - 2 * step) % groups) for i in range...  5.54 us
    ppermute x3, starting transfers between devices, pass_round(): lax.ppermute(piece, 'group', [(i, (i - 2 * step) % groups) for i in range...  5.16 us
  transfers between devices with their start and end apart: 12, of which 9 were waited for; matrix products, arithmetic and copies ran while one was open for 1% of the time, Pallas kernels for 10%

profile of v5, /device:TPU:10, one launch (start us, length us, event | category | flops | bytes accessed | tf_op | source)
XLA Modules:
  0.0 188.0 jit_solution(14012477193730358618)
XLA Ops:
  0.6 2.5 %begin.1 = (bf16[256,768]{1,0:T(8,128)(2,1)}, f32[8,128]{1,0:T(8,128)}) custom-call(f32[9,128,128]{2,1,0:T(8,128)} %bitcast.29, s32[1,128]{1,0:T(1,128)} %bitcast.42, s32[1,128]{1,0:T(1,128)} %bitcast.45, s32[1,128]{1,0:T(1,128)} %bitcast.53), custom_call_target="tpu_custom_call" | custom-call | tf_op jit(solution)/shard_map/begin/pallas_call | solution.py:51
  3.2 11.6 %all-to-all-start = ((bf16[32,8,768]{2,1,0:T(8,128)(2,1)}), bf16[32,8,768]{2,1,0:T(8,128)(2,1)S(1)}, u32[]{:S(2)}, u32[]{:S(2)}) async-start(bf16[32,8,768]{2,1,0:T(8,128)(2,1)} %bitcast.52), calls=%async_computation | async-start | bytes 786432 | tf_op jit(solution)/shard_map/answer/all_to_all | solution.py:23
  15.6 3.9 %regroup.2 = (bf16[4,48,1536]{2,1,0:T(8,128)(2,1)S(1)}, bf16[4,48,1536]{2,1,0:T(8,128)(2,1)}) custom-call(f32[8,128]{1,0:T(8,128)S(1)} %copy-done.15, s32[1,3]{1,0:T(1,128)S(1)} %add_bitcast_fusion.refs_1_, bf16[45,11520]{1,0:T(8,128)(2,1)S(1)} %copy-done.17), custom_call_target="tpu_custom_call" | custom-call | flops 1811939328 | tf_op jit(solution)/shard_map/regroup/pallas_call | solution.py:51
  19.8 9.0 %all-to-all-done = bf16[32,8,768]{2,1,0:T(8,128)(2,1)S(1)} async-done(((bf16[32,8,768]{2,1,0:T(8,128)(2,1)}), bf16[32,8,768]{2,1,0:T(8,128)(2,1)S(1)}, u32[]{:S(2)}, u32[]{:S(2)}) %all-to-all-start) | async-done | bytes 393248 | tf_op jit(solution)/shard_map/answer/all_to_all | solution.py:23
  30.2 5.6 %all-to-all-start.1 = ((bf16[32,8,1920]{2,1,0:T(8,128)(2,1)}), bf16[32,8,1920]{2,1,0:T(8,128)(2,1)S(1)}, u32[]{:S(2)}, u32[]{:S(2)}) async-start(bf16[32,8,1920]{2,1,0:T(8,128)(2,1)} %bitcast.6), calls=%async_computation.1 | async-start | bytes 1966080 | tf_op jit(solution)/shard_map/all_to_all | solution.py:23
  37.6 2.7 %collective-permute-start.2 = (bf16[2,48,1536]{2,1,0:T(8,128)(2,1)S(1)}, bf16[2,48,1536]{2,1,0:T(8,128)(2,1)S(1)}, u32[]{:S(2)}, u32[]{:S(2)}) collective-permute-start(bf16[2,48,1536]{2,1,0:T(8,128)(2,1)S(1)} %pad_maximum_fusion.1), channel_id=1, source_target_pairs={{0,128},{32,160},{64,192},{96,224},{128,0},{160,32},{192,64},{224,... | collective-permute-start | bytes 884744 | tf_op jit(solution)/shard_map/regroup/ppermute | solution.py:430
  40.3 2.0 %collective-permute-start.3 = (bf16[2,48,1536]{2,1,0:T(8,128)(2,1)S(1)}, bf16[2,48,1536]{2,1,0:T(8,128)(2,1)S(1)}, u32[]{:S(2)}, u32[]{:S(2)}) collective-permute-start(bf16[2,48,1536]{2,1,0:T(8,128)(2,1)S(1)} %pad_maximum_fusion.2), channel_id=1, source_target_pairs={{0,64},{32,96},{64,128},{96,160},{128,192},{160,224},{192,0},{224,... | collective-permute-start | bytes 884744 | tf_op jit(solution)/shard_map/regroup/ppermute | solution.py:430
  43.1 3.1 %own_half_first.1 = (f32[128,2304]{1,0:T(8,128)S(1)}, f32[8,128]{1,0:T(8,128)S(1)}) custom-call(f32[8,128]{1,0:T(8,128)S(1)} %get-tuple-element.34.refs_0_, f32[9,128,128]{2,1,0:T(8,128)S(1)} %bitcast.31, bf16[9,2,128,2304]{3,2,1,0:T(8,128)(2,1)} %bitcast.47), custom_call_target="tpu_custom_call" | custom-call | flops 679477248 | bytes 5308416 | tf_op jit(solution)/shard_map/own_half_first/pallas_call | solution.py:51
  47.2 4.6 %collective-permute-done.2.refs_5_ = bf16[2,48,1536]{2,1,0:T(8,128)(2,1)S(1)} collective-permute-done((bf16[2,48,1536]{2,1,0:T(8,128)(2,1)S(1)}, bf16[2,48,1536]{2,1,0:T(8,128)(2,1)S(1)}, u32[]{:S(2)}, u32[]{:S(2)}) %collective-permute-start.2) | collective-permute-done | bytes 294944 | tf_op jit(solution)/shard_map/regroup/ppermute | solution.py:430
  54.5 7.1 %all-to-all-done.1 = bf16[32,8,1920]{2,1,0:T(8,128)(2,1)S(1)} async-done(((bf16[32,8,1920]{2,1,0:T(8,128)(2,1)}), bf16[32,8,1920]{2,1,0:T(8,128)(2,1)S(1)}, u32[]{:S(2)}, u32[]{:S(2)}) %all-to-all-start.1) | async-done | bytes 983072 | tf_op jit(solution)/shard_map/all_to_all | solution.py:23
  62.7 4.9 %all-to-all-start.2 = ((bf16[8,48,128]{2,1,0:T(8,128)(2,1)}), bf16[8,48,128]{2,1,0:T(8,128)(2,1)S(1)}, u32[]{:S(2)}, u32[]{:S(2)}) async-start(bf16[8,48,128]{2,1,0:T(8,128)(2,1)} %coarse_first.1), calls=%async_computation.2 | async-start | bytes 196608 | tf_op jit(solution)/shard_map/coarse_first/all_to_all | solution.py:23
  68.9 3.2 %solve_first.1.refs_1_ = f32[128,2304]{1,0:T(8,128)S(1)} custom-call(bf16[256,1920]{1,0:T(8,128)(2,1)S(1)} %bitcast.27, f32[128,2304]{1,0:T(8,128)S(1)} %copy-done.4, bf16[1024,256]{1,0:T(8,128)(2,1)S(1)} %get-tuple-element.36.refs_2_.refs_3_.refs_4_, bf16[9,2,128,2304]{3,2,1,0:T(8,128)(2,1)} %bitcast.48), custom_call_target="tpu_custom_call" | custom-call | flops 679477248 | bytes 5308416 | tf_op jit(solution)/shard_map/solve_first/pallas_call | solution.py:51
  73.1 35.7 %all_to_all.35 = bf16[32,8,2176]{2,1,0:T(8,128)(2,1)S(1)} all-to-all(bf16[32,8,2176]{2,1,0:T(8,128)(2,1)S(1)} %bitcast.39), channel_id=1, replica_groups=mesh['group'=8,'sub'=32] {'sub'}, dimensions={0} | all-to-all | bytes 2228224 | tf_op jit(solution)/shard_map/return_first/all_to_all | solution.py:23
  111.1 5.6 %all-to-all-start.4 = ((bf16[32,8,1920]{2,1,0:T(8,128)(2,1)}), bf16[32,8,1920]{2,1,0:T(8,128)(2,1)S(1)}, u32[]{:S(2)}, u32[]{:S(2)}) async-start(bf16[32,8,1920]{2,1,0:T(8,128)(2,1)} %bitcast.18), calls=%async_computation.4 | async-start | bytes 1966080 | tf_op jit(solution)/shard_map/all_to_all | solution.py:23
  116.7 1.5 collective-permute-start.6
  119.2 2.3 %collective-permute-start.4 = (bf16[256,256]{1,0:T(8,128)(2,1)S(1)}, bf16[256,256]{1,0:T(8,128)(2,1)S(1)}, u32[]{:S(2)}, u32[]{:S(2)}) collective-permute-start(bf16[256,256]{1,0:T(8,128)(2,1)S(1)} %get-tuple-element.49.refs_7_), channel_id=1, source_target_pairs={{0,3},{1,0},{2,1},{3,2},{4,7},{5,4},{6,5},{7,6},{8,11},{9,8},{10,9... | collective-permute-start | bytes 393224 | tf_op jit(solution)/shard_map/own_half_second/ppermute | solution.py:598
  121.5 3.9 %collective-permute-done.6.refs_10_ = bf16[256,256]{1,0:T(8,128)(2,1)S(1)} collective-permute-done((bf16[256,256]{1,0:T(8,128)(2,1)S(1)}, bf16[256,256]{1,0:T(8,128)(2,1)S(1)}, u32[]{:S(2)}, u32[]{:S(2)}) %collective-permute-start.6) | collective-permute-done | bytes 131104 | tf_op jit(solution)/shard_map/own_half_second/ppermute | solution.py:598
  125.4 3.7 %collective-permute-done.5.refs_9_ = bf16[256,256]{1,0:T(8,128)(2,1)S(1)} collective-permute-done((bf16[256,256]{1,0:T(8,128)(2,1)S(1)}, bf16[256,256]{1,0:T(8,128)(2,1)S(1)}, u32[]{:S(2)}, u32[]{:S(2)}) %collective-permute-start.5) | collective-permute-done | bytes 131104 | tf_op jit(solution)/shard_map/own_half_second/ppermute | solution.py:598
  129.1 2.6 %collective-permute-done.4.refs_8_ = bf16[256,256]{1,0:T(8,128)(2,1)S(1)} collective-permute-done((bf16[256,256]{1,0:T(8,128)(2,1)S(1)}, bf16[256,256]{1,0:T(8,128)(2,1)S(1)}, u32[]{:S(2)}, u32[]{:S(2)}) %collective-permute-start.4) | collective-permute-done | bytes 131104 | tf_op jit(solution)/shard_map/own_half_second/ppermute | solution.py:598
  133.7 3.9 %own_half_second.1 = (f32[9,128,128]{2,1,0:T(8,128)}, f32[2,128]{1,0:T(2,128)S(1)}, f32[128,3456]{1,0:T(8,128)S(1)}) custom-call(f32[8,128]{1,0:T(8,128)S(1)} %get-tuple-element.46.refs_0_, s32[1,3]{1,0:T(1,128)S(1)} %add_bitcast_fusion.refs_1_, f32[128,1152]{1,0:T(8,128)S(1)} %copy-done.8, bf16[1024,256]{1,0:T(8,128)(2,1)S(1)} %get-tuple-element.36.refs_2_.refs_3_.refs_4_, ...), custom_call_target="tpu_custom_call" | custom-call | flops 679477248 | bytes 5308416 | tf_op jit(solution)/shard_map/own_half_second/pallas_call | solution.py:51
  138.9 3.7 %all-to-all-done.4 = bf16[32,8,1920]{2,1,0:T(8,128)(2,1)S(1)} async-done(((bf16[32,8,1920]{2,1,0:T(8,128)(2,1)}), bf16[32,8,1920]{2,1,0:T(8,128)(2,1)S(1)}, u32[]{:S(2)}, u32[]{:S(2)}) %all-to-all-start.4) | async-done | bytes 983072 | tf_op jit(solution)/shard_map/all_to_all | solution.py:23
  143.7 4.8 %all-to-all-start.5 = ((bf16[8,64,128]{2,1,0:T(8,128)(2,1)}), bf16[8,64,128]{2,1,0:T(8,128)(2,1)S(1)}, u32[]{:S(2)}, u32[]{:S(2)}) async-start(bf16[8,64,128]{2,1,0:T(8,128)(2,1)} %coarse_second.1), calls=%async_computation.5 | async-start | bytes 262144 | tf_op jit(solution)/shard_map/coarse_second/all_to_all | solution.py:23
  150.0 3.1 %solve_second.1.refs_0_ = f32[128,2304]{1,0:T(8,128)S(1)} custom-call(bf16[256,1920]{1,0:T(8,128)(2,1)S(1)} %bitcast.34, f32[128,3456]{1,0:T(8,128)S(1)} %copy-done.2, bf16[1024,256]{1,0:T(8,128)(2,1)S(1)} %get-tuple-element.36.refs_2_.refs_3_.refs_4_, bf16[9,2,128,2304]{3,2,1,0:T(8,128)(2,1)} %bitcast.50), custom_call_target="tpu_custom_call" | custom-call | flops 679477248 | bytes 5308416 | tf_op jit(solution)/shard_map/solve_second/pallas_call | solution.py:51
  153.7 32.9 %all_to_all.36 = bf16[32,8,1920]{2,1,0:T(8,128)(2,1)S(1)} all-to-all(bf16[32,8,1920]{2,1,0:T(8,128)(2,1)S(1)} %bitcast.40), channel_id=1, replica_groups=mesh['group'=8,'sub'=32] {'sub'}, dimensions={0} | all-to-all | bytes 1966080 | tf_op jit(solution)/shard_map/return_second/all_to_all | solution.py:23
  (60 shorter events, 23.2 us)
Async XLA Ops:
  0.6 14.3 %copy-start.17 = (bf16[45,11520]{1,0:T(8,128)(2,1)S(1)}, bf16[45,11520]{1,0:T(8,128)(2,1)}, u32[]{:S(2)}) copy-start(bf16[45,11520]{1,0:T(8,128)(2,1)} %refs_2_.1) | copy-start | bytes 3110404
  3.2 25.7 %all-to-all-start = ((bf16[32,8,768]{2,1,0:T(8,128)(2,1)}), bf16[32,8,768]{2,1,0:T(8,128)(2,1)S(1)}, u32[]{:S(2)}, u32[]{:S(2)}) async-start(bf16[32,8,768]{2,1,0:T(8,128)(2,1)} %bitcast.52), calls=%async_computation | async-start | bytes 786432 | tf_op jit(solution)/shard_map/answer/all_to_all | solution.py:23
  15.6 3.9 %copy-start = (f32[128,9,128]{2,0,1:T(8,128)S(1)}, f32[128,9,128]{2,0,1:T(8,128)}, u32[]{:S(2)}) copy-start(f32[128,9,128]{2,0,1:T(8,128)} %param.6) | copy-start | bytes 1769476
  15.6 3.9 %copy-start.14 = (s32[128]{0:T(128)S(1)}, s32[128]{0:T(128)}, u32[]{:S(2)}) copy-start(s32[128]{0:T(128)} %param.9) | copy-start | bytes 1540
  15.6 3.9 %copy-start.16 = (s32[128,1]{0,1:T(1,128)S(1)}, s32[128,1]{0,1:T(1,128)}, u32[]{:S(2)}) copy-start(s32[128,1]{0,1:T(1,128)} %param.10) | copy-start | bytes 1540
  19.5 16.3 %collective-permute-start = (bf16[4,48,1536]{2,1,0:T(8,128)(2,1)}, bf16[4,48,1536]{2,1,0:T(8,128)(2,1)}, u32[]{:S(2)}, u32[]{:S(2)}) collective-permute-start(bf16[4,48,1536]{2,1,0:T(8,128)(2,1)} %get-tuple-element.40), channel_id=1, source_target_pairs={{0,32},{32,0},{64,96},{96,64},{128,160},{160,128},{192,224},{224,1... | collective-permute-start | bytes 1769480 | tf_op jit(solution)/shard_map/regroup/ppermute | solution.py:426
  30.2 31.5 %all-to-all-start.1 = ((bf16[32,8,1920]{2,1,0:T(8,128)(2,1)}), bf16[32,8,1920]{2,1,0:T(8,128)(2,1)S(1)}, u32[]{:S(2)}, u32[]{:S(2)}) async-start(bf16[32,8,1920]{2,1,0:T(8,128)(2,1)} %bitcast.6), calls=%async_computation.1 | async-start | bytes 1966080 | tf_op jit(solution)/shard_map/all_to_all | solution.py:23
  37.0 10.2 %collective-permute-start.1 = (bf16[2,48,1536]{2,1,0:T(8,128)(2,1)S(1)}, bf16[2,48,1536]{2,1,0:T(8,128)(2,1)S(1)}, u32[]{:S(2)}, u32[]{:S(2)}) collective-permute-start(bf16[2,48,1536]{2,1,0:T(8,128)(2,1)S(1)} %pad_maximum_fusion), channel_id=1, source_target_pairs={{0,192},{32,224},{64,0},{96,32},{128,64},{160,96},{192,128},{224,1... | collective-permute-start | bytes 884744 | tf_op jit(solution)/shard_map/regroup/ppermute | solution.py:430
  37.6 14.3 %collective-permute-start.2 = (bf16[2,48,1536]{2,1,0:T(8,128)(2,1)S(1)}, bf16[2,48,1536]{2,1,0:T(8,128)(2,1)S(1)}, u32[]{:S(2)}, u32[]{:S(2)}) collective-permute-start(bf16[2,48,1536]{2,1,0:T(8,128)(2,1)S(1)} %pad_maximum_fusion.1), channel_id=1, source_target_pairs={{0,128},{32,160},{64,192},{96,224},{128,0},{160,32},{192,64},{224,... | collective-permute-start | bytes 884744 | tf_op jit(solution)/shard_map/regroup/ppermute | solution.py:430
  40.3 12.5 %collective-permute-start.3 = (bf16[2,48,1536]{2,1,0:T(8,128)(2,1)S(1)}, bf16[2,48,1536]{2,1,0:T(8,128)(2,1)S(1)}, u32[]{:S(2)}, u32[]{:S(2)}) collective-permute-start(bf16[2,48,1536]{2,1,0:T(8,128)(2,1)S(1)} %pad_maximum_fusion.2), channel_id=1, source_target_pairs={{0,64},{32,96},{64,128},{96,160},{128,192},{160,224},{192,0},{224,... | collective-permute-start | bytes 884744 | tf_op jit(solution)/shard_map/regroup/ppermute | solution.py:430
  62.7 9.4 %all-to-all-start.2 = ((bf16[8,48,128]{2,1,0:T(8,128)(2,1)}), bf16[8,48,128]{2,1,0:T(8,128)(2,1)S(1)}, u32[]{:S(2)}, u32[]{:S(2)}) async-start(bf16[8,48,128]{2,1,0:T(8,128)(2,1)} %coarse_first.1), calls=%async_computation.2 | async-start | bytes 196608 | tf_op jit(solution)/shard_map/coarse_first/all_to_all | solution.py:23
  67.6 1.3 copy-start.4
  73.1 37.2 %copy-start.10 = (bf16[640,256]{1,0:T(8,128)(2,1)}, bf16[640,256]{1,0:T(8,128)(2,1)S(1)}, u32[]{:S(2)}) copy-start(bf16[640,256]{1,0:T(8,128)(2,1)S(1)} %get-tuple-element.48.refs_4_) | copy-start | bytes 983044
  73.1 35.8 %copy-start.13 = (bf16[384,256]{1,0:T(8,128)(2,1)S(1)}, bf16[384,256]{1,0:T(8,128)(2,1)}, u32[]{:S(2)}) copy-start(bf16[384,256]{1,0:T(8,128)(2,1)} %copy-done.12) | copy-start | bytes 589828
  111.1 31.5 %all-to-all-start.4 = ((bf16[32,8,1920]{2,1,0:T(8,128)(2,1)}), bf16[32,8,1920]{2,1,0:T(8,128)(2,1)S(1)}, u32[]{:S(2)}, u32[]{:S(2)}) async-start(bf16[32,8,1920]{2,1,0:T(8,128)(2,1)} %bitcast.18), calls=%async_computation.4 | async-start | bytes 1966080 | tf_op jit(solution)/shard_map/all_to_all | solution.py:23
  116.7 8.7 %collective-permute-start.6 = (bf16[256,256]{1,0:T(8,128)(2,1)S(1)}, bf16[256,256]{1,0:T(8,128)(2,1)S(1)}, u32[]{:S(2)}, u32[]{:S(2)}) collective-permute-start(bf16[256,256]{1,0:T(8,128)(2,1)S(1)} %get-tuple-element.49.refs_7_), channel_id=1, source_target_pairs={{0,1},{1,2},{2,3},{3,0},{4,5},{5,6},{6,7},{7,4},{8,9},{9,10},{10,1... | collective-permute-start | bytes 393224 | tf_op jit(solution)/shard_map/own_half_second/ppermute | solution.py:598
  118.3 10.8 %collective-permute-start.5 = (bf16[256,256]{1,0:T(8,128)(2,1)S(1)}, bf16[256,256]{1,0:T(8,128)(2,1)S(1)}, u32[]{:S(2)}, u32[]{:S(2)}) collective-permute-start(bf16[256,256]{1,0:T(8,128)(2,1)S(1)} %get-tuple-element.49.refs_7_), channel_id=1, source_target_pairs={{0,2},{1,3},{2,0},{3,1},{4,6},{5,7},{6,4},{7,5},{8,10},{9,11},{10,... | collective-permute-start | bytes 393224 | tf_op jit(solution)/shard_map/own_half_second/ppermute | solution.py:598
  119.2 12.5 %collective-permute-start.4 = (bf16[256,256]{1,0:T(8,128)(2,1)S(1)}, bf16[256,256]{1,0:T(8,128)(2,1)S(1)}, u32[]{:S(2)}, u32[]{:S(2)}) collective-permute-start(bf16[256,256]{1,0:T(8,128)(2,1)S(1)} %get-tuple-element.49.refs_7_), channel_id=1, source_target_pairs={{0,3},{1,0},{2,1},{3,2},{4,7},{5,4},{6,5},{7,6},{8,11},{9,8},{10,9... | collective-permute-start | bytes 393224 | tf_op jit(solution)/shard_map/own_half_second/ppermute | solution.py:598
  131.7 1.1 copy-start.8
  133.7 8.9 %copy-start.6 = (bf16[8,48,1536]{2,1,0:T(8,128)(2,1)S(1)}, bf16[8,48,1536]{2,1,0:T(8,128)(2,1)}, u32[]{:S(2)}) copy-start(bf16[8,48,1536]{2,1,0:T(8,128)(2,1)} %copy-done.5) | copy-start | bytes 3538948
  137.7 1.2 copy-start.1
  143.7 9.5 %all-to-all-start.5 = ((bf16[8,64,128]{2,1,0:T(8,128)(2,1)}), bf16[8,64,128]{2,1,0:T(8,128)(2,1)S(1)}, u32[]{:S(2)}, u32[]{:S(2)}) async-start(bf16[8,64,128]{2,1,0:T(8,128)(2,1)} %coarse_second.1), calls=%async_computation.5 | async-start | bytes 262144 | tf_op jit(solution)/shard_map/coarse_second/all_to_all | solution.py:23
  148.5 1.5 copy-start.2
  153.7 32.9 %copy-start.9 = (f32[9,128,128]{2,1,0:T(8,128)S(1)}, f32[9,128,128]{2,1,0:T(8,128)}, u32[]{:S(2)}) copy-start(f32[9,128,128]{2,1,0:T(8,128)} %get-tuple-element.50.refs_2_) | copy-start | bytes 1769476
  (6 other events, 5.2 us)

commit v6 on v5

--- a/solution.py
+++ b/solution.py
@@ -272,16 +272,19 @@
             else:
                 out[...] = part[...] + value
 
-    def half(res, inverse, out, token, turned, buffer, sems):
+    def half(res, inverse, far, token, turned, buffer, sems, out, far_sem):
         token[...] = jnp.zeros((ROWS, LANES), F32)
         copies = loads(inverse, 0, buffer, sems)
         for k in range(comps):
             turned[:, k * LANES : (k + 1) * LANES] = res[k].astype(BF16)
         product(copies, turned, buffer, None, out)
+        put = pltpu.make_async_copy(out, far.at[0], far_sem)
+        put.start()
+        put.wait()
 
     def half_first(place, spread, maps, over_maps, res, inverse, *refs):
         pieces, refs = refs[:RING], refs[RING:]
-        first_out, inner, both, turned, buffer, sems, tiles = refs
+        first_out, inner, far, turned, buffer, sems, both, far_sem, tiles = refs
         out = both.at[:, : (own + over) * comps]
         copies = loads(inverse, 0, buffer, sems)
         for step, piece in enumerate(pieces):
@@ -306,17 +309,29 @@
         inner[0:1, :] = jnp.sum(rf.T, axis=0, keepdims=True)
         inner[1:2, :] = jnp.sum(ff.T, axis=0, keepdims=True)
         product(copies, turned, buffer, None, out)
+        put = pltpu.make_async_copy(both, far.at[0], far_sem)
+        put.start()
+        put.wait()
 
     def solve(got, part, maps, inverse, *refs):
-        out, turned, buffer, sems = refs
+        out, turned, buffer, sems, kept, kept_sems = refs
         size = out.shape[1]
+        rest = kept.shape[1] - size
+        if rest:
+            bring_rest = pltpu.make_async_copy(part.at[0, :, pl.ds(size, rest)], kept.at[:, pl.ds(size, rest)], kept_sems.at[1])
+            bring_rest.start()
         copies = loads(inverse, 1, buffer, sems)
+        bring = pltpu.make_async_copy(part.at[0, :, pl.ds(0, size)], kept.at[:, pl.ds(0, size)], kept_sems.at[0])
+        bring.start()
         arrived = dot(maps[at_take : at_take + over, :], got[:, :lanes])
-        if part.shape[1] > size:
-            arrived += part[:, size:]
+        if rest:
+            bring_rest.wait()
+            arrived += kept[:, size:]
         for k in range(comps):
             turned[:, k * LANES : (k + 1) * LANES] = tile(arrived, k).T.astype(BF16)
-        product(copies, turned, buffer, part.at[:, :size], out)
+        product(copies, turned, buffer, None, out)
+        bring.wait()
+        out[...] += kept[:, :size]
 
     def finish_first(got, total, parts, maps, send, res_own, over_maps, sol, token, own16, over16):
         token[...] = jnp.zeros((ROWS, LANES), F32)
@@ -450,6 +465,8 @@
     vmem = pltpu.VMEM
     half_cost = dict(flops=rhs * width * width, moved=width * width)
     mark = ((ROWS, LANES), F32)
+    spare = 16
+    far = pl.BlockSpec(memory_space=pl.ANY)
     half_scratch = [
         vmem((rhs, lanes), BF16),
         vmem((comps, own, width), BF16),
@@ -478,8 +495,8 @@
             part,
             maps,
             inverse,
-            in_specs=[here, here, here, hbm],
-            scratch_shapes=half_scratch,
+            in_specs=[here, far, here, hbm],
+            scratch_shapes=half_scratch + [vmem(part.shape[1:], F32), pltpu.SemaphoreType.DMA((2,))],
             limit=48,
             **half_cost,
         )[0]
@@ -540,12 +557,13 @@
     with jax.named_scope("own_half_first"):
         part, half_token = kernel_call(
             m["half"],
-            [((rhs, width), F32), mark],
+            [((spare, rhs, width), F32), mark],
             residual,
             inverse,
             after=[token],
             in_specs=[here, hbm],
-            scratch_shapes=half_scratch,
+            out_specs=[far, here],
+            scratch_shapes=half_scratch + [vmem((rhs, width), F32), pltpu.SemaphoreType.DMA],
             **half_cost,
         )
     with jax.named_scope("regroup"):
@@ -598,7 +616,8 @@
             pieces_x.append(lax.ppermute(third, "sub", turn))
         first, inner, part = kernel_call(
             m["half_first"],
-            [((comps, rhs, own), F32), ((2, LANES), F32), ((rhs, width + lanes), F32)],
+            [((comps, rhs, own), F32), ((2, LANES), F32), ((spare, rhs, width + lanes), F32)],
+
             place,
             spread,
             maps,
@@ -608,7 +627,9 @@
             *pieces_x,
             after=[token],
             in_specs=[pl.BlockSpec(memory_space=pltpu.SMEM)] + [here] * 4 + [hbm] + [here] * RING,
-            scratch_shapes=half_scratch + [vmem((slots, block), BF16)],
+            out_specs=[here, here, far],
+            scratch_shapes=half_scratch
+            + [vmem((rhs, width + lanes), F32), pltpu.SemaphoreType.DMA, vmem((slots, block), BF16)],
             limit=48,
             **half_cost,
         )

time: 189 us -> 189 us (level)
  local copies, waits for them, and re-layouts: 11.5 us -> 6.52 us
  Pallas kernels: 28.7 us -> 32.8 us
    unnamed x36 -> x28, local copies, waits for them, and re-layouts: 10.3 us -> 5.32 us
    pallas_call x16, Pallas kernels: 28.7 us -> 32.8 us  [kernel_call(): pl.pallas_call(lambda *refs: body(*refs[count:]), out_shape=[jax.ShapeDty...]
  transfers between devices with their start and end apart: 12 -> 12, of which waited for: 9 -> 10; matrix products, arithmetic and copies ran while one was open for 1% -> 1% of each run, Pallas kernels for 10% -> 13%
where the time goes in v6:
time: 189 us; the launch traced here: 187 us
  blocking collectives  68.2 us (36%)
  starting transfers between devices  42.5 us (22%)
  waiting for transfers between devices  36.3 us (19%)
  Pallas kernels  32.8 us (17%)
  local copies, waits for them, and re-layouts  6.52 us (3%)
    all_to_all x2, blocking collectives, exchange(): return lax.all_to_all(values, axis, split_axis=0, concat_axis=0, tiled=True)  68.2 us
    pallas_call x16, Pallas kernels, kernel_call(): pl.pallas_call(lambda *refs: body(*refs[count:]), out_shape=[jax.ShapeDty...  32.8 us
    all_to_all x5, starting transfers between devices, exchange(): return lax.all_to_all(values, axis, split_axis=0, concat_axis=0, tiled=True)  32.5 us
    all_to_all x5, waiting for transfers between devices, exchange(): return lax.all_to_all(values, axis, split_axis=0, concat_axis=0, tiled=True)  20.4 us
    ppermute x3, waiting for transfers between devices, body(): pieces_x.append(lax.ppermute(third, 'sub', turn))  10.3 us
    ppermute x3, waiting for transfers between devices, pass_round(): lax.ppermute(piece, 'group', [(i, (i - 2 * step) % groups) for i in range...  5.54 us
    unnamed x28, local copies, waits for them, and re-layouts  5.32 us
    ppermute x3, starting transfers between devices, pass_round(): lax.ppermute(piece, 'group', [(i, (i - 2 * step) % groups) for i in range...  5.16 us
  transfers between devices with their start and end apart: 12, of which 10 were waited for; matrix products, arithmetic and copies ran while one was open for 1% of the time, Pallas kernels for 13%

profile of v6, /device:TPU:10, one launch (start us, length us, event | category | flops | bytes accessed | tf_op | source)
XLA Modules:
  0.0 187.4 jit_solution(15823799549794543917)
XLA Ops:
  0.6 2.5 %begin.1 = (bf16[256,768]{1,0:T(8,128)(2,1)}, f32[8,128]{1,0:T(8,128)}) custom-call(f32[9,128,128]{2,1,0:T(8,128)} %bitcast.29, s32[1,128]{1,0:T(1,128)} %bitcast.42, s32[1,128]{1,0:T(1,128)} %bitcast.45, s32[1,128]{1,0:T(1,128)} %bitcast.53), custom_call_target="tpu_custom_call" | custom-call | tf_op jit(solution)/shard_map/begin/pallas_call | solution.py:51
  3.2 11.6 %all-to-all-start = ((bf16[32,8,768]{2,1,0:T(8,128)(2,1)}), bf16[32,8,768]{2,1,0:T(8,128)(2,1)S(1)}, u32[]{:S(2)}, u32[]{:S(2)}) async-start(bf16[32,8,768]{2,1,0:T(8,128)(2,1)} %bitcast.52), calls=%async_computation | async-start | bytes 786432 | tf_op jit(solution)/shard_map/answer/all_to_all | solution.py:23
  15.6 3.9 %regroup.2 = (bf16[4,48,1536]{2,1,0:T(8,128)(2,1)S(1)}, bf16[4,48,1536]{2,1,0:T(8,128)(2,1)}) custom-call(f32[8,128]{1,0:T(8,128)S(1)} %copy-done.11, s32[1,3]{1,0:T(1,128)S(1)} %add_bitcast_fusion.refs_1_, bf16[45,11520]{1,0:T(8,128)(2,1)S(1)} %copy-done.13), custom_call_target="tpu_custom_call" | custom-call | flops 1811939328 | tf_op jit(solution)/shard_map/regroup/pallas_call | solution.py:51
  19.8 9.0 %all-to-all-done = bf16[32,8,768]{2,1,0:T(8,128)(2,1)S(1)} async-done(((bf16[32,8,768]{2,1,0:T(8,128)(2,1)}), bf16[32,8,768]{2,1,0:T(8,128)(2,1)S(1)}, u32[]{:S(2)}, u32[]{:S(2)}) %all-to-all-start) | async-done | bytes 393248 | tf_op jit(solution)/shard_map/answer/all_to_all | solution.py:23
  30.2 5.6 %all-to-all-start.1 = ((bf16[32,8,1920]{2,1,0:T(8,128)(2,1)}), bf16[32,8,1920]{2,1,0:T(8,128)(2,1)S(1)}, u32[]{:S(2)}, u32[]{:S(2)}) async-start(bf16[32,8,1920]{2,1,0:T(8,128)(2,1)} %bitcast.6), calls=%async_computation.1 | async-start | bytes 1966080 | tf_op jit(solution)/shard_map/all_to_all | solution.py:23
  37.6 2.7 %collective-permute-start.2 = (bf16[2,48,1536]{2,1,0:T(8,128)(2,1)S(1)}, bf16[2,48,1536]{2,1,0:T(8,128)(2,1)S(1)}, u32[]{:S(2)}, u32[]{:S(2)}) collective-permute-start(bf16[2,48,1536]{2,1,0:T(8,128)(2,1)S(1)} %pad_maximum_fusion.1), channel_id=1, source_target_pairs={{0,128},{32,160},{64,192},{96,224},{128,0},{160,32},{192,64},{224,... | collective-permute-start | bytes 884744 | tf_op jit(solution)/shard_map/regroup/ppermute | solution.py:445
  40.3 2.0 %collective-permute-start.3 = (bf16[2,48,1536]{2,1,0:T(8,128)(2,1)S(1)}, bf16[2,48,1536]{2,1,0:T(8,128)(2,1)S(1)}, u32[]{:S(2)}, u32[]{:S(2)}) collective-permute-start(bf16[2,48,1536]{2,1,0:T(8,128)(2,1)S(1)} %pad_maximum_fusion.2), channel_id=1, source_target_pairs={{0,64},{32,96},{64,128},{96,160},{128,192},{160,224},{192,0},{224,... | collective-permute-start | bytes 884744 | tf_op jit(solution)/shard_map/regroup/ppermute | solution.py:445
  43.1 4.1 %own_half_first.1 = (f32[16,128,2304]{2,1,0:T(8,128)}, f32[8,128]{1,0:T(8,128)S(1)}) custom-call(f32[8,128]{1,0:T(8,128)S(1)} %get-tuple-element.34.refs_0_, f32[9,128,128]{2,1,0:T(8,128)S(1)} %bitcast.31, bf16[9,2,128,2304]{3,2,1,0:T(8,128)(2,1)} %bitcast.47), custom_call_target="tpu_custom_call" | custom-call | flops 679477248 | bytes 5308416 | tf_op jit(solution)/shard_map/own_half_first/pallas_call | solution.py:51
  47.2 4.6 %collective-permute-done.2.refs_5_ = bf16[2,48,1536]{2,1,0:T(8,128)(2,1)S(1)} collective-permute-done((bf16[2,48,1536]{2,1,0:T(8,128)(2,1)S(1)}, bf16[2,48,1536]{2,1,0:T(8,128)(2,1)S(1)}, u32[]{:S(2)}, u32[]{:S(2)}) %collective-permute-start.2) | collective-permute-done | bytes 294944 | tf_op jit(solution)/shard_map/regroup/ppermute | solution.py:445
  54.6 7.1 %all-to-all-done.1 = bf16[32,8,1920]{2,1,0:T(8,128)(2,1)S(1)} async-done(((bf16[32,8,1920]{2,1,0:T(8,128)(2,1)}), bf16[32,8,1920]{2,1,0:T(8,128)(2,1)S(1)}, u32[]{:S(2)}, u32[]{:S(2)}) %all-to-all-start.1) | async-done | bytes 983072 | tf_op jit(solution)/shard_map/all_to_all | solution.py:23
  62.7 4.9 %all-to-all-start.2 = ((bf16[8,48,128]{2,1,0:T(8,128)(2,1)}), bf16[8,48,128]{2,1,0:T(8,128)(2,1)S(1)}, u32[]{:S(2)}, u32[]{:S(2)}) async-start(bf16[8,48,128]{2,1,0:T(8,128)(2,1)} %coarse_first.1), calls=%async_computation.2 | async-start | bytes 196608 | tf_op jit(solution)/shard_map/coarse_first/all_to_all | solution.py:23
  67.7 3.3 %solve_first.1.refs_1_ = f32[128,2304]{1,0:T(8,128)S(1)} custom-call(bf16[256,1920]{1,0:T(8,128)(2,1)S(1)} %bitcast.27, f32[16,128,2304]{2,1,0:T(8,128)} %get-tuple-element.35.refs_1_, bf16[1024,256]{1,0:T(8,128)(2,1)S(1)} %get-tuple-element.36.refs_2_.refs_3_.refs_4_, bf16[9,2,128,2304]{3,2,1,0:T(8,128)(2,1)} %bitcast.48), custom_call_target="tpu_custom_call" | custom-call | flops 679477248 | bytes 5308416 | tf_op jit(solution)/shard_map/solve_first/pallas_call | solution.py:51
  73.0 35.2 %all_to_all.35 = bf16[32,8,2176]{2,1,0:T(8,128)(2,1)S(1)} all-to-all(bf16[32,8,2176]{2,1,0:T(8,128)(2,1)S(1)} %bitcast.39), channel_id=1, replica_groups=mesh['group'=8,'sub'=32] {'sub'}, dimensions={0} | all-to-all | bytes 2228224 | tf_op jit(solution)/shard_map/return_first/all_to_all | solution.py:23
  110.5 5.7 %all-to-all-start.4 = ((bf16[32,8,1920]{2,1,0:T(8,128)(2,1)}), bf16[32,8,1920]{2,1,0:T(8,128)(2,1)S(1)}, u32[]{:S(2)}, u32[]{:S(2)}) async-start(bf16[32,8,1920]{2,1,0:T(8,128)(2,1)} %bitcast.18), calls=%async_computation.4 | async-start | bytes 1966080 | tf_op jit(solution)/shard_map/all_to_all | solution.py:23
  116.2 1.5 collective-permute-start.6
  118.6 2.3 %collective-permute-start.4 = (bf16[256,256]{1,0:T(8,128)(2,1)S(1)}, bf16[256,256]{1,0:T(8,128)(2,1)S(1)}, u32[]{:S(2)}, u32[]{:S(2)}) collective-permute-start(bf16[256,256]{1,0:T(8,128)(2,1)S(1)} %get-tuple-element.49.refs_7_), channel_id=1, source_target_pairs={{0,3},{1,0},{2,1},{3,2},{4,7},{5,4},{6,5},{7,6},{8,11},{9,8},{10,9... | collective-permute-start | bytes 393224 | tf_op jit(solution)/shard_map/own_half_second/ppermute | solution.py:616
  120.9 3.8 %collective-permute-done.6.refs_10_ = bf16[256,256]{1,0:T(8,128)(2,1)S(1)} collective-permute-done((bf16[256,256]{1,0:T(8,128)(2,1)S(1)}, bf16[256,256]{1,0:T(8,128)(2,1)S(1)}, u32[]{:S(2)}, u32[]{:S(2)}) %collective-permute-start.6) | collective-permute-done | bytes 131104 | tf_op jit(solution)/shard_map/own_half_second/ppermute | solution.py:616
  124.8 3.7 %collective-permute-done.5.refs_9_ = bf16[256,256]{1,0:T(8,128)(2,1)S(1)} collective-permute-done((bf16[256,256]{1,0:T(8,128)(2,1)S(1)}, bf16[256,256]{1,0:T(8,128)(2,1)S(1)}, u32[]{:S(2)}, u32[]{:S(2)}) %collective-permute-start.5) | collective-permute-done | bytes 131104 | tf_op jit(solution)/shard_map/own_half_second/ppermute | solution.py:616
  128.5 2.8 %collective-permute-done.4.refs_8_ = bf16[256,256]{1,0:T(8,128)(2,1)S(1)} collective-permute-done((bf16[256,256]{1,0:T(8,128)(2,1)S(1)}, bf16[256,256]{1,0:T(8,128)(2,1)S(1)}, u32[]{:S(2)}, u32[]{:S(2)}) %collective-permute-start.4) | collective-permute-done | bytes 131104 | tf_op jit(solution)/shard_map/own_half_second/ppermute | solution.py:616
  133.3 5.7 %own_half_second.1 = (f32[9,128,128]{2,1,0:T(8,128)}, f32[2,128]{1,0:T(2,128)S(1)}, f32[16,128,3456]{2,1,0:T(8,128)}) custom-call(f32[8,128]{1,0:T(8,128)S(1)} %get-tuple-element.46.refs_0_, s32[1,3]{1,0:T(1,128)S(1)} %add_bitcast_fusion.refs_1_, f32[128,1152]{1,0:T(8,128)S(1)} %copy-done.4, bf16[1024,256]{1,0:T(8,128)(2,1)S(1)} %get-tuple-element.36.refs_2_.refs_3_.refs_4_, ...), custom_call_target="tpu_custom_call" | custom-call | flops 679477248 | bytes 5308416 | tf_op jit(solution)/shard_map/own_half_second/pallas_call | solution.py:51
  139.0 2.9 %all-to-all-done.4 = bf16[32,8,1920]{2,1,0:T(8,128)(2,1)S(1)} async-done(((bf16[32,8,1920]{2,1,0:T(8,128)(2,1)}), bf16[32,8,1920]{2,1,0:T(8,128)(2,1)S(1)}, u32[]{:S(2)}, u32[]{:S(2)}) %all-to-all-start.4) | async-done | bytes 983072 | tf_op jit(solution)/shard_map/all_to_all | solution.py:23
  143.0 4.7 %all-to-all-start.5 = ((bf16[8,64,128]{2,1,0:T(8,128)(2,1)}), bf16[8,64,128]{2,1,0:T(8,128)(2,1)S(1)}, u32[]{:S(2)}, u32[]{:S(2)}) async-start(bf16[8,64,128]{2,1,0:T(8,128)(2,1)} %coarse_second.1), calls=%async_computation.5 | async-start | bytes 262144 | tf_op jit(solution)/shard_map/coarse_second/all_to_all | solution.py:23
  147.8 4.3 %solve_second.1.refs_0_ = f32[128,2304]{1,0:T(8,128)S(1)} custom-call(bf16[256,1920]{1,0:T(8,128)(2,1)S(1)} %bitcast.34, f32[16,128,3456]{2,1,0:T(8,128)} %get-tuple-element.52.refs_1_, bf16[1024,256]{1,0:T(8,128)(2,1)S(1)} %get-tuple-element.36.refs_2_.refs_3_.refs_4_, bf16[9,2,128,2304]{3,2,1,0:T(8,128)(2,1)} %bitcast.50), custom_call_target="tpu_custom_call" | custom-call | flops 679477248 | bytes 5308416 | tf_op jit(solution)/shard_map/solve_second/pallas_call | solution.py:51
  153.0 33.0 %all_to_all.36 = bf16[32,8,1920]{2,1,0:T(8,128)(2,1)S(1)} all-to-all(bf16[32,8,1920]{2,1,0:T(8,128)(2,1)S(1)} %bitcast.40), channel_id=1, replica_groups=mesh['group'=8,'sub'=32] {'sub'}, dimensions={0} | all-to-all | bytes 1966080 | tf_op jit(solution)/shard_map/return_second/all_to_all | solution.py:23
  (52 shorter events, 19.6 us)
Async XLA Ops:
  0.6 14.3 %copy-start.13 = (bf16[45,11520]{1,0:T(8,128)(2,1)S(1)}, bf16[45,11520]{1,0:T(8,128)(2,1)}, u32[]{:S(2)}) copy-start(bf16[45,11520]{1,0:T(8,128)(2,1)} %refs_2_.1) | copy-start | bytes 3110404
  3.2 25.7 %all-to-all-start = ((bf16[32,8,768]{2,1,0:T(8,128)(2,1)}), bf16[32,8,768]{2,1,0:T(8,128)(2,1)S(1)}, u32[]{:S(2)}, u32[]{:S(2)}) async-start(bf16[32,8,768]{2,1,0:T(8,128)(2,1)} %bitcast.52), calls=%async_computation | async-start | bytes 786432 | tf_op jit(solution)/shard_map/answer/all_to_all | solution.py:23
  15.6 3.9 %copy-start = (f32[128,9,128]{2,0,1:T(8,128)S(1)}, f32[128,9,128]{2,0,1:T(8,128)}, u32[]{:S(2)}) copy-start(f32[128,9,128]{2,0,1:T(8,128)} %param.6) | copy-start | bytes 1769476
  15.6 3.9 %copy-start.10 = (s32[128]{0:T(128)S(1)}, s32[128]{0:T(128)}, u32[]{:S(2)}) copy-start(s32[128]{0:T(128)} %param.9) | copy-start | bytes 1540
  15.6 3.9 %copy-start.12 = (s32[128,1]{0,1:T(1,128)S(1)}, s32[128,1]{0,1:T(1,128)}, u32[]{:S(2)}) copy-start(s32[128,1]{0,1:T(1,128)} %param.10) | copy-start | bytes 1540
  19.5 16.3 %collective-permute-start = (bf16[4,48,1536]{2,1,0:T(8,128)(2,1)}, bf16[4,48,1536]{2,1,0:T(8,128)(2,1)}, u32[]{:S(2)}, u32[]{:S(2)}) collective-permute-start(bf16[4,48,1536]{2,1,0:T(8,128)(2,1)} %get-tuple-element.40), channel_id=1, source_target_pairs={{0,32},{32,0},{64,96},{96,64},{128,160},{160,128},{192,224},{224,1... | collective-permute-start | bytes 1769480 | tf_op jit(solution)/shard_map/regroup/ppermute | solution.py:441
  30.2 31.5 %all-to-all-start.1 = ((bf16[32,8,1920]{2,1,0:T(8,128)(2,1)}), bf16[32,8,1920]{2,1,0:T(8,128)(2,1)S(1)}, u32[]{:S(2)}, u32[]{:S(2)}) async-start(bf16[32,8,1920]{2,1,0:T(8,128)(2,1)} %bitcast.6), calls=%async_computation.1 | async-start | bytes 1966080 | tf_op jit(solution)/shard_map/all_to_all | solution.py:23
  37.0 10.2 %collective-permute-start.1 = (bf16[2,48,1536]{2,1,0:T(8,128)(2,1)S(1)}, bf16[2,48,1536]{2,1,0:T(8,128)(2,1)S(1)}, u32[]{:S(2)}, u32[]{:S(2)}) collective-permute-start(bf16[2,48,1536]{2,1,0:T(8,128)(2,1)S(1)} %pad_maximum_fusion), channel_id=1, source_target_pairs={{0,192},{32,224},{64,0},{96,32},{128,64},{160,96},{192,128},{224,1... | collective-permute-start | bytes 884744 | tf_op jit(solution)/shard_map/regroup/ppermute | solution.py:445
  37.6 14.3 %collective-permute-start.2 = (bf16[2,48,1536]{2,1,0:T(8,128)(2,1)S(1)}, bf16[2,48,1536]{2,1,0:T(8,128)(2,1)S(1)}, u32[]{:S(2)}, u32[]{:S(2)}) collective-permute-start(bf16[2,48,1536]{2,1,0:T(8,128)(2,1)S(1)} %pad_maximum_fusion.1), channel_id=1, source_target_pairs={{0,128},{32,160},{64,192},{96,224},{128,0},{160,32},{192,64},{224,... | collective-permute-start | bytes 884744 | tf_op jit(solution)/shard_map/regroup/ppermute | solution.py:445
  40.3 12.5 %collective-permute-start.3 = (bf16[2,48,1536]{2,1,0:T(8,128)(2,1)S(1)}, bf16[2,48,1536]{2,1,0:T(8,128)(2,1)S(1)}, u32[]{:S(2)}, u32[]{:S(2)}) collective-permute-start(bf16[2,48,1536]{2,1,0:T(8,128)(2,1)S(1)} %pad_maximum_fusion.2), channel_id=1, source_target_pairs={{0,64},{32,96},{64,128},{96,160},{128,192},{160,224},{192,0},{224,... | collective-permute-start | bytes 884744 | tf_op jit(solution)/shard_map/regroup/ppermute | solution.py:445
  53.5 1.1 copy-start.1
  62.7 9.3 %all-to-all-start.2 = ((bf16[8,48,128]{2,1,0:T(8,128)(2,1)}), bf16[8,48,128]{2,1,0:T(8,128)(2,1)S(1)}, u32[]{:S(2)}, u32[]{:S(2)}) async-start(bf16[8,48,128]{2,1,0:T(8,128)(2,1)} %coarse_first.1), calls=%async_computation.2 | async-start | bytes 196608 | tf_op jit(solution)/shard_map/coarse_first/all_to_all | solution.py:23
  72.9 36.7 %copy-start.6 = (bf16[640,256]{1,0:T(8,128)(2,1)}, bf16[640,256]{1,0:T(8,128)(2,1)S(1)}, u32[]{:S(2)}) copy-start(bf16[640,256]{1,0:T(8,128)(2,1)S(1)} %get-tuple-element.48.refs_4_) | copy-start | bytes 983044
  72.9 35.2 %copy-start.9 = (bf16[384,256]{1,0:T(8,128)(2,1)S(1)}, bf16[384,256]{1,0:T(8,128)(2,1)}, u32[]{:S(2)}) copy-start(bf16[384,256]{1,0:T(8,128)(2,1)} %copy-done.8) | copy-start | bytes 589828
  109.7 0.8 copy-start.3
  110.5 31.4 %all-to-all-start.4 = ((bf16[32,8,1920]{2,1,0:T(8,128)(2,1)}), bf16[32,8,1920]{2,1,0:T(8,128)(2,1)S(1)}, u32[]{:S(2)}, u32[]{:S(2)}) async-start(bf16[32,8,1920]{2,1,0:T(8,128)(2,1)} %bitcast.18), calls=%async_computation.4 | async-start | bytes 1966080 | tf_op jit(solution)/shard_map/all_to_all | solution.py:23
  116.2 8.6 %collective-permute-start.6 = (bf16[256,256]{1,0:T(8,128)(2,1)S(1)}, bf16[256,256]{1,0:T(8,128)(2,1)S(1)}, u32[]{:S(2)}, u32[]{:S(2)}) collective-permute-start(bf16[256,256]{1,0:T(8,128)(2,1)S(1)} %get-tuple-element.49.refs_7_), channel_id=1, source_target_pairs={{0,1},{1,2},{2,3},{3,0},{4,5},{5,6},{6,7},{7,4},{8,9},{9,10},{10,1... | collective-permute-start | bytes 393224 | tf_op jit(solution)/shard_map/own_half_second/ppermute | solution.py:616
  117.7 10.8 %collective-permute-start.5 = (bf16[256,256]{1,0:T(8,128)(2,1)S(1)}, bf16[256,256]{1,0:T(8,128)(2,1)S(1)}, u32[]{:S(2)}, u32[]{:S(2)}) collective-permute-start(bf16[256,256]{1,0:T(8,128)(2,1)S(1)} %get-tuple-element.49.refs_7_), channel_id=1, source_target_pairs={{0,2},{1,3},{2,0},{3,1},{4,6},{5,7},{6,4},{7,5},{8,10},{9,11},{10,... | collective-permute-start | bytes 393224 | tf_op jit(solution)/shard_map/own_half_second/ppermute | solution.py:616
  118.6 12.6 %collective-permute-start.4 = (bf16[256,256]{1,0:T(8,128)(2,1)S(1)}, bf16[256,256]{1,0:T(8,128)(2,1)S(1)}, u32[]{:S(2)}, u32[]{:S(2)}) collective-permute-start(bf16[256,256]{1,0:T(8,128)(2,1)S(1)} %get-tuple-element.49.refs_7_), channel_id=1, source_target_pairs={{0,3},{1,0},{2,1},{3,2},{4,7},{5,4},{6,5},{7,6},{8,11},{9,8},{10,9... | collective-permute-start | bytes 393224 | tf_op jit(solution)/shard_map/own_half_second/ppermute | solution.py:616
  131.2 1.1 copy-start.4
  132.3 1.0 copy-start.7
  133.3 8.6 %copy-start.2 = (bf16[8,48,1536]{2,1,0:T(8,128)(2,1)S(1)}, bf16[8,48,1536]{2,1,0:T(8,128)(2,1)}, u32[]{:S(2)}) copy-start(bf16[8,48,1536]{2,1,0:T(8,128)(2,1)} %copy-done.1) | copy-start | bytes 3538948
  143.0 9.5 %all-to-all-start.5 = ((bf16[8,64,128]{2,1,0:T(8,128)(2,1)}), bf16[8,64,128]{2,1,0:T(8,128)(2,1)S(1)}, u32[]{:S(2)}, u32[]{:S(2)}) async-start(bf16[8,64,128]{2,1,0:T(8,128)(2,1)} %coarse_second.1), calls=%async_computation.5 | async-start | bytes 262144 | tf_op jit(solution)/shard_map/coarse_second/all_to_all | solution.py:23
  152.9 33.0 %copy-start.5 = (f32[9,128,128]{2,1,0:T(8,128)S(1)}, f32[9,128,128]{2,1,0:T(8,128)}, u32[]{:S(2)}) copy-start(f32[9,128,128]{2,1,0:T(8,128)} %get-tuple-element.50.refs_2_) | copy-start | bytes 1769476
  (2 other events, 1.4 us)
